TPU v7x, 32 devices: a whole 2x2x4 slice. The times are simulated.
32 devices in a mesh: dp: 8 (over y, x, core), head: 4 (over z).
Axes of the slice: x: 2, y: 2, z: 4, core: 2. Of those that a mesh axis runs over, the one named last changes fastest.
Arguments:
- hidden_in: bfloat16 [4096, 1024], P(('dp', 'head')), may hold values from -6 to 6
- segments: int32 [4096], P('dp'), may hold values from 0 to 6, as said below
- value_pick: int32 [4096, 4, 2], P('dp', 'head'), may hold values from 0 to 4, all different within a row
- output_pick: int32 [4096, 4, 2], P('dp', 'head'), may hold values from 0 to 4, all different within a row
- expert_pick: int32 [4096, 16], P(('dp', 'head')), may hold values from 0 to 95, all different within a row; in each aligned block of 128 rows (0 to 127, 128 to 255, ...) at most 32 rows name the same one
- attend_gain: bfloat16 [1024], replicated, may hold values from 0.5 to 1.5
- query_weight: bfloat16 [4, 1024, 128], P('head'), may hold values from -0.1875 to 0.1875
- key_weight: bfloat16 [4, 1024, 128], P('head'), may hold values from -0.1875 to 0.1875
- value_weight: bfloat16 [4, 1024, 640], P('head'), may hold values from -0.1875 to 0.1875
- output_weight: bfloat16 [4, 640, 1024], P('head'), may hold values from -3 to 3
- head_router: bfloat16 [4, 1024, 10], P('head'), may hold values from -0.1875 to 0.1875
- expert_gain: bfloat16 [1024], replicated, may hold values from 0.5 to 1.5
- router: bfloat16 [1024, 96], replicated, may hold values from -0.09375 to 0.09375
- expert_in: bfloat16 [96, 1024, 128], P(('dp', 'head')), may hold values from -0.1875 to 0.1875
- expert_out: bfloat16 [96, 128, 1024], P(('dp', 'head')), may hold values from -0.5 to 0.5
- cotangent: bfloat16 [4096, 1024], P(('dp', 'head')), may hold values from -6 to 6
Outputs:
- output: float32 [4096, 1024], P(('dp', 'head'))
- input_grad: float32 [4096, 1024], P(('dp', 'head'))
- grad_attend_gain: float32 [1024], replicated
- grad_query_weight: float32 [4, 1024, 128], P('head')
- grad_key_weight: float32 [4, 1024, 128], P('head')
- grad_value_weight: float32 [4, 1024, 640], P('head')
- grad_output_weight: float32 [4, 640, 1024], P('head')
- grad_head_router: float32 [4, 1024, 10], P('head')
- grad_expert_gain: float32 [1024], replicated
- grad_router: float32 [1024, 96], replicated
- grad_expert_in: float32 [96, 1024, 128], P(('dp', 'head'))
- grad_expert_out: float32 [96, 128, 1024], P(('dp', 'head'))
Inputs may be any that keep to these rules, and one draw needn't show every extreme that they name: `segments`: within each group of 512 rows that share an index of dp the numbers start at 0 and rise by 0 or 1 from row to row; equal numbers in a group mark one document, and a group's longest document has 384 tokens. `value_pick`: the two numbers of a token and head differ. `output_pick`: the two numbers of a token and head differ. `expert_pick`: A token's 16 numbers differ; the 128 rows of one device name no expert more than 32 times.
All inputs are finite; a program needn't handle non-finite values.
Results may differ from a plain program's by a relative error of at most 0.019.
Values may be sent and summed in bfloat16 or wider, within the bound.
A program may use at most 128 MiB of HBM per device.

v0:
```python
import jax
import jax.numpy as jnp
from jax import lax
from jax.sharding import PartitionSpec as P

REPEATS = 1


epsilon = 1e-06
theta = 10000.0
negative = -1e30
score_block = 512
rank_block = 128


def product(left, right, left_axis, right_axis):
    return lax.dot_general(
        left, right, (((left_axis,), (right_axis,)), ((), ())), preferred_element_type=jnp.float32
    )


def rms_scale(residual):
    return lax.rsqrt(jnp.mean(residual * residual, axis=-1, keepdims=True) + epsilon)


def rotary_tables(row_count, head_width):
    half_width = head_width // 2
    position = jnp.arange(row_count, dtype=jnp.float32)[:, None]
    exponent = jnp.arange(half_width, dtype=jnp.float32)[None, :]
    angles = position * jnp.power(theta, -2.0 * exponent / head_width)
    return (jnp.cos(angles), jnp.sin(angles))


def rotate(matrix, cosine_table, sine_table):
    half_width = matrix.shape[-1] // 2
    first_half, second = (matrix[:, :half_width], matrix[:, half_width:])
    return jnp.concatenate(
        [
            first_half * cosine_table - second * sine_table,
            second * cosine_table + first_half * sine_table,
        ],
        axis=-1,
    )


def rotate_back(matrix, cosine_table, sine_table):
    half_width = matrix.shape[-1] // 2
    first_half, second = (matrix[:, :half_width], matrix[:, half_width:])
    return jnp.concatenate(
        [
            first_half * cosine_table + second * sine_table,
            second * cosine_table - first_half * sine_table,
        ],
        axis=-1,
    )


def pick_mask(picks, expert_count):
    hits = picks[:, 0, :, None] == jnp.arange(expert_count, dtype=jnp.int32)[None, None, :]
    return jnp.any(hits, axis=1).astype(jnp.float32)


def norm_back(residual, inverse, gain, incoming):
    unit_rows = residual * inverse
    scaled = incoming * gain
    gain_grad = jnp.sum(incoming * unit_rows, axis=0)
    row_grad = inverse * (scaled - unit_rows * jnp.mean(scaled * unit_rows, axis=-1, keepdims=True))
    return (row_grad, gain_grad)


def head_inputs(
    grouped, attend_scale, query_mat, key_mat, value_mat, gate_mat, value_mask, output_mask
):
    row_count = grouped.shape[0]
    head_width = query_mat.shape[1]
    experts = value_mask.shape[1]
    inverse = rms_scale(grouped)
    normed = (grouped * inverse * attend_scale).astype(jnp.bfloat16)
    plain_rows = grouped.astype(jnp.bfloat16)
    cosine_table, sine_table = rotary_tables(row_count, head_width)
    queries = rotate(
        jnp.dot(normed, query_mat, preferred_element_type=jnp.float32), cosine_table, sine_table
    ).astype(jnp.bfloat16)
    key_rows = rotate(
        jnp.dot(normed, key_mat, preferred_element_type=jnp.float32), cosine_table, sine_table
    ).astype(jnp.bfloat16)
    squash = jax.nn.sigmoid(jnp.dot(normed, gate_mat, preferred_element_type=jnp.float32))
    value_gates = squash[:, :experts] * value_mask
    output_gates = squash[:, experts:] * output_mask
    expert_values = jnp.dot(plain_rows, value_mat, preferred_element_type=jnp.float32).reshape(
        row_count, experts, head_width
    )
    values = jnp.sum(expert_values * value_gates[:, :, None], axis=1).astype(jnp.bfloat16)
    return (
        inverse,
        normed,
        plain_rows,
        queries,
        key_rows,
        squash,
        value_gates,
        output_gates,
        expert_values,
        values,
        cosine_table,
        sine_table,
    )


def block_scores(queries, key_rows, doc_marks, first_row, block_rows):
    places = jnp.arange(key_rows.shape[0], dtype=jnp.int32)
    positions = first_row + jnp.arange(block_rows, dtype=jnp.int32)
    allowed = (places[None, :] <= positions[:, None]) & (doc_marks[:, None] == doc_marks[None, :])
    scores = product(queries, key_rows, 1, 1) * queries.shape[1] ** (-0.5)
    return (queries, jnp.where(allowed, scores, negative))


def attend(queries, key_rows, values, doc_marks):
    row_count, head_width = queries.shape
    block_rows = min(score_block, row_count)

    def one_block(block_index):
        row_block, scores = block_scores(
            queries, key_rows, doc_marks, block_index * block_rows, block_rows
        )
        highest_score = jnp.max(scores, axis=-1, keepdims=True)
        exponents = jnp.exp(scores - highest_score)
        summed = jnp.sum(exponents, axis=-1, keepdims=True)
        probabilities = (exponents / summed).astype(jnp.bfloat16)
        attended = jnp.dot(probabilities, values, preferred_element_type=jnp.float32)
        return (attended, (highest_score + jnp.log(summed))[:, 0])

    attended, log_sums = lax.map(one_block, jnp.arange(row_count // block_rows, dtype=jnp.int32))
    return (attended.reshape(row_count, head_width), log_sums.reshape(row_count))


def attend_back(queries, key_rows, values, doc_marks, log_sums, attended_grad):
    row_count, head_width = queries.shape
    block_rows = min(score_block, row_count)
    scale = head_width ** (-0.5)

    def one_block(running, block_index):
        key_grad, value_grad = running
        first_row = block_index * block_rows
        row_block, scores = block_scores(queries, key_rows, doc_marks, first_row, block_rows)
        probabilities = jnp.exp(scores - log_sums[:, None])
        prob_grad = product(attended_grad, values, 1, 1)
        centre = jnp.sum(probabilities * prob_grad, axis=-1, keepdims=True)
        score_grad = (probabilities * (prob_grad - centre)).astype(jnp.bfloat16)
        query_grad = product(score_grad, key_rows, 1, 0) * scale
        key_grad = key_grad + product(score_grad, row_block, 0, 0) * scale
        value_grad = value_grad + product(probabilities.astype(jnp.bfloat16), attended_grad, 0, 0)
        return ((key_grad, value_grad), query_grad)

    zeros_block = jnp.zeros((row_count, head_width), jnp.float32)
    (key_grad, value_grad), query_grad = lax.scan(
        one_block, (zeros_block, zeros_block), jnp.arange(row_count // block_rows, dtype=jnp.int32)
    )
    return (query_grad.reshape(row_count, head_width), key_grad, value_grad)


def head_backward(
    grouped,
    group_grads,
    attended,
    log_sums,
    doc_marks,
    attend_scale,
    matrices,
    value_mask,
    output_mask,
):
    query_mat, key_mat, value_mat, output_mat, gate_mat = matrices
    (
        inverse,
        normed,
        plain_rows,
        queries,
        key_rows,
        squash,
        value_gates,
        output_gates,
        expert_values,
        values,
        cosine_table,
        sine_table,
    ) = head_inputs(
        grouped, attend_scale, query_mat, key_mat, value_mat, gate_mat, value_mask, output_mask
    )
    row_count, head_width = queries.shape
    experts = value_mask.shape[1]
    weighted = (
        (output_gates[:, :, None] * attended[:, None, :])
        .reshape(row_count, experts * head_width)
        .astype(jnp.bfloat16)
    )
    weighted_grad = product(group_grads, output_mat, 1, 1).reshape(row_count, experts, head_width)
    output_grad = product(weighted, group_grads, 0, 0)
    output_gate_grad = jnp.sum(weighted_grad * attended[:, None, :], axis=-1)
    attended_grad = jnp.sum(weighted_grad * output_gates[:, :, None], axis=1).astype(jnp.bfloat16)
    query_grad, key_grad, values_grad = attend_back(
        queries, key_rows, values, doc_marks, log_sums, attended_grad
    )
    expert_grad = (
        (value_gates[:, :, None] * values_grad[:, None, :])
        .reshape(row_count, experts * head_width)
        .astype(jnp.bfloat16)
    )
    value_gate_grad = jnp.sum(expert_values * values_grad[:, None, :], axis=-1)
    query_grad = rotate_back(query_grad, cosine_table, sine_table).astype(jnp.bfloat16)
    key_grad = rotate_back(key_grad, cosine_table, sine_table).astype(jnp.bfloat16)
    logit_grad = (
        jnp.concatenate([value_gate_grad * value_mask, output_gate_grad * output_mask], axis=1)
        * squash
        * (1.0 - squash)
    ).astype(jnp.bfloat16)
    weight_grads = (
        product(normed, query_grad, 0, 0),
        product(normed, key_grad, 0, 0),
        product(plain_rows, expert_grad, 0, 0),
        output_grad,
        product(normed, logit_grad, 0, 0),
    )
    normed_grad = (
        product(query_grad, query_mat, 1, 1)
        + product(key_grad, key_mat, 1, 1)
        + product(logit_grad, gate_mat, 1, 1)
    )
    row_grad, gain_grad = norm_back(grouped, inverse, attend_scale, normed_grad)
    return (row_grad + product(expert_grad, value_mat, 1, 1), gain_grad, weight_grads)


def slot_tables(picks, experts_total, capacity):
    tokens, chosen = picks.shape
    choice_count = tokens * chosen
    block_rows = min(rank_block, choice_count)
    flat_picks = picks.reshape(choice_count)
    onehot = (flat_picks[:, None] == jnp.arange(experts_total, dtype=jnp.int32)[None, :]).astype(
        jnp.bfloat16
    )
    onehot = onehot.reshape(choice_count // block_rows, block_rows, experts_total)
    triangle = (jnp.arange(block_rows)[:, None] > jnp.arange(block_rows)[None, :]).astype(
        jnp.bfloat16
    )
    within = jnp.einsum("ij,bje->bie", triangle, onehot, preferred_element_type=jnp.float32)
    totals = jnp.sum(onehot, axis=1, dtype=jnp.float32)
    before = jnp.cumsum(totals, axis=0) - totals
    ranking = (
        jnp.sum((within + before[:, None, :]) * onehot, axis=-1)
        .reshape(choice_count)
        .astype(jnp.int32)
    )
    slot_of = flat_picks * capacity + ranking
    owners = (
        jnp.full((experts_total * capacity,), -1, jnp.int32)
        .at[slot_of]
        .set(jnp.arange(choice_count, dtype=jnp.int32))
    )
    filled = owners >= 0
    owners = jnp.where(filled, owners, 0)
    return (slot_of, filled, owners, owners // chosen)


def expert_forward(arrived, expert_in, expert_out):
    hidden = jnp.einsum("secd,edh->sech", arrived, expert_in, preferred_element_type=jnp.float32)
    activations = jax.nn.gelu(hidden).astype(jnp.bfloat16)
    return jnp.einsum(
        "sech,ehd->secd", activations, expert_out, preferred_element_type=jnp.float32
    ).astype(jnp.bfloat16)


def expert_backward(arrived, incoming, expert_in, expert_out):
    hidden = jnp.einsum("secd,edh->sech", arrived, expert_in, preferred_element_type=jnp.float32)
    lifted, gelu_back = jax.vjp(jax.nn.gelu, hidden)
    activations = lifted.astype(jnp.bfloat16)
    act_grad = jnp.einsum(
        "secd,ehd->sech", incoming, expert_out, preferred_element_type=jnp.float32
    )
    hidden_grad = gelu_back(act_grad)[0].astype(jnp.bfloat16)
    in_grad = jnp.einsum("secd,sech->edh", arrived, hidden_grad, preferred_element_type=jnp.float32)
    out_grad = jnp.einsum(
        "sech,secd->ehd", activations, incoming, preferred_element_type=jnp.float32
    )
    return (activations, hidden_grad, in_grad, out_grad)


def body(
    hidden_in,
    segments,
    value_pick,
    output_pick,
    expert_pick,
    attend_gain,
    query_weight,
    key_weight,
    value_weight,
    output_weight,
    head_router,
    expert_gain,
    router,
    expert_in,
    expert_out,
    cotangent,
):
    tokens, features = hidden_in.shape
    chosen = expert_pick.shape[1]
    experts_total = router.shape[1]
    per_device = expert_in.shape[0]
    devices = lax.axis_size("dp") * lax.axis_size("head")
    capacity = max(2, 3 * tokens * chosen // (2 * experts_total))
    head_experts = head_router.shape[2] // 2
    matrices = (query_weight[0], key_weight[0], value_weight[0], output_weight[0], head_router[0])
    query_mat, key_mat, value_mat, output_mat, gate_mat = matrices
    value_mask = pick_mask(value_pick, head_experts)
    output_mask = pick_mask(output_pick, head_experts)
    attend_scale = attend_gain.astype(jnp.float32)
    expert_scale = expert_gain.astype(jnp.float32)
    slot_of, filled, owners, token_of = slot_tables(expert_pick, experts_total, capacity)
    buffer_shape = (devices, per_device * capacity, features)
    expert_shape = (devices, per_device, capacity, features)
    flat_shape = (experts_total * capacity, features)

    def gather_group(residual):
        return lax.all_gather(residual, "head", axis=0, tiled=True)

    def router_side(middle):
        inverse = rms_scale(middle)
        normed = (middle * inverse * expert_scale).astype(jnp.bfloat16)
        logits = jnp.dot(normed, router, preferred_element_type=jnp.float32)
        gate_values = jax.nn.sigmoid(jnp.take_along_axis(logits, expert_pick, axis=1))
        outgoing = jnp.where(
            filled[:, None], normed[token_of], jnp.zeros((), jnp.bfloat16)
        ).reshape(buffer_shape)
        return (inverse, normed, gate_values, outgoing)

    current = hidden_in.astype(jnp.float32)
    repeat = 0
    grouped = gather_group(current)
    pieces = head_inputs(
        grouped, attend_scale, query_mat, key_mat, value_mat, gate_mat, value_mask, output_mask
    )
    attended, log_sums = attend(pieces[3], pieces[4], pieces[9], segments)
    weighted = (
        (pieces[7][:, :, None] * attended[:, None, :])
        .reshape(grouped.shape[0], -1)
        .astype(jnp.bfloat16)
    )
    middle = current + lax.psum_scatter(
        jnp.dot(weighted, output_mat, preferred_element_type=jnp.float32),
        "head",
        scatter_dimension=0,
        tiled=True,
    )
    inverse, normed, gate_values, outgoing = router_side(middle)
    arrived = lax.all_to_all(outgoing, ("dp", "head"), split_axis=0, concat_axis=0, tiled=True)
    produced = expert_forward(arrived.reshape(expert_shape), expert_in, expert_out)
    returned = lax.all_to_all(
        produced.reshape(buffer_shape), ("dp", "head"), split_axis=0, concat_axis=0, tiled=True
    ).reshape(flat_shape)
    picked = returned[slot_of].reshape(tokens, chosen, features)
    stored = [(current, grouped, middle, attended, log_sums, arrived, returned)]
    current = middle + jnp.sum(picked.astype(jnp.float32) * gate_values[:, :, None], axis=1)
    output = current
    gradient = cotangent.astype(jnp.float32)
    grad_attend = jnp.zeros((features,), jnp.float32)
    grad_gain_expert = jnp.zeros((features,), jnp.float32)
    grad_router = jnp.zeros((features, experts_total), jnp.float32)
    grad_in = jnp.zeros(expert_in.shape, jnp.float32)
    grad_out = jnp.zeros(expert_out.shape, jnp.float32)
    head_grads = (
        jnp.zeros(query_mat.shape, jnp.float32),
        jnp.zeros(key_mat.shape, jnp.float32),
        jnp.zeros(value_mat.shape, jnp.float32),
        jnp.zeros(output_mat.shape, jnp.float32),
        jnp.zeros(gate_mat.shape, jnp.float32),
    )
    for repeat in reversed(range(REPEATS)):
        current, grouped, middle, attended, log_sums, arrived, returned = stored[repeat]
        inverse, normed, gate_values, outgoing = router_side(middle)
        gate_flat = gate_values.reshape(-1)
        slot_grads = (
            jnp.where(filled[:, None], gate_flat[owners][:, None] * gradient[token_of], 0.0)
            .astype(jnp.bfloat16)
            .reshape(buffer_shape)
        )
        expert_rows, slot_incoming = (
            lax.all_to_all(outgoing, ("dp", "head"), split_axis=0, concat_axis=0, tiled=True),
            lax.all_to_all(slot_grads, ("dp", "head"), split_axis=0, concat_axis=0, tiled=True),
        )
        activations, hidden_grad, in_grad, out_grad = expert_backward(
            expert_rows.reshape(expert_shape),
            slot_incoming.reshape(expert_shape),
            expert_in,
            expert_out,
        )
        grad_in = in_grad
        grad_out = out_grad
        row_grads = (
            jnp.einsum("sech,edh->secd", hidden_grad, expert_in, preferred_element_type=jnp.float32)
            .astype(jnp.bfloat16)
            .reshape(buffer_shape)
        )
        produced = (
            jnp.einsum(
                "sech,ehd->secd", activations, expert_out, preferred_element_type=jnp.float32
            )
            .astype(jnp.bfloat16)
            .reshape(buffer_shape)
        )
        outputs_back, sent_back = (
            lax.all_to_all(produced, ("dp", "head"), split_axis=0, concat_axis=0, tiled=True),
            lax.all_to_all(row_grads, ("dp", "head"), split_axis=0, concat_axis=0, tiled=True),
        )
        outputs_back = outputs_back.reshape(flat_shape)
        sent_back = sent_back.reshape(flat_shape)
        picked = outputs_back[slot_of].reshape(tokens, chosen, features)
        gate_grad = (
            jnp.sum(picked.astype(jnp.float32) * gradient[:, None, :], axis=-1)
            * gate_values
            * (1.0 - gate_values)
        )
        matches = (
            expert_pick[:, :, None] == jnp.arange(experts_total, dtype=jnp.int32)[None, None, :]
        )
        dense_grad = jnp.sum(jnp.where(matches, gate_grad[:, :, None], 0.0), axis=1).astype(
            jnp.bfloat16
        )
        grad_router = product(normed, dense_grad, 0, 0)
        normed_grad = product(dense_grad, router, 1, 1) + jnp.sum(
            sent_back[slot_of].reshape(tokens, chosen, features).astype(jnp.float32), axis=1
        )
        row_grad, gain_grad = norm_back(middle, inverse, expert_scale, normed_grad)
        grad_gain_expert = gain_grad
        middle_grad = gradient + row_grad
        group_input = gather_group(current)
        group_grads = lax.all_gather(middle_grad.astype(jnp.bfloat16), "head", axis=0, tiled=True)
        partial_value, gain_part, repeat_grads = head_backward(
            group_input,
            group_grads,
            attended,
            log_sums,
            segments,
            attend_scale,
            matrices,
            value_mask,
            output_mask,
        )
        grad_attend = gain_part
        head_grads = jax.tree.map(jnp.add, head_grads, tuple(repeat_grads))
        gradient = middle_grad + lax.psum_scatter(
            partial_value, "head", scatter_dimension=0, tiled=True
        )
    head_grads = lax.psum(
        (head_grads[0], head_grads[1], head_grads[2], head_grads[3], head_grads[4]), "dp"
    )
    grad_attend, grad_gain_expert, grad_router = lax.psum(
        (grad_attend, grad_gain_expert, grad_router), ("dp", "head")
    )
    return (
        output,
        gradient,
        grad_attend,
        head_grads[0][None],
        head_grads[1][None],
        head_grads[2][None],
        head_grads[3][None],
        head_grads[4][None],
        grad_gain_expert,
        grad_router,
        grad_in,
        grad_out,
    )


def solution(mesh):
    in_specs = (
        P(("dp", "head"), None),
        P("dp"),
        P("dp", "head", None),
        P("dp", "head", None),
        P(("dp", "head"), None),
        P(),
        P("head", None, None),
        P("head", None, None),
        P("head", None, None),
        P("head", None, None),
        P("head", None, None),
        P(),
        P(),
        P(("dp", "head"), None, None),
        P(("dp", "head"), None, None),
        P(("dp", "head"), None),
    )
    out_specs = (
        P(("dp", "head"), None),
        P(("dp", "head"), None),
        P(),
        P("head", None, None),
        P("head", None, None),
        P("head", None, None),
        P("head", None, None),
        P("head", None, None),
        P(),
        P(),
        P(("dp", "head"), None, None),
        P(("dp", "head"), None, None),
    )
    return jax.shard_map(body, mesh=mesh, in_specs=in_specs, out_specs=out_specs, check_vma=False)
```

profile of v0, /device:TPU:0, one launch (start us, length us, event | category | flops | bytes accessed | tf_op | source)
XLA Modules:
  0.0 1131.4 jit_solution(9721554597587775896)
XLA Ops:
  11.5 47.3 %all-gather.3.cloned.1.call-done = f32[512,1024]{1,0:T(8,128)} async-done(((f32[128,1024]{1,0:T(8,128)}), f32[512,1024]{1,0:T(8,128)}) %all-gather.3.cloned.1.call-update) | async-done | bytes 2097168 | tf_op jit(solution)/shard_map/all_gather | solution.py:324
  76.5 8.1 scatter_custom_fusion
  84.7 33.4 %reduce-scatter.3.cloned.1.call-done = f32[128,1024]{1,0:T(8,128)} async-done(((f32[512,1024]{1,0:T(8,128)}), f32[128,1024]{1,0:T(8,128)}) %reduce-scatter.3.cloned.1.call-update) | async-done | bytes 524304 | tf_op jit(solution)/shard_map/reduce_scatter | solution.py:348
  119.4 14.0 %gather_fusion = bf16[3072,1024]{1,0:T(8,128)(2,1)} fusion(bf16[128,1024]{1,0:T(8,128)(2,1)S(1)} %multiply_convert_fusion.4, s32[3072]{0:T(1024)S(1)} %get-tuple-element.167), kind=kCustom, calls=%fused_computation.1 | custom fusion | bytes 12595200 | tf_op jit(solution)/shard_map/gather | solution.py:332
  137.2 141.7 %all_to_all.22 = bf16[32,96,1024]{2,1,0:T(8,128)(2,1)S(1)} all-to-all(bf16[32,96,1024]{2,1,0:T(8,128)(2,1)S(1)} %broadcast_select_fusion), channel_id=1, replica_groups=mesh['dp'=8,'head'=4] {'dp','head'}, dimensions={0} | all-to-all | bytes 12582912 | tf_op jit(solution)/shard_map/all_to_all | solution.py:355
  288.5 4.6 all-to-all-start.1
  293.4 14.3 %gather_fusion.3 = f32[3072,1024]{1,0:T(8,128)} fusion(f32[128,1024]{1,0:T(8,128)S(1)} %convert_element_type.169, s32[3072]{0:T(1024)S(1)} %get-tuple-element.167), kind=kCustom, calls=%fused_computation.4 | custom fusion | bytes 25178112 | tf_op jit(solution)/shard_map/gather | solution.py:382
  307.9 13.5 %gather_fusion.5 = f32[2048]{0:T(1024)S(1)} fusion(f32[128,96]{0,1:T(8,128)S(1)} %fusion.99, s32[2048]{0:T(1024)S(1)} %reshape.332), kind=kCustom, calls=%fused_computation.clone | custom fusion | bytes 32768 | tf_op jit(solution)/shard_map/jit(take_along_axis)/gather | solution.py:330
  321.6 108.5 %all-to-all-done.1 = bf16[32,96,1024]{2,1,0:T(8,128)(2,1)} async-done(((bf16[32,96,1024]{2,1,0:T(8,128)(2,1)}), bf16[32,96,1024]{2,1,0:T(8,128)(2,1)}, u32[]{:S(2)}, u32[]{:S(2)}) %all-to-all-start.1) | async-done | bytes 6291488 | tf_op jit(solution)/shard_map/all_to_all | solution.py:357
  430.0 14.6 %gather_fusion.1 = bf16[2048,1024]{1,0:T(8,128)(2,1)} fusion(bf16[3072,1024]{1,0:T(8,128)(2,1)} %bitcast.24, s32[2048]{0:T(1024)S(1)} %broadcast_clamp_fusion), kind=kCustom, calls=%fused_computation.2 | custom fusion | bytes 8396800 | tf_op jit(solution)/shard_map/gather | solution.py:360
  448.0 17.4 %gather_fusion.2 = f32[3072]{0:T(1024)S(1)} fusion(f32[2048]{0:T(1024)S(1)} %reshape.263, s32[3072]{0:T(1024)S(1)} %get-tuple-element.166), kind=kCustom, calls=%fused_computation.3 | custom fusion | bytes 36864 | tf_op jit(solution)/shard_map/gather | solution.py:382
  465.5 5.5 select_convert_fusion
  471.1 144.3 %all_to_all.23 = bf16[32,96,1024]{2,1,0:T(8,128)(2,1)S(1)} all-to-all(bf16[32,96,1024]{2,1,0:T(8,128)(2,1)S(1)} %select_convert_fusion), channel_id=1, replica_groups=mesh['dp'=8,'head'=4] {'dp','head'}, dimensions={0} | all-to-all | bytes 12582912 | tf_op jit(solution)/shard_map/all_to_all | solution.py:388
  629.4 136.1 %all-to-all-done.3 = bf16[32,96,1024]{2,1,0:T(8,128)(2,1)} async-done(((bf16[32,96,1024]{2,1,0:T(8,128)(2,1)}), bf16[32,96,1024]{2,1,0:T(8,128)(2,1)}, u32[]{:S(2)}, u32[]{:S(2)}) %all-to-all-start.3) | async-done | bytes 6291488 | tf_op jit(solution)/shard_map/all_to_all | solution.py:412
  765.5 14.6 %gather_fusion.4 = bf16[2048,1024]{1,0:T(8,128)(2,1)} fusion(bf16[3072,1024]{1,0:T(8,128)(2,1)} %bitcast.35, s32[2048]{0:T(1024)S(1)} %broadcast_clamp_fusion), kind=kCustom, calls=%fused_computation.5 | custom fusion | bytes 8396800 | tf_op jit(solution)/shard_map/gather | solution.py:430
  787.7 29.9 %all-gather.5.cloned.1.call-done = bf16[512,1024]{1,0:T(8,128)(2,1)} async-done(((bf16[128,1024]{1,0:T(8,128)(2,1)}), bf16[512,1024]{1,0:T(8,128)(2,1)}) %all-gather.5.cloned.1.call-update) | async-done | bytes 1048592 | tf_op jit(solution)/shard_map/all_gather | solution.py:436
  841.8 5.0 fusion
  846.8 6.0 fusion.19
  852.8 6.4 convolution_bitcast_fusion.2
  859.5 24.3 %psum.61 = f32[1,1024,10]{1,2,0:T(8,128)S(1)} all-reduce(f32[1,1024,10]{1,2,0:T(8,128)S(1)} %convolution_bitcast_fusion.5), channel_id=1, replica_groups=mesh['dp'=8,'head'=4] {'dp'}, use_global_device_ids=true, to_apply=%region_29.31 | all-reduce | flops 10240 | bytes 81920 | tf_op jit(solution)/shard_map/psum | solution.py:453
  884.4 39.4 %all-reduce = (f32[1024]{0:T(1024)}, f32[1024]{0:T(1024)}) all-reduce(f32[1024]{0:T(1024)S(1)} %get-tuple-element.136, f32[1024]{0:T(1024)S(1)} %copy-done.66), channel_id=1, replica_groups=mesh['dp'=8,'head'=4] {'dp','head'}, use_global_device_ids=true, to_apply=%region_24.26 | all-reduce | flops 2048 | bytes 16384 | tf_op jit(solution)/shard_map/psum | solution.py:456
  923.8 13.0 %all-reduce.7.cloned.1.call-done = (f32[1,1024,128]{2,1,0:T(8,128)}, f32[1,1024,128]{2,1,0:T(8,128)}, f32[1,1024,640]{1,2,0:T(8,128)}, f32[1,640,1024]{2,1,0:T(8,128)}) async-done(((f32[1,1024,128]{2,1,0:T(8,128)}, f32[1,1024,128]{2,1,0:T(8,128)}, f32[1,1024,640]{1,2,0:T(8,128)}, f32[1,640,1024]{2,1,0:T(8,128)}), (f32[1,1024,128]{2,1,0:T(8,128)}, f32[1,1024,128]{2,1,0:T(8,128)}, f32[1,1024,640]{1,2,0:T(8,128)}, ...) | async-done | bytes 6291472 | tf_op jit(solution)/shard_map/psum | solution.py:453
  940.1 42.7 %reduce-scatter.5.cloned.1.call-done = f32[128,1024]{1,0:T(8,128)} async-done(((f32[512,1024]{1,0:T(8,128)}), f32[128,1024]{1,0:T(8,128)}) %reduce-scatter.5.cloned.1.call-update) | async-done | bytes 524304 | tf_op jit(solution)/shard_map/reduce_scatter | solution.py:450
  985.1 131.1 %all-reduce.5.cloned.1.call-done = f32[1024,96]{0,1:T(8,128)} async-done(((f32[1024,96]{0,1:T(8,128)}), f32[1024,96]{0,1:T(8,128)}) %all-reduce.5.cloned.1.call-update) | async-done | bytes 393232 | tf_op jit(solution)/shard_map/psum | solution.py:456
  (265 shorter events, 100.3 us)
Async XLA Ops:
  7.2 65.8 %copy-start = (bf16[1,640,1024]{2,1,0:T(8,128)(2,1)S(1)}, bf16[1,640,1024]{2,1,0:T(8,128)(2,1)}, u32[]{:S(2)}) copy-start(bf16[1,640,1024]{2,1,0:T(8,128)(2,1)} %param.27) | copy-start | bytes 3932164
  7.2 51.6 %all-gather.3.cloned.1.call-start = ((), (), s32[]{:S(2)}) async-start(), calls=%async_computation.6 | async-start | bytes 2621440 | tf_op jit(solution)/shard_map/all_gather | solution.py:324
  9.2 108.9 %reduce-scatter.3.cloned.1.call-start = ((), (), s32[]{:S(2)}) async-start(), calls=%async_computation.7 | async-start | bytes 2621440 | tf_op jit(solution)/shard_map/reduce_scatter | solution.py:348
  10.0 50.9 %copy-start.57 = (f32[1024]{0:T(1024)}, f32[1024]{0:T(1024)S(1)}, u32[]{:S(2)}) copy-start(f32[1024]{0:T(1024)S(1)} %convert_element_type.151) | copy-start | bytes 12292
  11.5 54.8 %copy-start.74 = (f32[64]{0:T(128)}, f32[64]{0:T(128)S(1)}, u32[]{:S(2)}) copy-start(f32[64]{0:T(128)S(1)} %multiply_power_fusion) | copy-start | bytes 772
  11.5 51.8 %copy-start.62 = (pred[512,5]{0,1:T(8,128)(4,1)}, pred[512,5]{0,1:T(8,128)(4,1)S(1)}, u32[]{:S(2)}) copy-start(pred[512,5]{0,1:T(8,128)(4,1)S(1)} %get-tuple-element.181) | copy-start | bytes 7684
  11.5 51.8 %copy-start.63 = (pred[512,5]{0,1:T(8,128)(4,1)}, pred[512,5]{0,1:T(8,128)(4,1)S(1)}, u32[]{:S(2)}) copy-start(pred[512,5]{0,1:T(8,128)(4,1)S(1)} %get-tuple-element.180) | copy-start | bytes 7684
  75.4 42.8 %copy-start.23 = (bf16[128,1024]{1,0:T(8,128)(2,1)S(1)}, bf16[128,1024]{1,0:T(8,128)(2,1)}, u32[]{:S(2)}) copy-start(bf16[128,1024]{1,0:T(8,128)(2,1)} %param.18) | copy-start | bytes 786436
  75.4 710.0 %copy-start.55 = (f32[1024]{0:T(1024)}, f32[1024]{0:T(1024)S(1)}, u32[]{:S(2)}) copy-start(f32[1024]{0:T(1024)S(1)} %convert_element_type.162) | copy-start | bytes 12292
  119.3 666.1 %copy-start.67 = (f32[128]{0:T(128)}, f32[128]{0:T(128)S(1)}, u32[]{:S(2)}) copy-start(f32[128]{0:T(128)S(1)} %add_rsqrt_fusion.1) | copy-start | bytes 1540
  137.2 144.3 %copy-start.34 = (bf16[3,1024,128]{2,1,0:T(8,128)(2,1)S(1)}, bf16[3,1024,128]{2,1,0:T(8,128)(2,1)}, u32[]{:S(2)}) copy-start(bf16[3,1024,128]{2,1,0:T(8,128)(2,1)} %param.31) | copy-start | bytes 2359300
  288.5 141.5 %all-to-all-start.1 = ((bf16[32,96,1024]{2,1,0:T(8,128)(2,1)}), bf16[32,96,1024]{2,1,0:T(8,128)(2,1)}, u32[]{:S(2)}, u32[]{:S(2)}) async-start(bf16[32,96,1024]{2,1,0:T(8,128)(2,1)} %bitcast.166), calls=%async_computation.2 | async-start | bytes 12582912 | tf_op jit(solution)/shard_map/all_to_all | solution.py:357
  471.0 144.4 %copy-start.20 = (f32[3,32,32,128]{3,2,1,0:T(8,128)S(1)}, f32[3,32,32,128]{3,2,1,0:T(8,128)}, u32[]{:S(2)}) copy-start(f32[3,32,32,128]{3,2,1,0:T(8,128)} %copy-done.19) | copy-start | bytes 4718596
  471.0 144.3 %copy-start.31 = (bf16[3,128,1024]{2,1,0:T(8,128)(2,1)S(1)}, bf16[3,128,1024]{2,1,0:T(8,128)(2,1)}, u32[]{:S(2)}) copy-start(bf16[3,128,1024]{2,1,0:T(8,128)(2,1)} %param.32) | copy-start | bytes 2359300
  624.0 141.4 %all-to-all-start.3 = ((bf16[32,96,1024]{2,1,0:T(8,128)(2,1)}), bf16[32,96,1024]{2,1,0:T(8,128)(2,1)}, u32[]{:S(2)}, u32[]{:S(2)}) async-start(bf16[32,96,1024]{2,1,0:T(8,128)(2,1)} %bitcast.167), calls=%async_computation.4 | async-start | bytes 12582912 | tf_op jit(solution)/shard_map/all_to_all | solution.py:412
  628.6 188.9 %all-gather.5.cloned.1.call-start = ((), (), s32[]{:S(2)}) async-start(), calls=%async_computation.8 | async-start | bytes 1310720 | tf_op jit(solution)/shard_map/all_gather | solution.py:436
  787.1 149.7 %all-reduce.7.cloned.1.call-start = ((), (), s32[]{:S(2)}) async-start(), calls=%async_computation.11 | async-start | bytes 12582912 | tf_op jit(solution)/shard_map/psum | solution.py:453
  830.8 152.0 %reduce-scatter.5.cloned.1.call-start = ((), (), s32[]{:S(2)}) async-start(), calls=%async_computation.9 | async-start | bytes 2621440 | tf_op jit(solution)/shard_map/reduce_scatter | solution.py:450
  840.1 276.1 %all-reduce.5.cloned.1.call-start = ((), (), s32[]{:S(2)}) async-start(), calls=%async_computation.10 | async-start | bytes 786432 | tf_op jit(solution)/shard_map/psum | solution.py:456
  936.8 46.1 %copy-start.14 = (f32[128,1024]{1,0:T(8,128)S(1)}, f32[128,1024]{1,0:T(8,128)}, u32[]{:S(2)}) copy-start(f32[128,1024]{1,0:T(8,128)} %copy-done.13) | copy-start | bytes 1572868
  936.8 46.1 %copy-start.18 = (f32[128,1024]{1,0:T(8,128)S(1)}, f32[128,1024]{1,0:T(8,128)}, u32[]{:S(2)}) copy-start(f32[128,1024]{1,0:T(8,128)} %fusion) | copy-start | bytes 1572868
  936.8 46.1 %copy-start.56 = (f32[1024]{0:T(1024)S(1)}, f32[1024]{0:T(1024)}, u32[]{:S(2)}) copy-start(f32[1024]{0:T(1024)} %copy-done.55) | copy-start | bytes 12292
  936.8 46.1 %copy-start.68 = (f32[128]{0:T(128)S(1)}, f32[128]{0:T(128)}, u32[]{:S(2)}) copy-start(f32[128]{0:T(128)} %copy-done.67) | copy-start | bytes 1540
  936.8 46.1 %copy-start.72 = (f32[128]{0:T(128)S(1)}, f32[128]{0:T(128)}, u32[]{:S(2)}) copy-start(f32[128]{0:T(128)} %copy-done.71) | copy-start | bytes 1540
  (62 other events, 202.9 us)
Sparse Core Ops, SparseCore 0:
  10.2 48.6 all-gather.2
  75.5 42.5 reduce-scatter.2
  787.2 30.3 all-gather.4
  831.0 105.8 all-reduce.6
  939.0 43.8 reduce-scatter.4
  989.5 126.7 all-reduce.4
where the time goes:
time: 1140 us; the launch traced here: 1130 us
  waiting for transfers between devices  542 us (48%)
  blocking collectives  350 us (31%)
  local copies, waits for them, and re-layouts  128 us (11%)
  matrix products  47 us (4%)
  other arithmetic  36.5 us (3%)
  between operations  15.4 us (1%)
    all_to_all x1, blocking collectives, body(): lax.all_to_all(slot_grads, ('dp', 'head'), split_axis=0, concat_axis=0, t...  144 us
    all_to_all x1, blocking collectives, body(): lax.all_to_all(outgoing, ('dp', 'head'), split_axis=0, concat_axis=0, til...  142 us
    all_to_all x1, waiting for transfers between devices, body(): lax.all_to_all(row_grads, ('dp', 'head'), split_axis=0, concat_axis=0, ti...  136 us
    psum x1, waiting for transfers between devices, body(): lax.psum((grad_attend, grad_gain_expert, grad_router), ('dp', 'head'))  131 us
    all_to_all x1, waiting for transfers between devices, body(): lax.all_to_all(produced.reshape(buffer_shape), ('dp', 'head'), split_axis...  108 us
    all_gather x1, waiting for transfers between devices, gather_group(): return lax.all_gather(residual, 'head', axis=0, tiled=True)  47.3 us
    reduce_scatter x1, waiting for transfers between devices, body(): lax.psum_scatter(partial_value, 'head', scatter_dimension=0, tiled=True)  42.7 us
    psum x1, blocking collectives, body(): lax.psum((grad_attend, grad_gain_expert, grad_router), ('dp', 'head'))  39.4 us
  transfers between devices with their start and end apart: 8, of which 8 were waited for; matrix products, arithmetic and copies ran while one was open for 6% of the time, Pallas kernels for 0%

commit v1 on v0

v1 whole, which is shorter than its diff:
```python
import jax
import jax.numpy as jnp
from jax import lax
from jax.sharding import PartitionSpec as P

epsilon = 1e-06
theta = 10000.0
negative = -1e30
f32 = jnp.float32
bf16 = jnp.bfloat16
everywhere = ("dp", "head")
whole_rows = 4096


def product(left, right, left_axis, right_axis):
    return lax.dot_general(
        left, right, (((left_axis,), (right_axis,)), ((), ())), preferred_element_type=f32
    )


def rms_scale(residual):
    return lax.rsqrt(jnp.mean(residual * residual, axis=-1, keepdims=True) + epsilon)


def rotary_tables(row_count, head_width):
    half_width = head_width // 2
    position = jnp.arange(row_count, dtype=f32)[:, None]
    exponent = jnp.arange(half_width, dtype=f32)[None, :]
    angles = position * jnp.power(theta, -2.0 * exponent / head_width)
    return (jnp.cos(angles), jnp.sin(angles))


def rotate(matrix, cosine, sine):
    half = matrix.shape[-1] // 2
    first, second = matrix[:, :half], matrix[:, half:]
    return jnp.concatenate([first * cosine - second * sine, second * cosine + first * sine], axis=-1)


def pick_mask(picks, expert_count):
    hits = picks[:, 0, :, None] == jnp.arange(expert_count, dtype=jnp.int32)[None, None, :]
    return jnp.any(hits, axis=1).astype(f32)


def norm_back(residual, inverse, gain, incoming):
    unit_rows = residual * inverse
    scaled = incoming * gain
    gain_grad = jnp.sum(incoming * unit_rows, axis=0)
    row_grad = inverse * (scaled - unit_rows * jnp.mean(scaled * unit_rows, axis=-1, keepdims=True))
    return (row_grad, gain_grad)


def gelu_pair(value):
    inner = jnp.tanh(0.7978845608028654 * (value + 0.044715 * value * value * value))
    slope = 0.5 * (1.0 + inner) + 0.5 * value * (1.0 - inner * inner) * 0.7978845608028654 * (
        1.0 + 3.0 * 0.044715 * value * value
    )
    return (0.5 * value * (1.0 + inner), slope)


def body(
    hidden_in,
    segments,
    value_pick,
    output_pick,
    expert_pick,
    attend_gain,
    query_weight,
    key_weight,
    value_weight,
    output_weight,
    head_router,
    expert_gain,
    router,
    expert_in,
    expert_out,
    cotangent,
):
    tokens, features = hidden_in.shape
    per_device, _, width = expert_in.shape
    head_experts = head_router.shape[2] // 2
    head_width = query_weight.shape[2]
    scale = head_width ** (-0.5)
    query_mat, key_mat, value_mat = query_weight[0], key_weight[0], value_weight[0]
    output_mat, gate_mat = output_weight[0], head_router[0]
    value_mask = pick_mask(value_pick, head_experts)
    output_mask = pick_mask(output_pick, head_experts)
    attend_scale = attend_gain.astype(f32)
    expert_scale = expert_gain.astype(f32)
    me = lax.axis_index("dp") * lax.axis_size("head") + lax.axis_index("head")

    rows = lax.all_gather(hidden_in, "head", axis=0, tiled=True)
    grouped = rows.astype(f32)
    group = grouped.shape[0]
    inverse = rms_scale(grouped)
    normed = (grouped * inverse * attend_scale).astype(bf16)
    cosine, sine = rotary_tables(group, head_width)
    queries = rotate(product(normed, query_mat, 1, 0), cosine, sine).astype(bf16)
    key_rows = rotate(product(normed, key_mat, 1, 0), cosine, sine).astype(bf16)
    squash = jax.nn.sigmoid(product(normed, gate_mat, 1, 0))
    value_gates = squash[:, :head_experts] * value_mask
    output_gates = squash[:, head_experts:] * output_mask
    expert_values = product(rows, value_mat, 1, 0).reshape(group, head_experts, head_width)
    values = jnp.sum(expert_values * value_gates[:, :, None], axis=1).astype(bf16)
    places = jnp.arange(group, dtype=jnp.int32)
    allowed = (places[None, :] <= places[:, None]) & (segments[:, None] == segments[None, :])
    scores = jnp.where(allowed, product(queries, key_rows, 1, 1) * scale, negative)
    exponents = jnp.exp(scores - jnp.max(scores, axis=-1, keepdims=True))
    probabilities = exponents / jnp.sum(exponents, axis=-1, keepdims=True)
    attended = product(probabilities.astype(bf16), values, 1, 0)
    weighted = (
        (output_gates[:, :, None] * attended[:, None, :]).reshape(group, -1).astype(bf16)
    )
    middle = hidden_in.astype(f32) + lax.psum_scatter(
        product(weighted, output_mat, 1, 0).astype(bf16), "head", scatter_dimension=0, tiled=True
    ).astype(f32)
    middle_inverse = rms_scale(middle)
    middle_normed = (middle * middle_inverse * expert_scale).astype(bf16)
    mine = me * per_device + jnp.arange(per_device, dtype=jnp.int32)
    my_router = lax.dynamic_slice_in_dim(router, me * per_device, per_device, axis=1)
    in_mat = expert_in.transpose(1, 0, 2).reshape(features, per_device * width)
    out_mat = expert_out.reshape(per_device * width, features)

    def turn(running, own):
        own_rows, own_cot, own_picks = own
        all_cot = lax.all_gather(own_cot, everywhere, axis=0, tiled=True)
        all_picks = lax.all_gather(own_picks, everywhere, axis=0, tiled=True)
        all_rows = lax.all_gather(own_rows, everywhere, axis=0, tiled=True)
        mask = jnp.any(all_picks[:, :, None] == mine[None, None, :], axis=1).astype(f32)
        gates = jax.nn.sigmoid(product(all_rows, my_router, 1, 0))
        live = gates * mask
        act, slope = gelu_pair(product(all_rows, in_mat, 1, 0).reshape(-1, per_device, width))
        lifted = product(all_cot, out_mat, 1, 1).reshape(-1, per_device, width)
        dense_grad = (jnp.sum(act * lifted, axis=-1) * live * (1.0 - gates)).astype(bf16)
        act_live = (act * live[:, :, None]).astype(bf16).reshape(-1, per_device * width)
        hidden_grad = (slope * lifted * live[:, :, None]).astype(bf16)
        hidden_grad = hidden_grad.reshape(-1, per_device * width)
        part_out = product(act_live, out_mat, 1, 0).astype(bf16)
        part_grad = (
            product(hidden_grad, in_mat, 1, 1) + product(dense_grad, my_router, 1, 1)
        ).astype(bf16)
        back = lax.psum_scatter(part_grad, everywhere, scatter_dimension=0, tiled=True)
        forth = lax.psum_scatter(part_out, everywhere, scatter_dimension=0, tiled=True)
        grads = (
            product(all_rows, hidden_grad, 0, 0),
            product(act_live, all_cot, 0, 0),
            product(dense_grad, all_rows, 0, 0),
        )
        if running is not None:
            grads = jax.tree.map(jnp.add, running, grads)
        return grads, (forth, back)

    turns = max(1, lax.axis_size("dp") * lax.axis_size("head") * tokens // whole_rows)
    owned = (middle_normed, cotangent, expert_pick)
    if turns == 1:
        grads, (summed, normed_grad) = turn(None, owned)
    else:
        owned = jax.tree.map(lambda a: a.reshape(turns, -1, a.shape[1]), owned)
        zeros = (
            jnp.zeros(in_mat.shape, f32),
            jnp.zeros(out_mat.shape, f32),
            jnp.zeros((per_device, features), f32),
        )
        grads, sums = lax.scan(turn, zeros, owned)
        summed, normed_grad = (a.reshape(tokens, features) for a in sums)
    grad_in = grads[0].reshape(features, per_device, width).transpose(1, 0, 2)
    grad_out = grads[1].reshape(per_device, width, features)
    grad_router = lax.all_gather(grads[2], everywhere, axis=0, tiled=True).T
    output = middle + summed.astype(f32)
    incoming = cotangent.astype(f32)
    row_grad, grad_gain_expert = norm_back(
        middle, middle_inverse, expert_scale, normed_grad.astype(f32)
    )
    middle_grad = incoming + row_grad
    group_grads = lax.all_gather(middle_grad.astype(bf16), "head", axis=0, tiled=True)
    weighted_grad = product(group_grads, output_mat, 1, 1).reshape(group, head_experts, head_width)
    output_grad = product(weighted, group_grads, 0, 0)
    output_gate_grad = jnp.sum(weighted_grad * attended[:, None, :], axis=-1)
    attended_grad = jnp.sum(weighted_grad * output_gates[:, :, None], axis=1).astype(bf16)
    prob_grad = product(attended_grad, values, 1, 1)
    centre = jnp.sum(probabilities * prob_grad, axis=-1, keepdims=True)
    score_grad = (probabilities * (prob_grad - centre)).astype(bf16)
    query_grad = product(score_grad, key_rows, 1, 0) * scale
    key_grad = product(score_grad, queries, 0, 0) * scale
    values_grad = product(probabilities.astype(bf16), attended_grad, 0, 0)
    expert_grad = (value_gates[:, :, None] * values_grad[:, None, :]).reshape(group, -1).astype(bf16)
    value_gate_grad = jnp.sum(expert_values * values_grad[:, None, :], axis=-1)
    query_grad = rotate(query_grad, cosine, -sine).astype(bf16)
    key_grad = rotate(key_grad, cosine, -sine).astype(bf16)
    logit_grad = (
        jnp.concatenate([value_gate_grad * value_mask, output_gate_grad * output_mask], axis=1)
        * squash
        * (1.0 - squash)
    ).astype(bf16)
    head_grads = (
        product(normed, query_grad, 0, 0),
        product(normed, key_grad, 0, 0),
        product(rows, expert_grad, 0, 0),
        output_grad,
        product(normed, logit_grad, 0, 0),
    )
    head_grads = tuple(grad.astype(bf16) for grad in head_grads)
    head_grads = tuple(grad.astype(f32)[None] for grad in lax.psum(head_grads, "dp"))
    back = (
        product(query_grad, query_mat, 1, 1)
        + product(key_grad, key_mat, 1, 1)
        + product(logit_grad, gate_mat, 1, 1)
    )
    row_back, grad_attend = norm_back(grouped, inverse, attend_scale, back)
    partial = (row_back + product(expert_grad, value_mat, 1, 1)).astype(bf16)
    input_grad = middle_grad + lax.psum_scatter(
        partial, "head", scatter_dimension=0, tiled=True
    ).astype(f32)
    grad_attend, grad_gain_expert = lax.psum((grad_attend, grad_gain_expert), everywhere)
    return (
        output,
        input_grad,
        grad_attend,
        *head_grads,
        grad_gain_expert,
        grad_router,
        grad_in,
        grad_out,
    )


def solution(mesh):
    rows = P(everywhere, None)
    heads = P("head", None, None)
    experts = P(everywhere, None, None)
    picks = P("dp", "head", None)
    in_specs = (
        rows, P("dp"), picks, picks, rows, P(), heads, heads, heads, heads, heads,
        P(), P(), experts, experts, rows,
    )
    out_specs = (
        rows, rows, P(), heads, heads, heads, heads, heads, P(), P(), experts, experts,
    )
    return jax.shard_map(body, mesh=mesh, in_specs=in_specs, out_specs=out_specs, check_vma=False)
```

time: 1140 us -> 806 us (0.71)
  blocking collectives: 350 us -> 206 us
  local copies, waits for them, and re-layouts: 128 us -> 11.7 us
  waiting for transfers between devices: 542 us -> 438 us
  matrix products: 47 us -> 103 us
  other arithmetic: 36.5 us -> 21.9 us
    all_to_all x2 -> x0, blocking collectives: 286 us -> none  [the longest x1 144 us: body(): lax.all_to_all(slot_grads, ('dp', 'head'), split_axis=0, concat_axis=0, t...]
    all_to_all x2 -> x0, waiting for transfers between devices: 245 us -> none  [the longest x1 136 us: body(): lax.all_to_all(row_grads, ('dp', 'head'), split_axis=0, concat_axis=0, ti...]
    reduce_scatter x2 -> x4, waiting for transfers between devices: 76.2 us -> 309 us  [the longest x1 184 us: turn(): lax.psum_scatter(part_grad, everywhere, scatter_dimension=0, tiled=True)]
    psum x2 -> x1, waiting for transfers between devices: 144 us -> 0.01 us  [body(): lax.psum(head_grads, 'dp')]
    all_gather x0 -> x2, blocking collectives: none -> 142 us  [the longest x1 73 us: body(): grad_router = lax.all_gather(grads[2], everywhere, axis=0, tiled=True).T]
    gather x10 -> x0, local copies, waits for them, and re-layouts: 88.7 us -> none  [the longest x1 17.4 us: body(): gate_flat[owners][:, None] * gradient[token_of]]
    dot_general x17 -> x29, matrix products: 20.6 us -> 103 us  [product(): lax.dot_general(left, right, (((left_axis,), (right_axis,)), ((), ())), p...]
    all_gather x2 -> x4, waiting for transfers between devices: 77.2 us -> 127 us  [the longest x1 67.6 us: turn(): all_cot = lax.all_gather(own_cot, everywhere, axis=0, tiled=True)]
  transfers between devices with their start and end apart: 8 -> 9, of which waited for: 8 -> 8; matrix products, arithmetic and copies ran while one was open for 6% -> 9% of each run, Pallas kernels for 0% -> 0%
where the time goes in v1:
time: 806 us; the launch traced here: 799 us
  waiting for transfers between devices  438 us (54%)
  blocking collectives  206 us (26%)
  matrix products  103 us (13%)
  other arithmetic  21.9 us (3%)
  between operations  15.1 us (2%)
  local copies, waits for them, and re-layouts  11.7 us (1%)
    reduce_scatter x1, waiting for transfers between devices, turn(): lax.psum_scatter(part_grad, everywhere, scatter_dimension=0, tiled=True)  184 us
    dot_general x29, matrix products, product(): lax.dot_general(left, right, (((left_axis,), (right_axis,)), ((), ())), p...  103 us
    all_gather x1, blocking collectives, body(): grad_router = lax.all_gather(grads[2], everywhere, axis=0, tiled=True).T  73 us
    reduce_scatter x1, waiting for transfers between devices, turn(): lax.psum_scatter(part_out, everywhere, scatter_dimension=0, tiled=True)  71.1 us
    all_gather x1, blocking collectives, turn(): all_picks = lax.all_gather(own_picks, everywhere, axis=0, tiled=True)  69.5 us
    all_gather x1, waiting for transfers between devices, turn(): all_cot = lax.all_gather(own_cot, everywhere, axis=0, tiled=True)  67.6 us
    psum x1, blocking collectives, body(): lax.psum((grad_attend, grad_gain_expert), everywhere)  39.9 us
    all_gather x1, waiting for transfers between devices, body(): rows = lax.all_gather(hidden_in, 'head', axis=0, tiled=True)  28.4 us
  transfers between devices with their start and end apart: 9, of which 8 were waited for; matrix products, arithmetic and copies ran while one was open for 9% of the time, Pallas kernels for 0%

profile of v1, /device:TPU:0, one launch (start us, length us, event | category | flops | bytes accessed | tf_op | source)
XLA Modules:
  0.0 799.2 jit_solution(738262051244594514)
XLA Ops:
  11.9 28.4 %all-gather.6.cloned.1.call-done = bf16[512,1024]{1,0:T(8,128)(2,1)} async-done(((bf16[128,1024]{1,0:T(8,128)(2,1)}), bf16[512,1024]{1,0:T(8,128)(2,1)}) %all-gather.6.cloned.1.call-update) | async-done | bytes 1048592 | tf_op jit(solution)/shard_map/all_gather | solution.py:91
  56.4 26.7 %reduce-scatter.5.cloned.1.call-done = bf16[128,1024]{1,0:T(8,128)(2,1)} async-done(((bf16[512,1024]{1,0:T(8,128)(2,1)}), bf16[128,1024]{1,0:T(8,128)(2,1)}) %reduce-scatter.5.cloned.1.call-update) | async-done | bytes 262160 | tf_op jit(solution)/shard_map/reduce_scatter | solution.py:113
  87.8 69.5 %all_gather.20 = s32[4096,16]{0,1:T(8,128)S(1)} all-gather(s32[128,16]{0,1:T(8,128)S(1)} %copy-done.52), channel_id=1, replica_groups=mesh['dp'=8,'head'=4] {'dp','head'}, dimensions={0}, use_global_device_ids=true | all-gather | bytes 270336 | tf_op jit(solution)/shard_map/all_gather | solution.py:126
  157.6 6.3 all-gather.8.cloned.1.call-done
  163.9 6.5 broadcast_select_fusion
  170.3 5.5 fusion.7
  175.9 67.6 %all-gather.10.cloned.1.call-done = bf16[4096,1024]{1,0:T(8,128)(2,1)} async-done(((bf16[128,1024]{1,0:T(8,128)(2,1)}), bf16[4096,1024]{1,0:T(8,128)(2,1)}) %all-gather.10.cloned.1.call-update) | async-done | bytes 8388624 | tf_op jit(solution)/shard_map/all_gather | solution.py:125
  243.5 11.7 %multiply_reduce_fusion = (f32[4096,3]{0,1:T(4,128)S(1)}, bf16[4096,3,128]{0,2,1:T(8,128)(2,1)S(1)}) fusion(f32[4096,3,128]{0,2,1:T(8,128)} %fusion.7, f32[4096,3]{0,1:T(4,128)} %get-tuple-element.94, bf16[3,128,1024]{2,1,0:T(8,128)(2,1)} %param.30, bf16[4096,1024]{1,0:T(8,128)(2,1)} %all-gather.10.cloned.1.call-done), kind=kOutput, calls=%fused_computation.21 | convolution fusion | flops 3257389056 | bytes 18710528 | tf_op jit(solution)/shard_map/dot_general | solution.py:16
  255.2 8.2 %fusion.58 = f32[4096,1024,1]{1,0,2:T(8,128)} fusion(bf16[4096,3,128]{0,2,1:T(8,128)(2,1)S(1)} %get-tuple-element.73, bf16[3,1024,128]{2,1,0:T(8,128)(2,1)S(1)} %copy-done.9), kind=kOutput, calls=%fused_computation.86 | convolution fusion | flops 3221225472 | bytes 20709376 | tf_op jit(solution)/shard_map/dot_general | solution.py:16
  263.4 11.4 %fusion = bf16[4096,1024]{1,0:T(8,128)(2,1)} fusion(f32[4096,1024,1]{1,0,2:T(8,128)} %fusion.58, bf16[4096,3]{0,1:T(4,128)(2,1)S(1)} %multiply_convert_fusion.5, bf16[1024,96]{0,1:T(8,128)(2,1)} %param.28, s32[]{:T(128)S(6)} %select_n.8), kind=kOutput, calls=%fused_computation.1 | convolution fusion | flops 33554432 | bytes 25198596 | tf_op jit(solution)/shard_map/dot_general | solution.py:16
  275.0 184.5 %reduce-scatter.9.cloned.1.call-done = bf16[128,1024]{1,0:T(8,128)(2,1)} async-done(((bf16[4096,1024]{1,0:T(8,128)(2,1)}), bf16[128,1024]{1,0:T(8,128)(2,1)}) %reduce-scatter.9.cloned.1.call-update) | async-done | bytes 262160 | tf_op jit(solution)/shard_map/reduce_scatter | solution.py:141
  463.9 25.2 %all-gather.12.cloned.1.call-done = bf16[512,1024]{1,0:T(8,128)(2,1)} async-done(((bf16[128,1024]{1,0:T(8,128)(2,1)}), bf16[512,1024]{1,0:T(8,128)(2,1)}) %all-gather.12.cloned.1.call-update) | async-done | bytes 1048592 | tf_op jit(solution)/shard_map/all_gather | solution.py:174
  489.0 2.7 multiply_reduce_fusion.1
  502.7 11.4 %bitcast_convert_fusion = bf16[4096,1024]{1,0:T(8,128)(2,1)} fusion(bf16[3,128,1024]{2,1,0:T(8,128)(2,1)S(1)} %copy-done.65, f32[4096,3]{0,1:T(4,128)S(1)} %copy-done.34, f32[4096,3,128]{0,2,1:T(8,128)} %fusion.7), kind=kOutput, calls=%fused_computation.2 | convolution fusion | flops 3241148416 | bytes 15515648 | tf_op jit(solution)/shard_map/dot_general | solution.py:16
  514.5 4.7 convolution_bitcast_fusion
  519.3 73.0 %all-gather = f32[32,3,1024]{2,1,0:T(4,128)S(1)} all-gather(f32[1,3,1024]{2,1,0:T(4,128)S(1)} %convolution_bitcast_fusion), channel_id=1, replica_groups=mesh['dp'=8,'head'=4] {'dp','head'}, dimensions={0}, use_global_device_ids=true | all-gather | bytes 405504 | tf_op jit(solution)/shard_map/all_gather | solution.py:167
  598.1 8.9 %fusion.34 = f32[3,1024,128]{2,1,0:T(8,128)} fusion(bf16[4096,3,128]{0,2,1:T(8,128)(2,1)} %copy-done.6, bf16[4096,1024]{1,0:T(8,128)(2,1)} %all-gather.8.cloned.1.call-done), kind=kOutput, calls=%fused_computation.47 | convolution fusion | flops 3221225472 | bytes 13107200 | tf_op jit(solution)/shard_map/dot_general | solution.py:16
  607.0 10.5 %fusion.1 = f32[3,128,1024]{2,1,0:T(8,128)} fusion(bf16[4096,1024]{1,0:T(8,128)(2,1)} %all-gather.10.cloned.1.call-done, f32[4096,3]{0,1:T(4,128)S(1)} %copy-done.34, f32[4096,3,128]{0,2,1:T(8,128)} %fusion.7), kind=kOutput, calls=%fused_computation.5 | convolution fusion | flops 3236954112 | bytes 16302080 | tf_op jit(solution)/shard_map/dot_general | solution.py:16
  617.9 23.6 %psum.54 = bf16[1,1024,10]{1,2,0:T(8,128)(2,1)S(1)} all-reduce(bf16[1,1024,10]{1,2,0:T(8,128)(2,1)S(1)} %fusion.46), channel_id=1, replica_groups=mesh['dp'=8,'head'=4] {'dp'}, use_global_device_ids=true, to_apply=%region_25.26 | all-reduce | flops 10240 | bytes 40960 | tf_op jit(solution)/shard_map/psum | solution.py:202
  642.2 39.9 %all-reduce = (f32[1024]{0:T(1024)}, f32[1024]{0:T(1024)}) all-reduce(f32[1024]{0:T(1024)S(1)} %get-tuple-element.60, f32[1024]{0:T(1024)S(1)} %copy-done.50), channel_id=1, replica_groups=mesh['dp'=8,'head'=4] {'dp','head'}, use_global_device_ids=true, to_apply=%region_20.21 | all-reduce | flops 2048 | bytes 16384 | tf_op jit(solution)/shard_map/psum | solution.py:213
  685.6 2.9 copy.87
  688.5 3.2 broadcast_in_dim.37
  691.7 71.1 %reduce-scatter.7.cloned.1.call-done = bf16[128,1024]{1,0:T(8,128)(2,1)} async-done(((bf16[4096,1024]{1,0:T(8,128)(2,1)}), bf16[128,1024]{1,0:T(8,128)(2,1)}) %reduce-scatter.7.cloned.1.call-update) | async-done | bytes 262160 | tf_op jit(solution)/shard_map/reduce_scatter | solution.py:142
  762.8 27.1 %reduce-scatter.11.cloned.1.call-done = bf16[128,1024]{1,0:T(8,128)(2,1)} async-done(((bf16[512,1024]{1,0:T(8,128)(2,1)}), bf16[128,1024]{1,0:T(8,128)(2,1)}) %reduce-scatter.11.cloned.1.call-update) | async-done | bytes 262160 | tf_op jit(solution)/shard_map/reduce_scatter | solution.py:210
  (208 shorter events, 53.6 us)
Async XLA Ops:
  7.2 33.1 %all-gather.6.cloned.1.call-start = ((), (), s32[]{:S(2)}) async-start(), calls=%async_computation.4 | async-start | bytes 1310720 | tf_op jit(solution)/shard_map/all_gather | solution.py:91
  7.9 75.2 %reduce-scatter.5.cloned.1.call-start = ((), (), s32[]{:S(2)}) async-start(), calls=%async_computation.5 | async-start | bytes 1310720 | tf_op jit(solution)/shard_map/reduce_scatter | solution.py:113
  56.3 107.5 %all-gather.8.cloned.1.call-start = ((), (), s32[]{:S(2)}) async-start(), calls=%async_computation.6 | async-start | bytes 8650752 | tf_op jit(solution)/shard_map/all_gather | solution.py:127
  56.4 113.9 %copy-start.35 = (f32[1024]{0:T(1024)}, f32[1024]{0:T(1024)S(1)}, u32[]{:S(2)}) copy-start(f32[1024]{0:T(1024)S(1)} %convert_element_type.139) | copy-start | bytes 12292
  84.2 86.1 %copy-start.53 = (f32[128]{0:T(128)}, f32[128]{0:T(128)S(1)}, u32[]{:S(2)}) copy-start(f32[128]{0:T(128)S(1)} %add_rsqrt_fusion.1) | copy-start | bytes 1540
  86.0 157.4 %all-gather.10.cloned.1.call-start = ((), (), s32[]{:S(2)}) async-start(), calls=%async_computation.8 | async-start | bytes 8650752 | tf_op jit(solution)/shard_map/all_gather | solution.py:125
  86.6 372.9 %reduce-scatter.9.cloned.1.call-start = ((), (), s32[]{:S(2)}) async-start(), calls=%async_computation.9 | async-start | bytes 8650752 | tf_op jit(solution)/shard_map/reduce_scatter | solution.py:141
  274.9 184.6 %copy-start.5 = (bf16[128,1024]{1,0:T(8,128)(2,1)S(1)}, bf16[128,1024]{1,0:T(8,128)(2,1)}, u32[]{:S(2)}) copy-start(bf16[128,1024]{1,0:T(8,128)(2,1)} %reduce-scatter.5.cloned.1.call-done) | copy-start | bytes 786436
  274.9 184.6 %copy-start.36 = (f32[1024]{0:T(1024)S(1)}, f32[1024]{0:T(1024)}, u32[]{:S(2)}) copy-start(f32[1024]{0:T(1024)} %copy-done.35) | copy-start | bytes 12292
  274.9 184.6 %copy-start.54 = (f32[128]{0:T(128)S(1)}, f32[128]{0:T(128)}, u32[]{:S(2)}) copy-start(f32[128]{0:T(128)} %copy-done.53) | copy-start | bytes 1540
  274.9 186.5 %copy-start.10 = (bf16[128,1024]{1,0:T(8,128)(2,1)S(1)}, bf16[128,1024]{1,0:T(8,128)(2,1)}, u32[]{:S(2)}) copy-start(bf16[128,1024]{1,0:T(8,128)(2,1)} %param.31) | copy-start | bytes 786436
  274.9 188.7 %copy-start.4 = (f32[512,512]{1,0:T(8,128)S(1)}, f32[512,512]{1,0:T(8,128)}, u32[]{:S(2)}) copy-start(f32[512,512]{1,0:T(8,128)} %get-tuple-element.97) | copy-start | bytes 3145732
  274.9 188.7 %copy-start.56 = (f32[512]{0:T(512)S(1)}, f32[512]{0:T(512)}, u32[]{:S(2)}) copy-start(f32[512]{0:T(512)} %get-tuple-element.96) | copy-start | bytes 6148
  274.9 214.1 %copy-start.41 = (f32[512,5]{0,1:T(8,128)S(1)}, f32[512,5]{0,1:T(8,128)}, u32[]{:S(2)}) copy-start(f32[512,5]{0,1:T(8,128)} %copy-done.40) | copy-start | bytes 30724
  274.9 214.1 %all-gather.12.cloned.1.call-start = ((), (), s32[]{:S(2)}) async-start(), calls=%async_computation.10 | async-start | bytes 1310720 | tf_op jit(solution)/shard_map/all_gather | solution.py:174
  463.3 218.8 %all-reduce.4.cloned.1.call-start = ((), (), s32[]{:S(2)}) async-start(), calls=%async_computation.12 | async-start | bytes 6291456 | tf_op jit(solution)/shard_map/psum | solution.py:202
  502.6 260.2 %reduce-scatter.7.cloned.1.call-start = ((), (), s32[]{:S(2)}) async-start(), calls=%async_computation.7 | async-start | bytes 8650752 | tf_op jit(solution)/shard_map/reduce_scatter | solution.py:142
  514.2 79.0 %copy-start.45 = (pred[512,5]{0,1:T(8,128)(4,1)S(1)}, pred[512,5]{0,1:T(8,128)(4,1)}, u32[]{:S(2)}) copy-start(pred[512,5]{0,1:T(8,128)(4,1)} %copy-done.44) | copy-start | bytes 7684
  514.2 79.0 %copy-start.21 = (bf16[1,1024,128]{2,1,0:T(8,128)(2,1)S(1)}, bf16[1,1024,128]{2,1,0:T(8,128)(2,1)}, u32[]{:S(2)}) copy-start(bf16[1,1024,128]{2,1,0:T(8,128)(2,1)} %param.22) | copy-start | bytes 786436
  514.2 275.7 %reduce-scatter.11.cloned.1.call-start = ((), (), s32[]{:S(2)}) async-start(), calls=%async_computation.11 | async-start | bytes 1310720 | tf_op jit(solution)/shard_map/reduce_scatter | solution.py:210
  685.6 104.4 %copy-start.11 = (bf16[128,1024]{1,0:T(8,128)(2,1)S(1)}, bf16[128,1024]{1,0:T(8,128)(2,1)}, u32[]{:S(2)}) copy-start(bf16[128,1024]{1,0:T(8,128)(2,1)} %reduce-scatter.9.cloned.1.call-done) | copy-start | bytes 786436
  685.6 104.4 %copy-start.55 = (f32[128]{0:T(128)S(1)}, f32[128]{0:T(128)}, u32[]{:S(2)}) copy-start(f32[128]{0:T(128)} %copy-done.53) | copy-start | bytes 1540
  685.6 104.4 %copy-start.60 = (f32[128]{0:T(128)S(1)}, f32[128]{0:T(128)}, u32[]{:S(2)}) copy-start(f32[128]{0:T(128)} %copy-done.59) | copy-start | bytes 1540
  688.5 103.8 %copy-start.1 = (bf16[1,640,1024]{2,1,0:T(8,128)(2,1)S(1)}, bf16[1,640,1024]{2,1,0:T(8,128)(2,1)}, u32[]{:S(2)}) copy-start(bf16[1,640,1024]{2,1,0:T(8,128)(2,1)} %param.25) | copy-start | bytes 3932164
  (52 other events, 827.7 us)
Sparse Core Ops, SparseCore 0:
  9.6 30.6 all-gather.5
  56.4 26.6 reduce-scatter.4
  87.0 76.7 all-gather.7
  167.1 76.3 all-gather.9
  275.1 184.3 reduce-scatter.8
  463.4 25.5 all-gather.11
  502.8 70.4 all-reduce.3
  575.5 187.2 reduce-scatter.6
  765.1 24.7 reduce-scatter.10

commit v2 on v1

--- a/solution.py
+++ b/solution.py
@@ -1,6 +1,11 @@
+import functools
+
 import jax
 import jax.numpy as jnp
+import numpy as np
 from jax import lax
+from jax.experimental import pallas as pl
+from jax.experimental.pallas import tpu as pltpu
 from jax.sharding import PartitionSpec as P
 
 epsilon = 1e-06
@@ -10,6 +15,7 @@
 bf16 = jnp.bfloat16
 everywhere = ("dp", "head")
 whole_rows = 4096
+vmem_for_weights = 16 << 20
 
 
 def product(left, right, left_axis, right_axis):
@@ -223,6 +229,478 @@
     )
 
 
+MESH = pl.DeviceIdType.MESH
+VM = pl.BlockSpec(memory_space=pltpu.VMEM)
+ANY = pl.BlockSpec(memory_space=pl.ANY)
+NN = (((1,), (0,)), ((), ()))
+NT = (((1,), (1,)), ((), ()))
+TN = (((0,), (0,)), ((), ()))
+
+
+def dot(left, right, dims=NN):
+    return lax.dot_general(left, right, dims, preferred_element_type=f32)
+
+
+def at_block(block, count):
+    return pl.ds(pl.multiple_of(block * count, count), count)
+
+
+def remote(src, dst, send, recv, where):
+    return pltpu.make_async_remote_copy(
+        src_ref=src, dst_ref=dst, send_sem=send, recv_sem=recv, device_id=where, device_id_type=MESH
+    )
+
+
+def greet(places):
+    barrier = pltpu.get_barrier_semaphore()
+    for place in places:
+        pl.semaphore_signal(barrier, inc=1, device_id=place, device_id_type=MESH)
+    pl.semaphore_wait(barrier, len(places))
+
+
+def swap_halves(value):
+    half = value.shape[-1] // 2
+    return jnp.concatenate([value[:, half:], value[:, :half]], axis=-1)
+
+
+def attend_kernel(
+    n_dp,
+    n_head,
+    x_ref,
+    cot_ref,
+    mask_ref,
+    attend_gain_ref,
+    expert_gain_ref,
+    cos_ref,
+    sin_ref,
+    gate_mask_ref,
+    seg_row_ref,
+    seg_col_ref,
+    wq_ref,
+    wk_ref,
+    wg_ref,
+    wv_ref,
+    wo_ref,
+    in_ref,
+    out_ref,
+    all_in_ref,
+    all_out_ref,
+    all_cot_ref,
+    all_mask_ref,
+    mid_ref,
+    mr_ref,
+    rows_ref,
+    q_ref,
+    k_ref,
+    v_ref,
+    prob_ref,
+    vx_ref,
+    squash_ref,
+    att_ref,
+    w_an,
+    w_v,
+    w_o,
+    part,
+    got,
+    local_sem,
+    z_send,
+    z_recv,
+    p_send,
+    p_recv,
+):
+    d, h = lax.axis_index("dp"), lax.axis_index("head")
+    chip, core = d // 2, d % 2
+    chips = n_dp // 2
+    tokens, features = x_ref.shape
+    width = q_ref.shape[1]
+    experts = vx_ref.shape[1] // width
+    scale = width ** (-0.5)
+    group = tokens * n_head
+    steps = (2, 3, 1)
+    partner = (chip * 2 + 1 - core, h)
+
+    def along(step):
+        return (d, jnp.bitwise_xor(h, step))
+
+    def across(step):
+        return (jnp.bitwise_xor(chip, step) * 2 + core, h)
+
+    def local(src, dst, number):
+        return pltpu.make_async_copy(src, dst, local_sem.at[number])
+
+    per_device = in_ref.shape[0]
+    slab = per_device * width
+    out_slot = lambda place, side: all_out_ref.at[place, at_block(side, slab), :]
+    in_slot = lambda place, side, e: all_in_ref.at[
+        place, :, at_block(side * per_device + e, width)
+    ]
+    loads = [
+        local(wq_ref, w_an.at[:, pl.ds(0, width)], 0),
+        local(wk_ref, w_an.at[:, pl.ds(width, width)], 1),
+        local(wg_ref, w_an.at[:, pl.ds(2 * width, width)], 2),
+        local(wv_ref, w_v, 3),
+        local(wo_ref, w_o, 4),
+        local(cot_ref, all_cot_ref.at[at_block(h, tokens), :], 5),
+        local(mask_ref.at[h], all_mask_ref.at[at_block(h, tokens), :], 6),
+        local(out_ref, out_slot(chip, core), 7),
+    ] + [local(in_ref.at[e], in_slot(chip, core, e), 8 + e) for e in range(per_device)]
+    for load in loads:
+        load.start()
+    greet([along(s) for s in steps] + [partner] + [across(s) for s in range(1, chips)])
+
+    def spread(kind, src, dst_of, order=steps):
+        copies = {}
+        for step in order:
+            copies[step] = remote(
+                src(step),
+                dst_of(step),
+                z_send.at[kind, step - 1],
+                z_recv.at[kind, step - 1],
+                along(step),
+            )
+            copies[step].start()
+        return copies
+
+    x_copies = spread(0, lambda s: x_ref, lambda s: rows_ref.at[at_block(h, tokens), :])
+
+    def weights_to(where, slot, place, side, own):
+        pieces = [
+            remote(
+                out_ref if own else out_slot(place, side),
+                out_slot(place, side),
+                p_send.at[slot, 0],
+                p_recv.at[slot, 0],
+                where,
+            )
+        ]
+        for e in range(per_device):
+            pieces.append(
+                remote(
+                    in_ref.at[e] if own else in_slot(place, side, e),
+                    in_slot(place, side, e),
+                    p_send.at[slot, 1 + e],
+                    p_recv.at[slot, 1 + e],
+                    where,
+                )
+            )
+        return pieces
+
+    first = [weights_to(across(s), s, chip, core, True) for s in range(1, chips)]
+    first.append(weights_to(partner, 0, chip, core, True))
+    for piece in range(1 + per_device):
+        for pieces in first:
+            pieces[piece].start()
+    mask_copies = spread(
+        1,
+        lambda s: mask_ref.at[jnp.bitwise_xor(h, s)],
+        lambda s: all_mask_ref.at[at_block(h, tokens), :],
+    )
+
+    rows_ref[at_block(h, tokens), :] = x_ref[...]
+    for load in loads[:5]:
+        load.wait()
+
+    def project(block):
+        at = at_block(block, tokens)
+        rows = rows_ref[at, :]
+        wide = rows.astype(f32)
+        inverse = lax.rsqrt(jnp.mean(wide * wide, axis=-1, keepdims=True) + epsilon)
+        normed = (wide * inverse * attend_gain_ref[...]).astype(bf16)
+        qkg = dot(normed, w_an[...])
+        cosine, sine = cos_ref[at, :], sin_ref[at, :]
+        q, k = qkg[:, :width], qkg[:, width : 2 * width]
+        q_ref[at, :] = (q * cosine + swap_halves(q) * sine).astype(bf16)
+        k_ref[at, :] = (k * cosine + swap_halves(k) * sine).astype(bf16)
+        squash = jax.nn.sigmoid(qkg[:, 2 * width :])
+        squash_ref[at, :] = squash
+        gates = squash * gate_mask_ref[at, :]
+        vx = dot(rows, w_v[...])
+        vx_ref[at, :] = vx
+        value = gates[:, 0:1] * vx[:, :width]
+        for e in range(1, experts):
+            value += gates[:, e : e + 1] * vx[:, e * width : (e + 1) * width]
+        v_ref[at, :] = value.astype(bf16)
+
+    project(h)
+    for step in (1, 2, 3):
+        x_copies[step].wait_recv()
+        project(jnp.bitwise_xor(h, step))
+    for step in steps:
+        x_copies[step].wait_send()
+    cot_copies = spread(2, lambda s: cot_ref, lambda s: all_cot_ref.at[at_block(h, tokens), :])
+
+    def attend(block):
+        at = at_block(block, tokens)
+        scores = dot(q_ref[at, :], k_ref[...], NT) * scale
+        row = block * tokens + lax.broadcasted_iota(jnp.int32, (tokens, group), 0)
+        column = lax.broadcasted_iota(jnp.int32, (tokens, group), 1)
+        allowed = (column <= row) & (seg_col_ref[at, :] == seg_row_ref[...])
+        scores = jnp.where(allowed, scores, negative)
+        exponents = jnp.exp(scores - jnp.max(scores, axis=-1, keepdims=True))
+        prob = exponents / jnp.sum(exponents, axis=-1, keepdims=True)
+        prob_ref[at, :] = prob
+        att = dot(prob.astype(bf16), v_ref[...])
+        att_ref[at, :] = att
+        gates = squash_ref[at, :] * gate_mask_ref[at, :]
+        wide = jnp.concatenate(
+            [(gates[:, experts + e : experts + e + 1] * att).astype(bf16) for e in range(experts)],
+            axis=-1,
+        )
+        return dot(wide, w_o[...])
+
+    part_copies = {}
+    for step in steps:
+        part[step - 1] = attend(jnp.bitwise_xor(h, step)).astype(bf16)
+        part_copies[step] = remote(
+            part.at[step - 1],
+            got.at[step - 1],
+            z_send.at[3, step - 1],
+            z_recv.at[3, step - 1],
+            along(step),
+        )
+        part_copies[step].start()
+    middle = x_ref[...].astype(f32) + attend(h)
+    for step in steps:
+        part_copies[step].wait_recv()
+    for step in steps:
+        middle += got[step - 1].astype(f32)
+    mid_ref[...] = middle
+    inverse = lax.rsqrt(jnp.mean(middle * middle, axis=-1, keepdims=True) + epsilon)
+    mr_ref[...] = (middle * inverse * expert_gain_ref[...]).astype(bf16)
+    for step in steps:
+        part_copies[step].wait_send()
+
+    onward = []
+    for s in range(1, chips):
+        place = jnp.bitwise_xor(chip, s)
+        pieces = weights_to(partner, chips - 1 + s, place, core, False)
+        for piece in range(1 + per_device):
+            first[s - 1][piece].wait_recv()
+            pieces[piece].start()
+        onward.append(pieces)
+    for pieces in first[:-1]:
+        for piece in pieces:
+            piece.wait_send()
+    for pieces in [first[-1]] + onward:
+        for piece in pieces:
+            piece.wait()
+    for copies in (mask_copies, cot_copies):
+        for step in steps:
+            copies[step].wait()
+    for load in loads[5:]:
+        load.wait()
+
+
+def attend_call(n_dp, n_head, tokens, features, width, experts, per_device, args):
+    group = tokens * n_head
+    chips = n_dp // 2
+    slab = per_device * width
+    shape = jax.ShapeDtypeStruct
+    outs = [
+        (shape((chips, features, 2 * slab), bf16), ANY),
+        (shape((chips, 2 * slab, features), bf16), ANY),
+        (shape((group, features), bf16), ANY),
+        (shape((group, 128), bf16), ANY),
+        (shape((tokens, features), f32), VM),
+        (shape((tokens, features), bf16), VM),
+        (shape((group, features), bf16), VM),
+        (shape((group, width), bf16), VM),
+        (shape((group, width), bf16), VM),
+        (shape((group, width), bf16), VM),
+        (shape((group, group), f32), VM),
+        (shape((group, experts * width), f32), VM),
+        (shape((group, 128), f32), VM),
+        (shape((group, width), f32), VM),
+    ]
+    return pl.pallas_call(
+        functools.partial(attend_kernel, n_dp, n_head),
+        out_shape=[o[0] for o in outs],
+        out_specs=[o[1] for o in outs],
+        in_specs=[VM, ANY, VM] + [VM] * 7 + [ANY] * 7,
+        scratch_shapes=[
+            pltpu.VMEM((features, 3 * width), bf16),
+            pltpu.VMEM((features, experts * width), bf16),
+            pltpu.VMEM((experts * width, features), bf16),
+            pltpu.VMEM((n_head - 1, tokens, features), bf16),
+            pltpu.VMEM((n_head - 1, tokens, features), bf16),
+            pltpu.SemaphoreType.DMA((8 + per_device,)),
+            pltpu.SemaphoreType.DMA((4, n_head - 1)),
+            pltpu.SemaphoreType.DMA((4, n_head - 1)),
+            pltpu.SemaphoreType.DMA((2 * chips - 1, 1 + per_device)),
+            pltpu.SemaphoreType.DMA((2 * chips - 1, 1 + per_device)),
+        ],
+        compiler_params=pltpu.CompilerParams(
+            collective_id=1, has_side_effects=True, vmem_limit_bytes=40 << 20
+        ),
+    )(*args)
+
+
+def kernel_body(
+    n_dp,
+    n_head,
+    hidden_in,
+    segments,
+    value_pick,
+    output_pick,
+    expert_pick,
+    attend_gain,
+    query_weight,
+    key_weight,
+    value_weight,
+    output_weight,
+    head_router,
+    expert_gain,
+    router,
+    expert_in,
+    expert_out,
+    cotangent,
+):
+    tokens, features = hidden_in.shape
+    per_device, _, width = expert_in.shape
+    experts = head_router.shape[2] // 2
+    experts_total = router.shape[1]
+    slab = per_device * width
+    group = tokens * n_head
+    chips = n_dp // 2
+    d, h = lax.axis_index("dp"), lax.axis_index("head")
+    lanes = 128
+    owner = np.arange(n_dp * per_device)
+    ids = (owner // per_device * n_head)[None, :] + np.arange(n_head)[:, None]
+    ids = ids * per_device + owner % per_device
+    ids = np.pad(ids, ((0, 0), (0, lanes - ids.shape[1])), constant_values=-1).astype(np.int32)
+    mask4 = jnp.any(expert_pick[None, :, :, None] == ids[:, None, None, :], axis=2).astype(bf16)
+    angles = np.arange(group)[:, None] * theta ** (-2.0 * np.arange(width // 2) / width)[None, :]
+    cosine = np.concatenate([np.cos(angles)] * 2, axis=1).astype(np.float32)
+    sine = np.concatenate([-np.sin(angles), np.sin(angles)], axis=1).astype(np.float32)
+    slots = np.arange(lanes, dtype=np.int32)
+    gate_mask = (
+        jnp.any(value_pick[:, 0, :, None] == slots, axis=1)
+        | jnp.any(output_pick[:, 0, :, None] + experts == slots, axis=1)
+    ).astype(f32)
+    gate_mat = jnp.pad(head_router[0], ((0, 0), (0, lanes - head_router.shape[2])))
+    attend_scale = attend_gain.astype(f32)[None, :]
+    expert_scale = expert_gain.astype(f32)[None, :]
+    (all_in, all_out, all_cot, all_mask, middle, mr, rows, q, k, v, prob, vx, squash, att) = (
+        attend_call(
+            n_dp,
+            n_head,
+            tokens,
+            features,
+            width,
+            experts,
+            per_device,
+            (
+                hidden_in,
+                cotangent,
+                mask4,
+                attend_scale,
+                expert_scale,
+                cosine,
+                sine,
+                gate_mask,
+                segments[None, :],
+                segments[:, None],
+                query_weight[0],
+                key_weight[0],
+                gate_mat,
+                value_weight[0],
+                output_weight[0],
+                expert_in,
+                expert_out.reshape(slab, features),
+            ),
+        )
+    )
+    n_all = n_dp * per_device
+    in_mat = all_in.transpose(1, 0, 2).reshape(features, -1)
+    out_mat = all_out.reshape(-1, features)
+    r_ids = jnp.maximum(jnp.asarray(ids)[h], 0)
+    my_router = jnp.take(router, r_ids, axis=1)
+    mr_all = lax.all_gather(mr, "head", axis=0, tiled=True)
+    gates = jax.nn.sigmoid(product(mr_all, my_router, 1, 0))
+    live = gates * all_mask.astype(f32)
+    act, slope = gelu_pair(product(mr_all, in_mat, 1, 0).reshape(-1, n_all, width))
+    lifted = product(all_cot, out_mat, 1, 1).reshape(-1, n_all, width)
+    dz = (jnp.sum(act * lifted, axis=-1) * (live * (1.0 - gates))[:, :n_all]).astype(bf16)
+    act_live = (act * live[:, :n_all, None]).astype(bf16).reshape(group, -1)
+    hg = (slope * lifted * live[:, :n_all, None]).astype(bf16).reshape(group, -1)
+    part_out = product(act_live, out_mat, 1, 0).astype(bf16)
+    part_grad = (product(hg, in_mat, 1, 1) + product(dz, my_router[:, :n_all], 1, 1)).astype(bf16)
+    normed_grad = lax.psum_scatter(part_grad, "head", scatter_dimension=0, tiled=True)
+    summed = lax.psum_scatter(part_out, "head", scatter_dimension=0, tiled=True)
+    gi = product(mr_all, hg, 0, 0).reshape(features, n_dp, per_device, width).transpose(1, 2, 0, 3)
+    go = product(act_live, all_cot, 0, 0).reshape(n_dp, per_device, width, features)
+    grad_in = lax.psum_scatter(gi.astype(bf16), "dp", scatter_dimension=0, tiled=False).astype(f32)
+    grad_out = lax.psum_scatter(go.astype(bf16), "dp", scatter_dimension=0, tiled=False).astype(f32)
+    gr = lax.psum(product(dz, mr_all, 0, 0), "dp").reshape(n_dp, per_device, features)
+    gr = lax.all_gather(gr, "head", axis=1, tiled=False)
+    grad_router = gr.reshape(experts_total, features).T
+    output = middle + summed.astype(f32)
+    incoming = cotangent.astype(f32)
+    row_grad, grad_gain_expert = norm_back(
+        middle, rms_scale(middle), expert_scale[0], normed_grad.astype(f32)
+    )
+    middle_grad = incoming + row_grad
+    group_grads = lax.all_gather(middle_grad.astype(bf16), "head", axis=0, tiled=True)
+    query_mat, key_mat, value_mat = query_weight[0], key_weight[0], value_weight[0]
+    output_mat, gate10 = output_weight[0], head_router[0]
+    grouped = rows.astype(f32)
+    inverse = rms_scale(grouped)
+    normed = (grouped * inverse * attend_scale).astype(bf16)
+    scale = width ** (-0.5)
+    og = (squash * gate_mask)[:, experts : 2 * experts]
+    vg = (squash * gate_mask)[:, :experts]
+    weighted = (og[:, :, None] * att[:, None, :]).reshape(group, -1).astype(bf16)
+    weighted_grad = product(group_grads, output_mat, 1, 1).reshape(group, experts, width)
+    output_grad = product(weighted, group_grads, 0, 0)
+    ogg = jnp.sum(weighted_grad * att[:, None, :], axis=-1)
+    attended_grad = jnp.sum(weighted_grad * og[:, :, None], axis=1).astype(bf16)
+    prob_grad = product(attended_grad, v, 1, 1)
+    centre = jnp.sum(prob * prob_grad, axis=-1, keepdims=True)
+    score_grad = (prob * (prob_grad - centre)).astype(bf16)
+    query_grad = product(score_grad, k, 1, 0) * scale
+    key_grad = product(score_grad, q, 0, 0) * scale
+    values_grad = product(prob.astype(bf16), attended_grad, 0, 0)
+    expert_grad = (vg[:, :, None] * values_grad[:, None, :]).reshape(group, -1).astype(bf16)
+    vgg = jnp.sum(vx.reshape(group, experts, width) * values_grad[:, None, :], axis=-1)
+    c64, s64 = cosine[:, : width // 2], -sine[:, : width // 2]
+    query_grad = rotate(query_grad, c64, -s64).astype(bf16)
+    key_grad = rotate(key_grad, c64, -s64).astype(bf16)
+    sq = squash[:, : 2 * experts]
+    logit_grad = (
+        jnp.concatenate([vgg, ogg], axis=1) * gate_mask[:, : 2 * experts] * sq * (1.0 - sq)
+    ).astype(bf16)
+    head_grads = (
+        product(normed, query_grad, 0, 0),
+        product(normed, key_grad, 0, 0),
+        product(rows, expert_grad, 0, 0),
+        output_grad,
+        product(normed, logit_grad, 0, 0),
+    )
+    head_grads = tuple(grad.astype(bf16) for grad in head_grads)
+    head_grads = tuple(grad.astype(f32)[None] for grad in lax.psum(head_grads, "dp"))
+    back = (
+        product(query_grad, query_mat, 1, 1)
+        + product(key_grad, key_mat, 1, 1)
+        + product(logit_grad, gate10, 1, 1)
+    )
+    row_back, grad_attend = norm_back(grouped, inverse, attend_scale[0], back)
+    partial = (row_back + product(expert_grad, value_mat, 1, 1)).astype(bf16)
+    input_grad = middle_grad + lax.psum_scatter(
+        partial, "head", scatter_dimension=0, tiled=True
+    ).astype(f32)
+    grad_attend, grad_gain_expert = lax.psum((grad_attend, grad_gain_expert), everywhere)
+    return (
+        output,
+        input_grad,
+        grad_attend,
+        *head_grads,
+        grad_gain_expert,
+        grad_router,
+        grad_in,
+        grad_out,
+    )
+
+
 def solution(mesh):
     rows = P(everywhere, None)
     heads = P("head", None, None)
@@ -235,4 +713,12 @@
     out_specs = (
         rows, rows, P(), heads, heads, heads, heads, heads, P(), P(), experts, experts,
     )
-    return jax.shard_map(body, mesh=mesh, in_specs=in_specs, out_specs=out_specs, check_vma=False)
+    n_dp, n_head = mesh.shape["dp"], mesh.shape["head"]
+
+    def program(*args):
+        held = 2 * n_dp * args[13].shape[0] * args[13].shape[1] * args[13].shape[2] * 2
+        if n_head == 4 and held <= vmem_for_weights:
+            return kernel_body(n_dp, n_head, *args)
+        return body(*args)
+
+    return jax.shard_map(program, mesh=mesh, in_specs=in_specs, out_specs=out_specs, check_vma=False)

time: 806 us -> 564 us (0.70)
  waiting for transfers between devices: 438 us -> 244 us
  blocking collectives: 206 us -> 76.9 us
  Pallas kernels: 2.62 us -> 82 us
  local copies, waits for them, and re-layouts: 11.7 us -> 47 us
  matrix products: 103 us -> 69.6 us
    all_gather x2 -> x1, blocking collectives: 142 us -> 14.4 us  [kernel_body(): gr = lax.all_gather(gr, 'head', axis=1, tiled=False)]
    reduce_scatter x4 -> x5, waiting for transfers between devices: 309 us -> 196 us  [the longest x1 62.8 us: kernel_body(): lax.psum_scatter(go.astype(bf16), 'dp', scatter_dimension=0, tiled=False)]
    all_gather x4 -> x2, waiting for transfers between devices: 127 us -> 34.1 us  [the longest x1 18.7 us: kernel_body(): mr_all = lax.all_gather(mr, 'head', axis=0, tiled=True)]
    pallas_call x0 -> x1, Pallas kernels: none -> 82 us  [attend_call(): pl.pallas_call(functools.partial(attend_kernel, n_dp, n_head), out_shape=...]
    dot_general x29 -> x23, matrix products: 103 us -> 69.6 us  [product(): lax.dot_general(left, right, (((left_axis,), (right_axis,)), ((), ())), p...]
    psum x1 -> x2, waiting for transfers between devices: 0.01 us -> 13.6 us  [the longest x1 13.6 us: kernel_body(): lax.psum(product(dz, mr_all, 0, 0), 'dp')]
    unnamed x140 -> x109, local copies, waits for them, and re-layouts: 10.8 us -> 22.8 us
    transpose x0 -> x1, local copies, waits for them, and re-layouts: none -> 8.54 us  [kernel_body(): in_mat = all_in.transpose(1, 0, 2).reshape(features, -1)]
  transfers between devices with their start and end apart: 9 -> 9, of which waited for: 8 -> 8; matrix products, arithmetic and copies ran while one was open for 9% -> 14% of each run, Pallas kernels for 0% -> 0%
where the time goes in v2:
time: 564 us; the launch traced here: 563 us
  waiting for transfers between devices  244 us (43%)
  Pallas kernels  82 us (15%)
  blocking collectives  76.9 us (14%)
  matrix products  69.6 us (12%)
  local copies, waits for them, and re-layouts  47 us (8%)
  other arithmetic  27.7 us (5%)
  between operations  14.3 us (3%)
    pallas_call x1, Pallas kernels, attend_call(): pl.pallas_call(functools.partial(attend_kernel, n_dp, n_head), out_shape=...  82 us
    dot_general x23, matrix products, product(): lax.dot_general(left, right, (((left_axis,), (right_axis,)), ((), ())), p...  69.6 us
    reduce_scatter x1, waiting for transfers between devices, kernel_body(): lax.psum_scatter(go.astype(bf16), 'dp', scatter_dimension=0, tiled=False)  62.8 us
    reduce_scatter x1, waiting for transfers between devices, kernel_body(): lax.psum_scatter(gi.astype(bf16), 'dp', scatter_dimension=0, tiled=False)  61.9 us
    psum x1, blocking collectives, kernel_body(): lax.psum((grad_attend, grad_gain_expert), everywhere)  39.6 us
    reduce_scatter x1, waiting for transfers between devices, kernel_body(): lax.psum_scatter(partial, 'head', scatter_dimension=0, tiled=True)  28.1 us
    reduce_scatter x1, waiting for transfers between devices, kernel_body(): lax.psum_scatter(part_grad, 'head', scatter_dimension=0, tiled=True)  26.6 us
    psum x1, blocking collectives, kernel_body(): lax.psum(head_grads, 'dp')  22.9 us
  transfers between devices with their start and end apart: 9, of which 8 were waited for; matrix products, arithmetic and copies ran while one was open for 14% of the time, Pallas kernels for 0%

profile of v2, /device:TPU:0, one launch (start us, length us, event | category | flops | bytes accessed | tf_op | source)
XLA Modules:
  0.0 562.5 jit_solution(11611282878954049827)
XLA Ops:
  10.2 3.2 compare_reduce_fusion
  27.8 82.0 %shard_map.319 = (bf16[4,1024,768]{2,1,0:T(8,128)(2,1)}, bf16[4,768,1024]{2,1,0:T(8,128)(2,1)}, bf16[512,1024]{1,0:T(8,128)(2,1)S(1)}, bf16[512,128]{1,0:T(8,128...) custom-call(bf16[128,1024]{1,0:T(8,128)(2,1)S(1)} %copy-done.16, ...), custom_call_target="tpu_custom_call" | custom-call | tf_op jit(solution)/shard_map/pallas_call | solution.py:515
  116.8 8.5 %copy.91 = bf16[1024,4,768]{0,2,1:T(8,128)(2,1)} copy(bf16[1024,4,768]{2,0,1:T(8,128)(2,1)} %bitcast.130) | data formatting | bytes 12582912 | tf_op jit(solution)/shard_map/transpose | solution.py:614
  128.7 18.7 %all-gather.3.cloned.1.call-done = bf16[512,1024]{1,0:T(8,128)(2,1)} async-done(((bf16[128,1024]{1,0:T(8,128)(2,1)}), bf16[512,1024]{1,0:T(8,128)(2,1)}) %all-gather.3.cloned.1.call-update) | async-done | bytes 1048592 | tf_op jit(solution)/shard_map/all_gather | solution.py:618
  147.4 2.6 convert_multiply_fusion.4
  151.1 6.1 %fusion.34 = f32[512,24,128]{0,2,1:T(8,128)S(1)} fusion(bf16[24,128,1024]{2,1,0:T(8,128)(2,1)} %bitcast.131, bf16[512,1024]{1,0:T(8,128)(2,1)} %all-gather.3.cloned.1.call-done), kind=kOutput, calls=%fused_computation.61 | convolution fusion | flops 3221225472 | bytes 13631488 | tf_op jit(solution)/shard_map/dot_general | solution.py:22
  157.2 12.1 %multiply_reduce_fusion = (f32[512,24]{0,1:T(8,128)S(1)}, bf16[512,24,128]{0,2,1:T(8,128)(2,1)}, bf16[512,24,128]{0,2,1:T(8,128)(2,1)}) fusion(f32[512,24,128]{0,2,1:T(8,128)S(1)} %fusion.34, f32[512,24]{0,1:T(8,128)S(1)} %copy.93, bf16[24,128,1024]{2,1,0:T(8,128)(2,1)} %bitcast.140, bf16[512,1024]{1,0:T(8,128)(2,1)S(1)} %copy-done.29), kind=kOutput, calls=%fused_computation.12 | convolution fusion | flops 3260534784 | bytes 20021248 | tf_op jit(solution)/shard_map/dot_general | solution.py:22
  170.2 6.6 %fusion.75 = f32[512,1024]{1,0:T(8,128)S(1)} fusion(bf16[512,3072]{0,1:T(8,128)(2,1)} %bitcast.144, bf16[1024,3072]{0,1:T(8,128)(2,1)} %bitcast.132), kind=kOutput, calls=%fused_computation.130 | convolution fusion | flops 3221225472 | bytes 11534336 | tf_op jit(solution)/shard_map/dot_general | solution.py:22
  179.3 26.6 %reduce-scatter.8.cloned.1.call-done = bf16[128,1024]{1,0:T(8,128)(2,1)} async-done(((bf16[512,1024]{1,0:T(8,128)(2,1)}), bf16[128,1024]{1,0:T(8,128)(2,1)}) %reduce-scatter.8.cloned.1.call-update) | async-done | bytes 262160 | tf_op jit(solution)/shard_map/reduce_scatter | solution.py:628
  214.8 2.8 copy.98
  220.4 15.3 %all-gather.5.cloned.1.call-done = bf16[512,1024]{1,0:T(8,128)(2,1)} async-done(((bf16[128,1024]{1,0:T(8,128)(2,1)}), bf16[512,1024]{1,0:T(8,128)(2,1)}) %all-gather.5.cloned.1.call-update) | async-done | bytes 1048592 | tf_op jit(solution)/shard_map/all_gather | solution.py:643
  235.7 3.2 multiply_reduce_fusion.1
  248.3 8.2 %convolution_convert_fusion.3 = bf16[512,1024]{1,0:T(8,128)(2,1)} fusion(bf16[512,3072]{0,1:T(8,128)(2,1)} %bitcast.142, bf16[3072,1024]{1,0:T(8,128)(2,1)} %bitcast.141), kind=kOutput, calls=%fused_computation.35 | convolution fusion | flops 3221749760 | bytes 10485760 | tf_op jit(solution)/shard_map/dot_general | solution.py:22
  262.6 7.3 %convert_bitcast_fusion = bf16[8,3,1024,128]{3,2,1,0:T(8,128)(2,1)} fusion(bf16[8,3,128,512]{3,2,1,0:T(8,128)(2,1)} %bitcast.145, bf16[512,1024]{1,0:T(8,128)(2,1)S(1)} %copy-done.39), kind=kOutput, calls=%fused_computation.11 | convolution fusion | flops 3224371200 | bytes 10485760 | tf_op jit(solution)/shard_map/dot_general | solution.py:22
  271.1 7.2 %convolution_convert_fusion = bf16[8,3,128,1024]{3,2,1,0:T(8,128)(2,1)} fusion(bf16[8,3,128,512]{3,2,1,0:T(8,128)(2,1)} %bitcast.143, bf16[512,1024]{1,0:T(8,128)(2,1)S(1)} %copy-done.30), kind=kOutput, calls=%fused_computation.16 | convolution fusion | flops 3224371200 | bytes 10485760 | tf_op jit(solution)/shard_map/dot_general | solution.py:22
  278.3 13.6 %all-reduce.6.cloned.1.call-done = f32[8,1,3,1024]{3,2,0,1:T(4,128)} async-done(((f32[8,1,3,1024]{3,2,0,1:T(4,128)}), f32[8,1,3,1024]{3,2,0,1:T(4,128)}) %all-reduce.6.cloned.1.call-update) | async-done | bytes 98320 | tf_op jit(solution)/shard_map/psum | solution.py:634
  292.9 14.4 %all_gather.11 = f32[8,4,3,1024]{3,0,2,1:T(8,128)S(1)} all-gather(f32[8,1,3,1024]{3,0,2,1:T(8,128)S(1)} %copy.103), channel_id=1, replica_groups=mesh['dp'=8,'head'=4] {'head'}, dimensions={1}, use_global_device_ids=true | all-gather | bytes 491520 | tf_op jit(solution)/shard_map/all_gather | solution.py:635
  309.0 22.9 %psum.61 = bf16[1,1024,10]{1,2,0:T(8,128)(2,1)S(1)} all-reduce(bf16[1,1024,10]{1,2,0:T(8,128)(2,1)S(1)} %fusion.27), channel_id=1, replica_groups=mesh['dp'=8,'head'=4] {'dp'}, use_global_device_ids=true, to_apply=%region_21.22 | all-reduce | flops 10240 | bytes 40960 | tf_op jit(solution)/shard_map/psum | solution.py:680
  332.5 39.6 %all-reduce.1 = (f32[1024]{0:T(1024)}, f32[1024]{0:T(1024)}) all-reduce(f32[1024]{0:T(1024)S(1)} %get-tuple-element.88, f32[1024]{0:T(1024)S(1)} %get-tuple-element.92), channel_id=1, replica_groups=mesh['dp'=8,'head'=4] {'dp','head'}, use_global_device_ids=true, to_apply=%region_16.17 | all-reduce | flops 2048 | bytes 16384 | tf_op jit(solution)/shard_map/psum | solution.py:691
  379.4 16.7 %reduce-scatter.6.cloned.1.call-done = bf16[128,1024]{1,0:T(8,128)(2,1)} async-done(((bf16[512,1024]{1,0:T(8,128)(2,1)}), bf16[128,1024]{1,0:T(8,128)(2,1)}) %reduce-scatter.6.cloned.1.call-update) | async-done | bytes 262160 | tf_op jit(solution)/shard_map/reduce_scatter | solution.py:629
  396.1 28.1 %reduce-scatter.10.cloned.1.call-done = bf16[128,1024]{1,0:T(8,128)(2,1)} async-done(((bf16[512,1024]{1,0:T(8,128)(2,1)}), bf16[128,1024]{1,0:T(8,128)(2,1)}) %reduce-scatter.10.cloned.1.call-update) | async-done | bytes 262160 | tf_op jit(solution)/shard_map/reduce_scatter | solution.py:688
  426.5 61.9 %reduce-scatter.12.cloned.1.call-done = bf16[1,3,1024,128]{3,2,1,0:T(8,128)(2,1)} async-done(((bf16[8,3,1024,128]{3,2,1,0:T(8,128)(2,1)}), bf16[1,3,1024,128]{3,2,1,0:T(8,128)(2,1)}) %reduce-scatter.12.cloned.1.call-update) | async-done | bytes 786448 | tf_op jit(solution)/shard_map/reduce_scatter | solution.py:632
  490.8 62.8 %reduce-scatter.14.cloned.1.call-done = bf16[1,3,128,1024]{3,2,1,0:T(8,128)(2,1)} async-done(((bf16[8,3,128,1024]{3,2,1,0:T(8,128)(2,1)}), bf16[1,3,128,1024]{3,2,1,0:T(8,128)(2,1)}) %reduce-scatter.14.cloned.1.call-update) | async-done | bytes 786448 | tf_op jit(solution)/shard_map/reduce_scatter | solution.py:633
  553.6 2.5 bitcast_convert_fusion
  (188 shorter events, 75.1 us)
Async XLA Ops:
  7.2 118.2 %copy-start = (bf16[1024,96]{0,1:T(8,128)(2,1)S(1)}, bf16[1024,96]{0,1:T(8,128)(2,1)}, u32[]{:S(2)}) copy-start(bf16[1024,96]{0,1:T(8,128)(2,1)} %param.36) | copy-start | bytes 589828
  7.2 9.9 %copy-start.27 = (s32[512]{0:T(512)S(1)}, s32[512]{0:T(512)}, u32[]{:S(2)}) copy-start(s32[512]{0:T(512)} %param.25) | copy-start | bytes 6148
  7.2 9.9 %copy-start.2 = (bf16[128,1024]{1,0:T(8,128)(2,1)S(1)}, bf16[128,1024]{1,0:T(8,128)(2,1)}, u32[]{:S(2)}) copy-start(bf16[128,1024]{1,0:T(8,128)(2,1)} %cot_ref.1) | copy-start | bytes 786436
  7.2 140.2 %all-gather.3.cloned.1.call-start = ((), (), s32[]{:S(2)}) async-start(), calls=%async_computation.5 | async-start | bytes 1310720 | tf_op jit(solution)/shard_map/all_gather | solution.py:618
  116.6 89.3 %reduce-scatter.8.cloned.1.call-start = ((), (), s32[]{:S(2)}) async-start(), calls=%async_computation.7 | async-start | bytes 1310720 | tf_op jit(solution)/shard_map/reduce_scatter | solution.py:628
  116.8 8.6 %copy-start.49 = (s32[4,128]{1,0:T(4,128)S(1)}, s32[4,128]{1,0:T(4,128)}, u32[]{:S(2)}) copy-start(s32[4,128]{1,0:T(4,128)} %constant.75.clone) | copy-start | bytes 6148
  125.4 22.1 %copy-start.32 = (bf16[512,128]{1,0:T(8,128)(2,1)S(1)}, bf16[512,128]{1,0:T(8,128)(2,1)}, u32[]{:S(2)}) copy-start(bf16[512,128]{1,0:T(8,128)(2,1)} %copy-done.31) | copy-start | bytes 393220
  170.2 6.6 %copy-start.38 = (f32[512,24]{1,0:T(8,128)S(1)}, f32[512,24]{1,0:T(8,128)}, u32[]{:S(2)}) copy-start(f32[512,24]{1,0:T(8,128)} %copy.94) | copy-start | bytes 147460
  170.2 6.6 %copy-start.42 = (f32[512,128]{1,0:T(8,128)S(1)}, f32[512,128]{1,0:T(8,128)}, u32[]{:S(2)}) copy-start(f32[512,128]{1,0:T(8,128)} %get-tuple-element.119) | copy-start | bytes 786436
  179.1 56.7 %all-gather.5.cloned.1.call-start = ((), (), s32[]{:S(2)}) async-start(), calls=%async_computation.8 | async-start | bytes 1310720 | tf_op jit(solution)/shard_map/all_gather | solution.py:643
  179.3 33.4 %copy-start.47 = (f32[128]{0:T(128)}, f32[128]{0:T(128)S(1)}, u32[]{:S(2)}) copy-start(f32[128]{0:T(128)S(1)} %add_rsqrt_fusion.1) | copy-start | bytes 1540
  207.1 7.7 %copy-start.50 = (f32[128]{0:T(128)}, f32[128]{0:T(128)S(1)}, u32[]{:S(2)}) copy-start(f32[128]{0:T(128)S(1)} %broadcast_multiply_fusion.1) | copy-start | bytes 1540
  209.0 83.0 %all-reduce.6.cloned.1.call-start = ((), (), s32[]{:S(2)}) async-start(), calls=%async_computation.10 | async-start | bytes 262144 | tf_op jit(solution)/shard_map/psum | solution.py:634
  220.1 152.0 %all-reduce.8.cloned.1.call-start = ((), (), s32[]{:S(2)}) async-start(), calls=%async_computation.13 | async-start | bytes 6291456 | tf_op jit(solution)/shard_map/psum | solution.py:680
  248.2 147.9 %reduce-scatter.6.cloned.1.call-start = ((), (), s32[]{:S(2)}) async-start(), calls=%async_computation.6 | async-start | bytes 1310720 | tf_op jit(solution)/shard_map/reduce_scatter | solution.py:629
  248.3 8.3 %copy-start.46 = (f32[512,5]{0,1:T(8,128)S(1)}, f32[512,5]{0,1:T(8,128)}, u32[]{:S(2)}) copy-start(f32[512,5]{0,1:T(8,128)} %get-tuple-element.90) | copy-start | bytes 30724
  248.3 8.5 %copy-start.12 = (f32[512,128]{1,0:T(8,128)S(1)}, f32[512,128]{1,0:T(8,128)}, u32[]{:S(2)}) copy-start(f32[512,128]{1,0:T(8,128)} %copy-done.11) | copy-start | bytes 786436
  256.5 167.7 %reduce-scatter.10.cloned.1.call-start = ((), (), s32[]{:S(2)}) async-start(), calls=%async_computation.9 | async-start | bytes 1310720 | tf_op jit(solution)/shard_map/reduce_scatter | solution.py:688
  262.2 226.2 %reduce-scatter.12.cloned.1.call-start = ((), (), s32[]{:S(2)}) async-start(), calls=%async_computation.11 | async-start | bytes 7077888 | tf_op jit(solution)/shard_map/reduce_scatter | solution.py:632
  269.9 283.7 %reduce-scatter.14.cloned.1.call-start = ((), (), s32[]{:S(2)}) async-start(), calls=%async_computation.12 | async-start | bytes 7077888 | tf_op jit(solution)/shard_map/reduce_scatter | solution.py:633
  377.5 46.8 %copy-start.34 = (bf16[128,1024]{1,0:T(8,128)(2,1)S(1)}, bf16[128,1024]{1,0:T(8,128)(2,1)}, u32[]{:S(2)}) copy-start(bf16[128,1024]{1,0:T(8,128)(2,1)} %reduce-scatter.8.cloned.1.call-done) | copy-start | bytes 786436
  377.5 46.8 %copy-start.48 = (f32[128]{0:T(128)S(1)}, f32[128]{0:T(128)}, u32[]{:S(2)}) copy-start(f32[128]{0:T(128)} %copy-done.47) | copy-start | bytes 1540
  377.5 46.8 %copy-start.51 = (f32[128]{0:T(128)S(1)}, f32[128]{0:T(128)}, u32[]{:S(2)}) copy-start(f32[128]{0:T(128)} %copy-done.50) | copy-start | bytes 1540
  424.2 131.8 %copy-start.1 = (bf16[1024,96]{0,1:T(8,128)(2,1)S(1)}, bf16[1024,96]{0,1:T(8,128)(2,1)}, u32[]{:S(2)}) copy-start(bf16[1024,96]{0,1:T(8,128)(2,1)} %param.36) | copy-start | bytes 589828
  (38 other events, 60.2 us)
Sparse Core Ops, SparseCore 0:
  116.7 30.7 all-gather.2
  179.2 26.6 reduce-scatter.7
  209.1 26.5 all-gather.4
  239.5 52.4 all-reduce.5
  296.6 69.9 all-reduce.7
  368.8 27.2 reduce-scatter.5
  398.4 25.7 reduce-scatter.9
  428.0 60.4 reduce-scatter.11
  491.8 61.7 reduce-scatter.13

commit v3 on v2

--- a/solution.py
+++ b/solution.py
@@ -531,6 +531,786 @@
         ],
         compiler_params=pltpu.CompilerParams(
             collective_id=1, has_side_effects=True, vmem_limit_bytes=40 << 20
+        ),
+    )(*args)
+
+
+def expert_kernel(
+    n_dp,
+    n_head,
+    mr_ref,
+    mid_ref,
+    own_cot_ref,
+    all_mask_ref,
+    router_ref,
+    gain_ref,
+    all_cot_ref,
+    all_in_ref,
+    all_out_ref,
+    da_ref,
+    dmid_ref,
+    po_ref,
+    gr_ref,
+    eg_ref,
+    gi_ref,
+    go_ref,
+    w_in,
+    w_out,
+    cot,
+    rows,
+    rows_t,
+    lifted,
+    acts,
+    hids,
+    dzs,
+    part,
+    got,
+    local_sem,
+    store_sem,
+    z_send,
+    z_recv,
+):
+    d, h = lax.axis_index("dp"), lax.axis_index("head")
+    chips = n_dp // 2
+    tokens, features = mr_ref.shape
+    wide = w_in.shape[2]
+    slab = wide // 2
+    lanes = router_ref.shape[1]
+    width = 128
+    group = tokens * n_head
+    pair = 2 * tokens
+    column = 256
+
+    def along(step):
+        return (d, jnp.bitwise_xor(h, step))
+
+    def local(src, dst, number):
+        return pltpu.make_async_copy(src, dst, local_sem.at[number])
+
+    loads = [local(all_cot_ref, cot, 0)]
+    loads += [local(all_out_ref.at[j], w_out.at[j], 1 + j) for j in range(chips)]
+    loads += [local(all_in_ref.at[j], w_in.at[j], 1 + chips + j) for j in range(chips)]
+    for load in loads:
+        load.start()
+    greet([along(s) for s in (1, 2, 3)])
+    mr_copies = {}
+    for step in (1, 2, 3):
+        mr_copies[step] = remote(
+            mr_ref,
+            rows.at[at_block(h, tokens), :],
+            z_send.at[0, step - 1],
+            z_recv.at[0, step - 1],
+            along(step),
+        )
+        mr_copies[step].start()
+    rows[at_block(h, tokens), :] = mr_ref[...]
+
+    loads[0].wait()
+    for j in range(chips):
+        loads[1 + j].wait()
+
+    @pl.loop(0, chips)
+    def _(j):
+        lifted[j] = dot(cot[...], w_out[j], NT).astype(bf16)
+
+    for j in range(chips):
+        loads[1 + chips + j].wait()
+
+    def spread_lanes(j):
+        lane = lax.broadcasted_iota(jnp.int32, (lanes, wide), 1) // width
+        slot = lax.broadcasted_iota(jnp.int32, (lanes, wide), 0)
+        return jnp.where(slot == lane + j * (wide // width), 1.0, 0.0).astype(bf16)
+
+    def pair_of_blocks(number):
+        at = at_block(number, pair)
+        own = rows[at, :]
+        gates = jax.nn.sigmoid(dot(own, router_ref[...]))
+        live = gates * all_mask_ref[at, :].astype(f32)
+        high = live.astype(bf16)
+        low = (live - high.astype(f32)).astype(bf16)
+        both = jnp.concatenate([high, low], axis=-1)
+
+        def chip_step(j, sums):
+            pick = spread_lanes(j)
+            hidden = dot(own, w_in[j])
+            spread = dot(both, jnp.concatenate([pick, pick], axis=0))
+            lift = lifted[j, at, :].astype(f32)
+            square = hidden * hidden
+            inner = jnp.tanh(0.7978845608028654 * hidden * (1.0 + 0.044715 * square))
+            half = 0.5 * (1.0 + inner)
+            act = hidden * half
+            slope = half + act * (1.0 - inner) * (
+                0.7978845608028654 + (0.7978845608028654 * 3.0 * 0.044715) * square
+            )
+            acts[j, at, :] = (act * spread).astype(bf16)
+            hids[j, at, :] = (slope * (lift * spread)).astype(bf16)
+            return sums + dot((act * lift).astype(bf16), pick, NT)
+
+        sums = lax.fori_loop(0, chips, chip_step, jnp.zeros((pair, lanes), f32))
+        dz = (sums * live * (1.0 - gates)).astype(bf16)
+        dzs[at, :] = dz
+
+        @pl.loop(0, features // column)
+        def _(c):
+            part_of = at_block(c, column)
+            total = dot(dz, router_ref[part_of, :], NT)
+            for j in range(chips):
+                total += dot(hids[j, at, :], w_in[j, part_of, :], NT)
+            part[at, part_of] = total.astype(bf16)
+
+    def send_back(step):
+        where = jnp.bitwise_xor(h, step)
+        copy = remote(
+            part.at[at_block(where, tokens), :],
+            got.at[step - 1],
+            z_send.at[1, step - 1],
+            z_recv.at[1, step - 1],
+            along(step),
+        )
+        copy.start()
+        return copy
+
+    near = h // 2
+    mr_copies[1].wait_recv()
+    pair_of_blocks(near)
+    back = {1: send_back(1)}
+    mr_copies[2].wait_recv()
+    mr_copies[3].wait_recv()
+    pair_of_blocks(1 - near)
+    back[2], back[3] = send_back(2), send_back(3)
+
+    @pl.loop(0, features // column)
+    def _(c):
+        part_of = at_block(c, column)
+        total = dot(acts[0], w_out[0, :, part_of])
+        for j in range(1, chips):
+            total += dot(acts[j], w_out[j, :, part_of])
+        po_ref[:, part_of] = total.astype(bf16)
+
+    rows_t[...] = rows[...].T
+
+    @pl.loop(0, chips)
+    def _(j):
+        for side in range(2):
+            mine = pl.ds(side * slab, slab)
+            w_in[j, :, mine] = dot(rows_t[...], hids[j, :, mine]).astype(bf16)
+            w_out[j, mine, :] = dot(acts[j, :, mine], cot[...], TN).astype(bf16)
+
+    stores = []
+    for j in range(chips):
+        for side in range(2):
+            mine = pl.ds(side * slab, slab)
+            number = 2 * j + side
+            stores.append(
+                pltpu.make_async_copy(
+                    w_in.at[j, :, mine], gi_ref.at[number], store_sem.at[0, number]
+                )
+            )
+            stores.append(
+                pltpu.make_async_copy(
+                    w_out.at[j, mine, :], go_ref.at[number], store_sem.at[1, number]
+                )
+            )
+    for store in stores:
+        store.start()
+    gr_ref[...] = dot(dzs[...], rows[...], TN)[: gr_ref.shape[0]]
+
+    for step in (1, 2, 3):
+        back[step].wait_recv()
+    incoming = part[at_block(h, tokens), :].astype(f32)
+    for step in (1, 2, 3):
+        incoming += got[step - 1].astype(f32)
+    middle = mid_ref[...]
+    inverse = lax.rsqrt(jnp.mean(middle * middle, axis=-1, keepdims=True) + epsilon)
+    unit = middle * inverse
+    scaled = incoming * gain_ref[...]
+    eg_ref[...] = jnp.sum(incoming * unit, axis=0, keepdims=True)
+    dmid = own_cot_ref[...].astype(f32) + inverse * (
+        scaled - unit * jnp.mean(scaled * unit, axis=-1, keepdims=True)
+    )
+    dmid_ref[...] = dmid
+    da_ref[...] = dmid.astype(bf16)
+    for step in (1, 2, 3):
+        back[step].wait_send()
+        mr_copies[step].wait_send()
+    for store in stores:
+        store.wait()
+
+
+def expert_call(n_dp, n_head, tokens, features, width, per_device, args):
+    group = tokens * n_head
+    chips = n_dp // 2
+    slab = per_device * width
+    lanes = 128
+    named = -(-n_dp * per_device // 8) * 8
+    shape = jax.ShapeDtypeStruct
+    outs = [
+        (shape((tokens, features), bf16), VM),
+        (shape((tokens, features), f32), VM),
+        (shape((group, features), bf16), VM),
+        (shape((named, features), f32), VM),
+        (shape((1, features), f32), VM),
+        (shape((n_dp, features, slab), bf16), ANY),
+        (shape((n_dp, slab, features), bf16), ANY),
+    ]
+    return pl.pallas_call(
+        functools.partial(expert_kernel, n_dp, n_head),
+        out_shape=[o[0] for o in outs],
+        out_specs=[o[1] for o in outs],
+        in_specs=[VM] * 6 + [ANY] * 3,
+        scratch_shapes=[
+            pltpu.VMEM((chips, features, 2 * slab), bf16),
+            pltpu.VMEM((chips, 2 * slab, features), bf16),
+            pltpu.VMEM((group, features), bf16),
+            pltpu.VMEM((group, features), bf16),
+            pltpu.VMEM((features, group), bf16),
+            pltpu.VMEM((chips, group, 2 * slab), bf16),
+            pltpu.VMEM((chips, group, 2 * slab), bf16),
+            pltpu.VMEM((chips, group, 2 * slab), bf16),
+            pltpu.VMEM((group, lanes), bf16),
+            pltpu.VMEM((group, features), bf16),
+            pltpu.VMEM((n_head - 1, tokens, features), bf16),
+            pltpu.SemaphoreType.DMA((1 + 2 * chips,)),
+            pltpu.SemaphoreType.DMA((2, n_dp)),
+            pltpu.SemaphoreType.DMA((2, n_head - 1)),
+            pltpu.SemaphoreType.DMA((2, n_head - 1)),
+        ],
+        compiler_params=pltpu.CompilerParams(
+            collective_id=2, has_side_effects=True, vmem_limit_bytes=56 << 20
+        ),
+    )(*args)
+
+
+def grads_kernel(
+    n_dp,
+    n_head,
+    da_ref,
+    dmid_ref,
+    mid_ref,
+    po_ref,
+    gr_ref,
+    eg_ref,
+    rows_ref,
+    q_ref,
+    k_ref,
+    v_ref,
+    prob_ref,
+    vx_ref,
+    squash_ref,
+    att_ref,
+    gate_mask_ref,
+    cos_ref,
+    sin_ref,
+    attend_gain_ref,
+    wq_ref,
+    wk_ref,
+    wg_ref,
+    wv_ref,
+    wo_ref,
+    gi_ref,
+    go_ref,
+    output_ref,
+    grad_x_ref,
+    wide_ref,
+    fin_in_ref,
+    fin_out_ref,
+    w_an,
+    w_v,
+    w_o,
+    das,
+    normed,
+    normed_t,
+    rows_t,
+    inverses,
+    datt,
+    gate_grads,
+    probs,
+    scores,
+    qkz,
+    vgrads,
+    part,
+    got,
+    got_out,
+    gain_part,
+    gain_got,
+    sums,
+    core_got,
+    chip_got,
+    piece,
+    blocks,
+    own_in,
+    own_out,
+    core_in,
+    core_out,
+    hop_in,
+    hop_out,
+    last_in,
+    last_out,
+    local_sem,
+    z_send,
+    z_recv,
+    c_send,
+    c_recv,
+    e_send,
+    e_recv,
+    s_send,
+    s_recv,
+):
+    d, h = lax.axis_index("dp"), lax.axis_index("head")
+    chip, core = d // 2, d % 2
+    chips = n_dp // 2
+    tokens, features = da_ref.shape
+    width = q_ref.shape[1]
+    experts = vx_ref.shape[1] // width
+    scale = width ** (-0.5)
+    group = tokens * n_head
+    named = gr_ref.shape[0]
+    side = features // 2
+    slice_ = side // chips
+    steps = (2, 3, 1)
+    partner = (chip * 2 + 1 - core, h)
+    xor = jnp.bitwise_xor
+
+    def along(step):
+        return (d, xor(h, step))
+
+    def across(step):
+        return (xor(chip, step) * 2 + core, h)
+
+    def local(src, dst, number):
+        return pltpu.make_async_copy(src, dst, local_sem.at[number])
+
+    loads = [
+        local(wo_ref, w_o, 0),
+        local(wq_ref, w_an.at[:, pl.ds(0, width)], 1),
+        local(wk_ref, w_an.at[:, pl.ds(width, width)], 2),
+        local(wg_ref, w_an.at[:, pl.ds(2 * width, width)], 3),
+        local(wv_ref, w_v, 4),
+    ]
+    order = (3, 1, 2, 0)
+    mine = {}
+    for n, s in enumerate(order):
+        place = xor(chip, s)
+        mine[s] = (
+            local(gi_ref.at[2 * place + core], own_in.at[place], 5 + 2 * n),
+            local(go_ref.at[2 * place + core], own_out.at[place], 6 + 2 * n),
+        )
+    for load in loads + [m for s in order for m in mine[s]]:
+        load.start()
+    greet([along(s) for s in steps] + [partner] + [across(s) for s in range(1, chips)])
+
+    def spread(kind, src, dst, send=steps):
+        copies = {}
+        for step in send:
+            copies[step] = remote(
+                src(step), dst(step), z_send.at[kind, step - 1], z_recv.at[kind, step - 1], along(step)
+            )
+            copies[step].start()
+        return copies
+
+    da_copies = spread(0, lambda s: da_ref, lambda s: das.at[at_block(h, tokens), :])
+    theirs = {}
+    for n, s in enumerate(order):
+        place = xor(chip, s)
+        theirs[s] = (
+            remote(
+                gi_ref.at[2 * place + 1 - core], core_in.at[place], c_send.at[0, n], c_recv.at[0, n], partner
+            ),
+            remote(
+                go_ref.at[2 * place + 1 - core], core_out.at[place], c_send.at[1, n], c_recv.at[1, n], partner
+            ),
+        )
+        for copy in theirs[s]:
+            copy.start()
+
+    def section(number, first, count):
+        at = pl.ds(first, count)
+        col = lambda c, j: at_block(c * chips + j, slice_)
+        state = {}
+
+        def start():
+            state["core"] = remote(
+                sums.at[at, at_block(1 - core, side)],
+                core_got.at[at, :],
+                s_send.at[number, 0],
+                s_recv.at[number, 0],
+                partner,
+            )
+            state["core"].start()
+
+        def mid():
+            state["core"].wait()
+            half = at_block(core, side)
+            sums[at, half] = sums[at, half] + core_got[at, :]
+            state["chips"] = []
+            for s in range(1, chips):
+                copy = remote(
+                    sums.at[at, col(core, xor(chip, s))],
+                    chip_got.at[s - 1, at, :],
+                    s_send.at[number, s],
+                    s_recv.at[number, s],
+                    across(s),
+                )
+                copy.start()
+                state["chips"].append(copy)
+
+        def add():
+            for copy in state["chips"]:
+                copy.wait()
+            total = sums[at, col(core, chip)].astype(f32)
+            for s in range(1, chips):
+                total += chip_got[s - 1, at, :].astype(f32)
+            piece[at, :] = total.astype(bf16)
+
+        def share(src=None, dst=None, at_dst=None):
+            src = piece.at[at, :] if src is None else src
+            dst = wide_ref if dst is None else dst
+            at_dst = at if at_dst is None else at_dst
+            state["end"] = (dst, at_dst)
+            mine = remote(
+                src,
+                dst.at[at_dst, col(core, chip)],
+                s_send.at[number, chips],
+                s_recv.at[number, chips],
+                partner,
+            )
+            mine.start()
+            own = pltpu.make_async_copy(
+                src, dst.at[at_dst, col(core, chip)], s_send.at[number, 3 * chips - 1]
+            )
+            own.start()
+            state["share"] = []
+            for s in range(1, chips):
+                copy = remote(
+                    src,
+                    dst.at[at_dst, col(core, chip)],
+                    s_send.at[number, chips + s],
+                    s_recv.at[number, chips + s],
+                    across(s),
+                )
+                copy.start()
+                state["share"].append(copy)
+            state["wait"] = [mine, own]
+
+        def forward():
+            dst, at_dst = state["end"]
+            for s in range(1, chips):
+                state["share"][s - 1].wait()
+                here = dst.at[at_dst, col(core, xor(chip, s))]
+                copy = remote(
+                    here,
+                    here,
+                    s_send.at[number, 2 * chips - 1 + s],
+                    s_recv.at[number, 2 * chips - 1 + s],
+                    partner,
+                )
+                copy.start()
+                state["wait"].append(copy)
+
+        def end():
+            for copy in state["wait"]:
+                copy.wait()
+
+        return start, mid, add, share, forward, end
+
+    top = features + w_o.shape[0]
+    small = -(-(named + 1) // 16) * 16
+    of_o = section(0, features, w_o.shape[0])
+    of_d = section(1, 0, features)
+    of_g = section(2, top + 16, small)
+    of_a = section(3, top, 16)
+
+    sums[pl.ds(top + 16, small), :] = jnp.concatenate(
+        [gr_ref[...], eg_ref[...], jnp.zeros((small - named - 1, features), f32)], axis=0
+    ).astype(bf16)
+    of_g[0]()
+
+    for block in range(n_head):
+        at = pl.ds(block * tokens, tokens)
+        wide = rows_ref[at, :].astype(f32)
+        inverse = lax.rsqrt(jnp.mean(wide * wide, axis=-1, keepdims=True) + epsilon)
+        inverses[at, :] = jnp.broadcast_to(inverse, (tokens, width))
+        normed[at, :] = (wide * inverse * attend_gain_ref[...]).astype(bf16)
+    normed_t[...] = normed[...].T
+    rows_t[...] = rows_ref[...].T
+    das[at_block(h, tokens), :] = da_ref[...]
+    for load in loads:
+        load.wait()
+
+    halves_in = (pl.ds(0, features // 2), pl.ds(features // 2, features // 2))
+    slab = own_out.shape[1]
+    halves_out = (pl.ds(0, slab // 2), pl.ds(slab // 2, slab // 2))
+    hops = {}
+
+    def hop(half, index, place, toward):
+        copies = (
+            remote(
+                own_in.at[place, halves_in[half], :],
+                hop_in.at[half, index],
+                e_send.at[0, 2 * half + index],
+                e_recv.at[0, 2 * half + index],
+                across(toward),
+            ),
+            remote(
+                own_out.at[place, halves_out[half], :],
+                hop_out.at[half, index],
+                e_send.at[1, 2 * half + index],
+                e_recv.at[1, 2 * half + index],
+                across(toward),
+            ),
+        )
+        for copy in copies:
+            copy.start()
+        hops[half, index] = copies
+
+    for s in order:
+        place = xor(chip, s)
+        for copy in mine[s] + theirs[s]:
+            copy.wait()
+        own_in[place] = own_in[place] + core_in[place]
+        own_out[place] = own_out[place] + core_out[place]
+        if s == 3:
+            hop(0, 1, place, 1)
+            hop(1, 1, place, 2)
+        elif s:
+            hop(s - 1, 0, place, s)
+
+    of_g[1]()
+
+    lane = lax.broadcasted_iota(jnp.int32, (tokens, width), 1)
+
+    def through_output(block):
+        at = at_block(block, tokens)
+        wide = dot(das[at, :], w_o[...], NT)
+        gates = squash_ref[at, :] * gate_mask_ref[at, :]
+        att = att_ref[at, :]
+        total = jnp.zeros((tokens, width), f32)
+        gate = jnp.zeros((tokens, width), f32)
+        for e in range(experts):
+            one = wide[:, e * width : (e + 1) * width]
+            total += gates[:, experts + e : experts + e + 1] * one
+            gate = jnp.where(
+                lane == experts + e, jnp.sum(one * att, axis=-1, keepdims=True), gate
+            )
+        datt[at, :] = total.astype(bf16)
+        gate_grads[at, :] = gate
+
+    through_output(h)
+    for step in (1, 2, 3):
+        da_copies[step].wait_recv()
+        through_output(xor(h, step))
+    for step in steps:
+        da_copies[step].wait_send()
+    out_copies = spread(1, lambda s: po_ref.at[at_block(xor(h, s), tokens), :], lambda s: got_out.at[s - 1])
+
+    gates = squash_ref[...] * gate_mask_ref[...]
+    for e in range(experts):
+        one = (gates[:, experts + e : experts + e + 1] * att_ref[...]).astype(bf16)
+        sums[pl.ds(features + e * width, width), :] = dot(one, das[...], TN).astype(bf16)
+    of_o[0]()
+
+    @pl.loop(0, n_head)
+    def _(block):
+        at = at_block(block, tokens)
+        prob = prob_ref[at, :]
+        dprob = dot(datt[at, :], v_ref[...], NT)
+        centre = jnp.sum(prob * dprob, axis=-1, keepdims=True)
+        scores[at, :] = (prob * (dprob - centre)).astype(bf16)
+        probs[at, :] = prob.astype(bf16)
+
+    dq = dot(scores[...], k_ref[...]) * scale
+    dk = dot(scores[...], q_ref[...], TN) * scale
+    dv = dot(probs[...], datt[...], TN)
+    of_o[1]()
+    cosine, sine = cos_ref[...], sin_ref[...]
+    qkz[:, pl.ds(0, width)] = (dq * cosine - swap_halves(dq) * sine).astype(bf16)
+    qkz[:, pl.ds(width, width)] = (dk * cosine - swap_halves(dk) * sine).astype(bf16)
+    gate = gate_grads[...]
+    lanes = lax.broadcasted_iota(jnp.int32, (group, width), 1)
+    for e in range(experts):
+        vgrads[:, pl.ds(e * width, width)] = (gates[:, e : e + 1] * dv).astype(bf16)
+        one = jnp.sum(vx_ref[:, pl.ds(e * width, width)] * dv, axis=-1, keepdims=True)
+        gate = jnp.where(lanes == e, one, gate)
+    squash = squash_ref[...]
+    qkz[:, pl.ds(2 * width, width)] = (gate * gates * (1.0 - squash)).astype(bf16)
+
+    sums[pl.ds(0, features), pl.ds(0, 3 * width)] = dot(normed_t[...], qkz[...]).astype(bf16)
+    sums[pl.ds(0, features), pl.ds(3 * width, experts * width)] = dot(
+        rows_t[...], vgrads[...]
+    ).astype(bf16)
+    of_d[0]()
+
+    def into_rows(block):
+        at = at_block(block, tokens)
+        wide = dot(qkz[at, :], w_an[...], NT)
+        unit = rows_ref[at, :].astype(f32) * inverses[at, 0:1]
+        scaled = wide * attend_gain_ref[...]
+        gain = jnp.sum(wide * unit, axis=0, keepdims=True)
+        total = inverses[at, 0:1] * (
+            scaled - unit * jnp.mean(scaled * unit, axis=-1, keepdims=True)
+        ) + dot(vgrads[at, :], w_v[...], NT)
+        return total, gain
+
+    x_copies = {}
+    gain = jnp.zeros((1, features), f32)
+    for step in steps:
+        total, one = into_rows(xor(h, step))
+        gain += one
+        part[step - 1] = total.astype(bf16)
+        x_copies[step] = remote(
+            part.at[step - 1], got.at[step - 1], z_send.at[2, step - 1], z_recv.at[2, step - 1], along(step)
+        )
+        x_copies[step].start()
+    total, one = into_rows(h)
+    gain += one
+    gain_part[...] = jnp.broadcast_to(gain, gain_part.shape)
+    gain_copies = spread(3, lambda s: gain_part, lambda s: gain_got.at[s - 1])
+    grad_x_ref[...] = dmid_ref[...] + total
+    of_d[1]()
+    of_g[2]()
+
+    own_block = at_block(h, small)
+    blocks[own_block, :] = piece[pl.ds(top + 16, small), :]
+    g_copies = spread(4, lambda s: blocks.at[own_block, :], lambda s: blocks.at[own_block, :])
+    of_o[2]()
+    of_o[3]()
+
+    lasts = {}
+    for half in range(2):
+        toward = 2 - half
+        for index, place in ((1, xor(chip, toward)), (0, chip)):
+            for copy in hops[half, index]:
+                copy.wait()
+            at_in, at_out = halves_in[half], halves_out[half]
+            own_in[place, at_in, :] = own_in[place, at_in, :] + hop_in[half, index]
+            own_out[place, at_out, :] = own_out[place, at_out, :] + hop_out[half, index]
+            if index:
+                lasts[half] = (
+                    remote(
+                        own_in.at[place, at_in, :],
+                        last_in.at[half],
+                        e_send.at[0, 4 + half],
+                        e_recv.at[0, 4 + half],
+                        across(toward),
+                    ),
+                    remote(
+                        own_out.at[place, at_out, :],
+                        last_out.at[half],
+                        e_send.at[1, 4 + half],
+                        e_recv.at[1, 4 + half],
+                        across(toward),
+                    ),
+                )
+                for copy in lasts[half]:
+                    copy.start()
+
+    for step in steps:
+        gain_copies[step].wait()
+    gain = gain_part[...]
+    for step in steps:
+        gain += gain_got[step - 1]
+    sums[pl.ds(top, 16), :] = jnp.concatenate([gain, gain], axis=0).astype(bf16)
+    of_a[0]()
+
+    for step in steps:
+        g_copies[step].wait()
+    of_g[3](blocks, wide_ref, pl.ds(top + 16, n_head * small))
+    of_a[1]()
+
+    for step in steps:
+        out_copies[step].wait()
+    output = mid_ref[...] + po_ref[at_block(h, tokens), :].astype(f32)
+    for step in steps:
+        output += got_out[step - 1].astype(f32)
+    output_ref[...] = output
+    of_d[2]()
+    of_d[3]()
+    of_a[2]()
+    of_a[3]()
+    of_o[4]()
+    of_g[4]()
+    for step in steps:
+        x_copies[step].wait()
+        grad_x_ref[...] += got[step - 1].astype(f32)
+    for half in range(2):
+        for copy in lasts[half]:
+            copy.wait()
+        at_in, at_out = halves_in[half], halves_out[half]
+        fin_in_ref[at_in, :] = own_in[chip, at_in, :] + last_in[half]
+        fin_out_ref[at_out, :] = own_out[chip, at_out, :] + last_out[half]
+    of_d[4]()
+    of_a[4]()
+    for one in (of_o, of_g, of_d, of_a):
+        one[5]()
+
+
+def grads_call(n_dp, n_head, tokens, features, width, experts, per_device, args):
+    group = tokens * n_head
+    chips = n_dp // 2
+    slab = per_device * width
+    named = -(-n_dp * per_device // 8) * 8
+    small = -(-(named + 1) // 16) * 16
+    top = features + experts * width
+    held = top + 16 + small
+    peers = n_head - 1
+    shape = jax.ShapeDtypeStruct
+    outs = [
+        (shape((tokens, features), f32), VM),
+        (shape((tokens, features), f32), VM),
+        (shape((top + 16 + n_head * small, features), bf16), ANY),
+        (shape((features, slab), bf16), VM),
+        (shape((slab, features), bf16), VM),
+    ]
+    return pl.pallas_call(
+        functools.partial(grads_kernel, n_dp, n_head),
+        out_shape=[o[0] for o in outs],
+        out_specs=[o[1] for o in outs],
+        in_specs=[VM] * 18 + [ANY] * 7,
+        scratch_shapes=[
+            pltpu.VMEM((features, 3 * width), bf16),
+            pltpu.VMEM((features, experts * width), bf16),
+            pltpu.VMEM((experts * width, features), bf16),
+            pltpu.VMEM((group, features), bf16),
+            pltpu.VMEM((group, features), bf16),
+            pltpu.VMEM((features, group), bf16),
+            pltpu.VMEM((features, group), bf16),
+            pltpu.VMEM((group, width), f32),
+            pltpu.VMEM((group, width), bf16),
+            pltpu.VMEM((group, width), f32),
+            pltpu.VMEM((group, group), bf16),
+            pltpu.VMEM((group, group), bf16),
+            pltpu.VMEM((group, 3 * width), bf16),
+            pltpu.VMEM((group, experts * width), bf16),
+            pltpu.VMEM((peers, tokens, features), bf16),
+            pltpu.VMEM((peers, tokens, features), bf16),
+            pltpu.VMEM((peers, tokens, features), bf16),
+            pltpu.VMEM((8, features), f32),
+            pltpu.VMEM((peers, 8, features), f32),
+            pltpu.VMEM((held, features), bf16),
+            pltpu.VMEM((held, features // 2), bf16),
+            pltpu.VMEM((chips - 1, held, features // n_dp), bf16),
+            pltpu.VMEM((held, features // n_dp), bf16),
+            pltpu.VMEM((n_head * small, features // n_dp), bf16),
+            pltpu.VMEM((chips, features, slab), bf16),
+            pltpu.VMEM((chips, slab, features), bf16),
+            pltpu.VMEM((chips, features, slab), bf16),
+            pltpu.VMEM((chips, slab, features), bf16),
+            pltpu.VMEM((2, 2, features // 2, slab), bf16),
+            pltpu.VMEM((2, 2, slab // 2, features), bf16),
+            pltpu.VMEM((2, features // 2, slab), bf16),
+            pltpu.VMEM((2, slab // 2, features), bf16),
+            pltpu.SemaphoreType.DMA((5 + 2 * chips,)),
+            pltpu.SemaphoreType.DMA((5, peers)),
+            pltpu.SemaphoreType.DMA((5, peers)),
+            pltpu.SemaphoreType.DMA((2, chips)),
+            pltpu.SemaphoreType.DMA((2, chips)),
+            pltpu.SemaphoreType.DMA((2, 6)),
+            pltpu.SemaphoreType.DMA((2, 6)),
+            pltpu.SemaphoreType.DMA((4, 3 * chips)),
+            pltpu.SemaphoreType.DMA((4, 3 * chips)),
+        ],
+        compiler_params=pltpu.CompilerParams(
+            collective_id=3, has_side_effects=True, vmem_limit_bytes=58 << 20
         ),
     )(*args)
 
@@ -610,94 +1390,74 @@
             ),
         )
     )
-    n_all = n_dp * per_device
-    in_mat = all_in.transpose(1, 0, 2).reshape(features, -1)
-    out_mat = all_out.reshape(-1, features)
-    r_ids = jnp.maximum(jnp.asarray(ids)[h], 0)
-    my_router = jnp.take(router, r_ids, axis=1)
-    mr_all = lax.all_gather(mr, "head", axis=0, tiled=True)
-    gates = jax.nn.sigmoid(product(mr_all, my_router, 1, 0))
-    live = gates * all_mask.astype(f32)
-    act, slope = gelu_pair(product(mr_all, in_mat, 1, 0).reshape(-1, n_all, width))
-    lifted = product(all_cot, out_mat, 1, 1).reshape(-1, n_all, width)
-    dz = (jnp.sum(act * lifted, axis=-1) * (live * (1.0 - gates))[:, :n_all]).astype(bf16)
-    act_live = (act * live[:, :n_all, None]).astype(bf16).reshape(group, -1)
-    hg = (slope * lifted * live[:, :n_all, None]).astype(bf16).reshape(group, -1)
-    part_out = product(act_live, out_mat, 1, 0).astype(bf16)
-    part_grad = (product(hg, in_mat, 1, 1) + product(dz, my_router[:, :n_all], 1, 1)).astype(bf16)
-    normed_grad = lax.psum_scatter(part_grad, "head", scatter_dimension=0, tiled=True)
-    summed = lax.psum_scatter(part_out, "head", scatter_dimension=0, tiled=True)
-    gi = product(mr_all, hg, 0, 0).reshape(features, n_dp, per_device, width).transpose(1, 2, 0, 3)
-    go = product(act_live, all_cot, 0, 0).reshape(n_dp, per_device, width, features)
-    grad_in = lax.psum_scatter(gi.astype(bf16), "dp", scatter_dimension=0, tiled=False).astype(f32)
-    grad_out = lax.psum_scatter(go.astype(bf16), "dp", scatter_dimension=0, tiled=False).astype(f32)
-    gr = lax.psum(product(dz, mr_all, 0, 0), "dp").reshape(n_dp, per_device, features)
-    gr = lax.all_gather(gr, "head", axis=1, tiled=False)
-    grad_router = gr.reshape(experts_total, features).T
-    output = middle + summed.astype(f32)
-    incoming = cotangent.astype(f32)
-    row_grad, grad_gain_expert = norm_back(
-        middle, rms_scale(middle), expert_scale[0], normed_grad.astype(f32)
-    )
-    middle_grad = incoming + row_grad
-    group_grads = lax.all_gather(middle_grad.astype(bf16), "head", axis=0, tiled=True)
-    query_mat, key_mat, value_mat = query_weight[0], key_weight[0], value_weight[0]
-    output_mat, gate10 = output_weight[0], head_router[0]
-    grouped = rows.astype(f32)
-    inverse = rms_scale(grouped)
-    normed = (grouped * inverse * attend_scale).astype(bf16)
-    scale = width ** (-0.5)
-    og = (squash * gate_mask)[:, experts : 2 * experts]
-    vg = (squash * gate_mask)[:, :experts]
-    weighted = (og[:, :, None] * att[:, None, :]).reshape(group, -1).astype(bf16)
-    weighted_grad = product(group_grads, output_mat, 1, 1).reshape(group, experts, width)
-    output_grad = product(weighted, group_grads, 0, 0)
-    ogg = jnp.sum(weighted_grad * att[:, None, :], axis=-1)
-    attended_grad = jnp.sum(weighted_grad * og[:, :, None], axis=1).astype(bf16)
-    prob_grad = product(attended_grad, v, 1, 1)
-    centre = jnp.sum(prob * prob_grad, axis=-1, keepdims=True)
-    score_grad = (prob * (prob_grad - centre)).astype(bf16)
-    query_grad = product(score_grad, k, 1, 0) * scale
-    key_grad = product(score_grad, q, 0, 0) * scale
-    values_grad = product(prob.astype(bf16), attended_grad, 0, 0)
-    expert_grad = (vg[:, :, None] * values_grad[:, None, :]).reshape(group, -1).astype(bf16)
-    vgg = jnp.sum(vx.reshape(group, experts, width) * values_grad[:, None, :], axis=-1)
-    c64, s64 = cosine[:, : width // 2], -sine[:, : width // 2]
-    query_grad = rotate(query_grad, c64, -s64).astype(bf16)
-    key_grad = rotate(key_grad, c64, -s64).astype(bf16)
-    sq = squash[:, : 2 * experts]
-    logit_grad = (
-        jnp.concatenate([vgg, ogg], axis=1) * gate_mask[:, : 2 * experts] * sq * (1.0 - sq)
-    ).astype(bf16)
-    head_grads = (
-        product(normed, query_grad, 0, 0),
-        product(normed, key_grad, 0, 0),
-        product(rows, expert_grad, 0, 0),
-        output_grad,
-        product(normed, logit_grad, 0, 0),
-    )
-    head_grads = tuple(grad.astype(bf16) for grad in head_grads)
-    head_grads = tuple(grad.astype(f32)[None] for grad in lax.psum(head_grads, "dp"))
-    back = (
-        product(query_grad, query_mat, 1, 1)
-        + product(key_grad, key_mat, 1, 1)
-        + product(logit_grad, gate10, 1, 1)
-    )
-    row_back, grad_attend = norm_back(grouped, inverse, attend_scale[0], back)
-    partial = (row_back + product(expert_grad, value_mat, 1, 1)).astype(bf16)
-    input_grad = middle_grad + lax.psum_scatter(
-        partial, "head", scatter_dimension=0, tiled=True
-    ).astype(f32)
-    grad_attend, grad_gain_expert = lax.psum((grad_attend, grad_gain_expert), everywhere)
+    my_router = jnp.take(router, jnp.maximum(jnp.asarray(ids)[h], 0), axis=1)
+    my_router = jnp.where(ids[0] >= 0, my_router, jnp.zeros((), bf16))
+    da, middle_grad, part_out, gr, eg, gi, go = expert_call(
+        n_dp,
+        n_head,
+        tokens,
+        features,
+        width,
+        per_device,
+        (mr, middle, cotangent, all_mask, my_router, expert_scale, all_cot, all_in, all_out),
+    )
+    output, input_grad, wide, fin_in, fin_out = grads_call(
+        n_dp,
+        n_head,
+        tokens,
+        features,
+        width,
+        experts,
+        per_device,
+        (
+            da,
+            middle_grad,
+            middle,
+            part_out,
+            gr,
+            eg,
+            rows,
+            q,
+            k,
+            v,
+            prob,
+            vx,
+            squash,
+            att,
+            gate_mask,
+            cosine,
+            sine,
+            attend_scale,
+            query_weight[0],
+            key_weight[0],
+            gate_mat,
+            value_weight[0],
+            output_weight[0],
+            gi,
+            go,
+        ),
+    )
+    top = features + experts * width
+    small = (wide.shape[0] - top - 16) // n_head
+    named = n_dp * per_device
+    planes = wide[top + 16 :].astype(f32).reshape(n_head, small, features)
+    grad_router = planes[:, :named].reshape(n_head, n_dp, per_device, features)
+    grad_router = grad_router.transpose(1, 0, 2, 3).reshape(experts_total, features).T
+    grad_gain = jnp.sum(planes[:, -(-named // 8) * 8], axis=0)
+    first = wide[:features]
     return (
         output,
         input_grad,
-        grad_attend,
-        *head_grads,
-        grad_gain_expert,
+        wide[top].astype(f32),
+        first[None, :, :width].astype(f32),
+        first[None, :, width : 2 * width].astype(f32),
+        first[None, :, 3 * width :].astype(f32),
+        wide[None, features:top].astype(f32),
+        first[None, :, 2 * width : 2 * width + 2 * experts].astype(f32),
+        grad_gain,
         grad_router,
-        grad_in,
-        grad_out,
+        fin_in.astype(f32).reshape(features, per_device, width).transpose(1, 0, 2),
+        fin_out.astype(f32).reshape(per_device, width, features),
     )
 
 

time: 564 us -> 303 us (0.54)
  waiting for transfers between devices: 244 us -> 0 us
  Pallas kernels: 82 us -> 248 us
  blocking collectives: 76.9 us -> 0 us
  matrix products: 69.6 us -> 0 us
  local copies, waits for them, and re-layouts: 47 us -> 29.5 us
  between operations: 14.3 us -> 0.92 us
    reduce_scatter x5 -> x0, waiting for transfers between devices: 196 us -> none  [the longest x1 62.8 us: kernel_body(): lax.psum_scatter(go.astype(bf16), 'dp', scatter_dimension=0, tiled=False)]
    pallas_call x0 -> x2, Pallas kernels: none -> 166 us  [the longest x1 110 us: grads_call(): pl.pallas_call(functools.partial(grads_kernel, n_dp, n_head), out_shape=[...]
    dot_general x23 -> x0, matrix products: 69.6 us -> none  [product(): lax.dot_general(left, right, (((left_axis,), (right_axis,)), ((), ())), p...]
    psum x2 -> x0, blocking collectives: 62.5 us -> none  [the longest x1 39.6 us: kernel_body(): lax.psum((grad_attend, grad_gain_expert), everywhere)]
    all_gather x2 -> x0, waiting for transfers between devices: 34.1 us -> none  [the longest x1 18.7 us: kernel_body(): mr_all = lax.all_gather(mr, 'head', axis=0, tiled=True)]
    all_gather x1 -> x0, blocking collectives: 14.4 us -> none  [kernel_body(): gr = lax.all_gather(gr, 'head', axis=1, tiled=False)]
    psum x2 -> x0, waiting for transfers between devices: 13.6 us -> none  [the longest x1 13.6 us: kernel_body(): lax.psum(product(dz, mr_all, 0, 0), 'dp')]
    transpose x1 -> x2, local copies, waits for them, and re-layouts: 8.54 us -> 0.56 us  [the longest x1 0.29 us: kernel_body(): fin_in.astype(f32).reshape(features, per_device, width).transpose(1, 0, 2)]
  transfers between devices with their start and end apart: 9 -> 0, of which waited for: 8 -> 0; matrix products, arithmetic and copies ran while one was open for 14% -> 0% of each run, Pallas kernels for 0% -> 0%
where the time goes in v3:
time: 303 us; the launch traced here: 302 us
  Pallas kernels  248 us (82%)
  local copies, waits for them, and re-layouts  29.5 us (10%)
  other arithmetic  23.2 us (8%)
    pallas_call x1, Pallas kernels, grads_call(): pl.pallas_call(functools.partial(grads_kernel, n_dp, n_head), out_shape=[...  110 us
    pallas_call x1, Pallas kernels, attend_call(): pl.pallas_call(functools.partial(attend_kernel, n_dp, n_head), out_shape=...  82 us
    pallas_call x1, Pallas kernels, expert_call(): pl.pallas_call(functools.partial(expert_kernel, n_dp, n_head), out_shape=...  55.9 us
    unnamed x77, local copies, waits for them, and re-layouts  24.4 us

profile of v3, /device:TPU:0, one launch (start us, length us, event | category | flops | bytes accessed | tf_op | source)
XLA Modules:
  0.0 301.9 jit_solution(8350254912758620602)
XLA Ops:
  5.2 3.2 %compare_reduce_fusion = pred[4,128,128]{2,1,0:T(8,128)(4,1)S(1)} fusion(s32[4,128]{1,0:T(4,128)} %constant.49.clone, s32[128,16]{1,0:T(8,128)S(1)} %copy.53), kind=kLoop, calls=%fused_computation.1 | loop fusion | flops 2031616 | bytes 75776 | tf_op jit(solution)/shard_map/reduce_or | solution.py:1351
  8.4 1.1 fusion
  11.3 1.7 select_bitcast_fusion.router_ref
  13.8 1.0 pad.4.wg_ref
  15.7 0.9 copy-done.7
  16.7 0.9 copy-done.8
  18.6 0.9 copy-done.10
  21.4 1.1 copy-done.16
  22.6 1.1 copy-done.17
  24.6 82.0 %shard_map.301 = (bf16[4,1024,768]{2,1,0:T(8,128)(2,1)}, bf16[4,768,1024]{2,1,0:T(8,128)(2,1)}, bf16[512,1024]{1,0:T(8,128)(2,1)S(1)}, bf16[512,128]{1,0:T(8,128...) custom-call(bf16[128,1024]{1,0:T(8,128)(2,1)S(1)} %copy-done.21, ...), custom_call_target="tpu_custom_call" | custom-call | tf_op jit(solution)/shard_map/pallas_call | solution.py:515
  107.5 1.1 copy-done.6
  108.6 1.0 copy-done.12
  109.5 1.0 copy-done.14
  110.5 1.0 copy-done.15
  116.2 55.9 %shard_map.302 = (bf16[128,1024]{1,0:T(8,128)(2,1)}, f32[128,1024]{1,0:T(8,128)}, bf16[512,1024]{1,0:T(8,128)(2,1)}, f32[24,1024]{1,0:T(8,128)}, f32[1,1024]{1,0...) custom-call(bf16[128,1024]{1,0:T(8,128)(2,1)} %copy-done.20, f32[128,1024]{1,0:T(8,128)} %copy-done.5, ...), custom_call_target="tpu_custom_call" | custom-call | tf_op jit(solution)/shard_map/pallas_call | solution.py:756
  172.1 110.4 %shard_map.303 = (f32[128,1024]{1,0:T(8,128)}, f32[128,1024]{1,0:T(8,128)}, bf16[1808,1024]{1,0:T(8,128)(2,1)}, bf16[1024,384]{1,0:T(8,128)(2,1)}, bf16[384,1024]{1,0:T(8,128)(2,1)}) custom-call(bf16[128,1024]{1,0:T(8,128)(2,1)} %get-tuple-element.44.da_ref, f32[128,1024]{1,0:T(8,128)} %get-tuple-element.45.dmid_ref, f32[128,1024]{1,0:T(8,128)} %copy-done.5, ...), custom_call_target="tpu_custom_call" | custom-call | tf_op jit(solution)/shard_map/pallas_call | solution.py:1264
  282.5 1.4 slice_convert_fusion
  283.9 1.0 bitcast_convert_fusion.5
  287.0 1.0 bitcast_convert_fusion.2
  288.8 2.1 bitcast_convert_fusion.3
  291.2 1.6 copy.61
  292.8 1.3 convert.18
  294.1 3.2 %bitcast_convert_fusion = f32[1,640,1024]{2,1,0:T(8,128)} fusion(bf16[1808,1024]{1,0:T(8,128)(2,1)} %get-tuple-element.61), kind=kLoop, calls=%fused_computation.2 | loop fusion | flops 655360 | bytes 3932160 | tf_op jit(solution)/shard_map/convert_element_type | solution.py:1455
  297.3 3.0 bitcast_convert_fusion.1
  (83 shorter events, 22.1 us)
Async XLA Ops:
  0.6 8.9 %copy-start = (bf16[1024,96]{0,1:T(8,128)(2,1)S(1)}, bf16[1024,96]{0,1:T(8,128)(2,1)}, u32[]{:S(2)}) copy-start(bf16[1024,96]{0,1:T(8,128)(2,1)} %param.34) | copy-start | bytes 589828
  0.7 10.6 %copy-start.34 = (pred[128]{0:T(512)(128)(4,1)S(1)}, pred[128]{0:T(512)(128)(4,1)}, u32[]{:S(2)}) copy-start(pred[128]{0:T(512)(128)(4,1)} %constant.50.clone) | copy-start | bytes 388
  0.7 14.2 %copy-start.28 = (s32[512]{0:T(512)S(1)}, s32[512]{0:T(512)}, u32[]{:S(2)}) copy-start(s32[512]{0:T(512)} %param.23) | copy-start | bytes 6148
  0.7 12.3 %copy-start.33 = (bf16[1,1024,10]{1,2,0:T(8,128)(2,1)S(1)}, bf16[1,1024,10]{1,2,0:T(8,128)(2,1)}, u32[]{:S(2)}) copy-start(bf16[1,1024,10]{1,2,0:T(8,128)(2,1)} %param.32) | copy-start | bytes 61444
  0.7 15.0 %copy-start.2 = (bf16[1,640,1024]{2,1,0:T(8,128)(2,1)S(1)}, bf16[1,640,1024]{2,1,0:T(8,128)(2,1)}, u32[]{:S(2)}) copy-start(bf16[1,640,1024]{2,1,0:T(8,128)(2,1)} %param.31) | copy-start | bytes 3932164
  0.7 15.0 %copy-start.1 = (bf16[1,1024,640]{2,1,0:T(8,128)(2,1)S(1)}, bf16[1,1024,640]{2,1,0:T(8,128)(2,1)}, u32[]{:S(2)}) copy-start(bf16[1,1024,640]{2,1,0:T(8,128)(2,1)} %param.30) | copy-start | bytes 3932164
  3.7 103.0 %copy-start.26 = (f32[1024]{0:T(1024)}, f32[1024]{0:T(1024)S(1)}, u32[]{:S(2)}) copy-start(f32[1024]{0:T(1024)S(1)} %broadcast_in_dim.52) | copy-start | bytes 12292
  4.4 102.3 %copy-start.27 = (f32[1024]{0:T(1024)}, f32[1024]{0:T(1024)S(1)}, u32[]{:S(2)}) copy-start(f32[1024]{0:T(1024)S(1)} %broadcast_in_dim.53) | copy-start | bytes 12292
  9.6 97.1 %copy-start.4 = (f32[512,128]{1,0:T(8,128)}, f32[512,128]{1,0:T(8,128)S(1)}, u32[]{:S(2)}) copy-start(f32[512,128]{1,0:T(8,128)S(1)} %or_convert_fusion.gate_mask_ref) | copy-start | bytes 786436
  14.8 157.2 %copy-start.3 = (bf16[1024,128]{1,0:T(8,128)(2,1)}, bf16[1024,128]{1,0:T(8,128)(2,1)S(1)}, u32[]{:S(2)}) copy-start(bf16[1024,128]{1,0:T(8,128)(2,1)S(1)} %pad.4.wg_ref) | copy-start | bytes 786436
  15.7 1.0 copy-start.7
  16.7 0.9 copy-start.8
  17.6 0.9 copy-start.9
  18.6 0.9 copy-start.10
  21.4 1.1 copy-start.16
  22.6 1.1 copy-start.17
  107.5 1.1 copy-start.6
  108.6 1.0 copy-start.12
  109.5 1.0 copy-start.14
  110.5 1.0 copy-start.15
  282.5 8.4 %copy-start.30 = (bf16[1024,384]{1,0:T(8,128)(2,1)S(1)}, bf16[1024,384]{1,0:T(8,128)(2,1)}, u32[]{:S(2)}) copy-start(bf16[1024,384]{1,0:T(8,128)(2,1)} %get-tuple-element.62) | copy-start | bytes 2359300
  288.0 4.8 %copy-start.29 = (bf16[384,1024]{1,0:T(8,128)(2,1)S(1)}, bf16[384,1024]{1,0:T(8,128)(2,1)}, u32[]{:S(2)}) copy-start(bf16[384,1024]{1,0:T(8,128)(2,1)} %get-tuple-element.63) | copy-start | bytes 2359300
  294.1 6.2 %copy-start.32 = (f32[128,1024]{1,0:T(8,128)S(1)}, f32[128,1024]{1,0:T(8,128)}, u32[]{:S(2)}) copy-start(f32[128,1024]{1,0:T(8,128)} %get-tuple-element.116) | copy-start | bytes 1572868
  294.1 7.0 %copy-start.31 = (f32[128,1024]{1,0:T(8,128)S(1)}, f32[128,1024]{1,0:T(8,128)}, u32[]{:S(2)}) copy-start(f32[128,1024]{1,0:T(8,128)} %get-tuple-element.117) | copy-start | bytes 1572868
  (11 other events, 8.4 us)

commit v4 on v1

--- a/solution.py
+++ b/solution.py
@@ -1,6 +1,11 @@
+import functools
+
 import jax
 import jax.numpy as jnp
+import numpy as np
 from jax import lax
+from jax.experimental import pallas as pl
+from jax.experimental.pallas import tpu as pltpu
 from jax.sharding import PartitionSpec as P
 
 epsilon = 1e-06
@@ -10,6 +15,8 @@
 bf16 = jnp.bfloat16
 everywhere = ("dp", "head")
 whole_rows = 4096
+vmem_for_weights = 16 << 20
+vmem_bytes = 62 << 20
 
 
 def product(left, right, left_axis, right_axis):
@@ -223,6 +230,1090 @@
     )
 
 
+MESH = pl.DeviceIdType.MESH
+VM = pl.BlockSpec(memory_space=pltpu.VMEM)
+ANY = pl.BlockSpec(memory_space=pl.ANY)
+NN = (((1,), (0,)), ((), ()))
+NT = (((1,), (1,)), ((), ()))
+TN = (((0,), (0,)), ((), ()))
+
+
+def dot(left, right, dims=NN):
+    return lax.dot_general(left, right, dims, preferred_element_type=f32)
+
+
+def at_block(block, count):
+    return pl.ds(pl.multiple_of(block * count, count), count)
+
+
+def remote(src, dst, send, recv, where):
+    return pltpu.make_async_remote_copy(
+        src_ref=src, dst_ref=dst, send_sem=send, recv_sem=recv, device_id=where, device_id_type=MESH
+    )
+
+
+def swap_halves(value):
+    half = value.shape[-1] // 2
+    return jnp.concatenate([value[:, half:], value[:, :half]], axis=-1)
+
+
+def ceil_to(number, step):
+    return -(-number // step) * step
+
+
+def layer_kernel(
+    n_dp,
+    n_head,
+    x_ref,
+    cot_ref,
+    pick_ref,
+    head_pick_ref,
+    seg_ref,
+    gain_ref,
+    cos_ref,
+    sin_ref,
+    wq_ref,
+    wk_ref,
+    wg_ref,
+    wv_ref,
+    wo_ref,
+    router_ref,
+    in_ref,
+    out_ref,
+    output_ref,
+    grad_x_ref,
+    wide_ref,
+    fin_in_ref,
+    fin_out_ref,
+    picks,
+    head_picks,
+    seg,
+    gains,
+    cosine,
+    sine,
+    w_an,
+    w_v,
+    w_o,
+    my_router,
+    w_in,
+    w_out,
+    rows,
+    cot,
+    mrs,
+    das,
+    turned,
+    rows_t,
+    inverses,
+    my_mask,
+    all_mask,
+    gate_mask,
+    q,
+    k,
+    v,
+    vx,
+    squash,
+    att,
+    middle,
+    part,
+    got,
+    outs,
+    got_out,
+    lifted,
+    core_out,
+    acts,
+    hids,
+    dzs,
+    datt,
+    gate_grads,
+    probs,
+    scores,
+    qkz,
+    vgrads,
+    gain_part,
+    gain_got,
+    sums,
+    core_got,
+    chip_got,
+    piece,
+    blocks,
+    hop_in,
+    hop_out,
+    local_sem,
+    z_send,
+    z_recv,
+    w_send,
+    w_recv,
+    c_send,
+    c_recv,
+    e_send,
+    e_recv,
+    s_send,
+    s_recv,
+    ready,
+    free,
+):
+    xor = jnp.bitwise_xor
+    d, h = lax.axis_index("dp"), lax.axis_index("head")
+    chip, core = d // 2, d % 2
+    chips = n_dp // 2
+    tokens, features = x_ref.shape
+    per_device, _, width = in_ref.shape
+    slab = per_device * width
+    wide = 2 * slab
+    experts = wv_ref.shape[1] // width
+    named = ceil_to(n_dp * per_device, 8)
+    group = tokens * n_head
+    pair = 2 * tokens
+    column = 256
+    lanes = 128
+    scale = width ** (-0.5)
+    peers = (2, 3, 1)
+    partner = (chip * 2 + 1 - core, h)
+    own_block = at_block(h, tokens)
+    own_side, other_side = at_block(core, slab), at_block(1 - core, slab)
+    halves_in = (pl.ds(0, features // 2), pl.ds(features // 2, features // 2))
+    halves_out = lambda side: (
+        at_block(2 * side, slab // 2),
+        at_block(2 * side + 1, slab // 2),
+    )
+
+    def along(step):
+        return (d, xor(h, step))
+
+    def across(step):
+        return (xor(chip, step) * 2 + core, h)
+
+    loads = []
+
+    def load(src, dst):
+        copy = pltpu.make_async_copy(src, dst, local_sem.at[len(loads)])
+        copy.start()
+        loads.append(copy)
+        return copy
+
+    own_weights = [load(out_ref, w_out.at[chip, own_side, :])] + [
+        load(in_ref.at[e], w_in.at[chip, :, at_block(core * per_device + e, width)])
+        for e in range(per_device)
+    ]
+    for_rows = [
+        load(x_ref, rows.at[own_block, :]),
+        load(gain_ref, gains),
+        load(wg_ref, w_an.at[:, pl.ds(2 * width, width)]),
+        load(wq_ref, w_an.at[:, pl.ds(0, width)]),
+        load(wk_ref, w_an.at[:, pl.ds(width, width)]),
+        load(wv_ref, w_v),
+        load(head_pick_ref, head_picks),
+        load(cos_ref, cosine),
+        load(sin_ref, sine),
+    ]
+    for_scores = [load(seg_ref, seg), load(wo_ref, w_o)]
+    for_mask = load(pick_ref, picks)
+    for_cot = load(cot_ref, cot.at[own_block, :])
+    for_router = load(router_ref, turned.at[:, pl.ds(0, lanes)])
+
+    barrier = pltpu.get_barrier_semaphore()
+    friends = [along(s) for s in peers] + [partner] + [across(s) for s in range(1, chips)]
+    for friend in friends:
+        pl.semaphore_signal(barrier, inc=1, device_id=friend, device_id_type=MESH)
+    pl.semaphore_wait(barrier, len(friends))
+
+    def spread(kind, src, dst, steps=peers):
+        copies = {}
+        for step in steps:
+            copies[step] = remote(
+                src(step), dst(step), z_send.at[kind, step - 1], z_recv.at[kind, step - 1], along(step)
+            )
+            copies[step].start()
+        return copies
+
+    x_copies = spread(0, lambda s: x_ref, lambda s: rows.at[own_block, :])
+
+    def slot(array, place, side, half=None):
+        if array == 0:
+            at = halves_out(side)[half] if half is not None else at_block(side, slab)
+            return w_out.at[place, at, :]
+        at = halves_in[half] if half is not None else pl.ds(0, features)
+        return w_in.at[place, at, at_block(side, slab)]
+
+    def weights(number, ref, where):
+        copy = remote(ref, ref, w_send.at[number], w_recv.at[number], where)
+        copy.start()
+        return copy
+
+    slabs, halves_on, to_core, diagonal = {}, {}, {}, {}
+    for copy in own_weights:
+        copy.wait()
+    for array in range(2):
+        for first in range(2):
+            for bit in (1, 2):
+                half = bit - 1 if first == 0 else 2 - bit
+                number = ((bit - 1) * 2 + half) * 2 + array
+                slabs[bit, half, array] = weights(
+                    number, slot(array, chip, core, half), across(bit)
+                )
+        to_core[0, array] = weights(12 + array, slot(array, chip, core), partner)
+
+    for_mask.wait()
+    lane = lax.broadcasted_iota(jnp.int32, (tokens, lanes), 1)
+    for plane in range(n_head):
+        expert = (lane // per_device * n_head + plane) * per_device + lane % per_device
+        expert = jnp.where(lane < n_dp * per_device, expert, -1)
+        hit = picks[:, 0:1] == expert
+        for c in range(1, picks.shape[1]):
+            hit = hit | (picks[:, c : c + 1] == expert)
+        my_mask[plane] = jnp.where(hit, 1.0, 0.0).astype(bf16)
+    mask_copies = spread(1, lambda s: my_mask.at[xor(h, s)], lambda s: all_mask.at[own_block, :])
+    all_mask[own_block, :] = my_mask[h]
+
+    for copy in for_rows:
+        copy.wait()
+    attend_gain = gains[0:1, :]
+    expert_gain = gains[1:2, :]
+    lane = lax.broadcasted_iota(jnp.int32, (group, width), 1)
+    hit = lane == head_picks[:, 0:1]
+    for c in range(1, head_picks.shape[1]):
+        hit = hit | (lane == head_picks[:, c : c + 1])
+    gate_mask[...] = jnp.where(hit, 1.0, 0.0)
+
+    def project(block):
+        at = at_block(block, tokens)
+        own = rows[at, :]
+        full = own.astype(f32)
+        inverse = lax.rsqrt(jnp.mean(full * full, axis=-1, keepdims=True) + epsilon)
+        inverses[at, :] = jnp.broadcast_to(inverse, (tokens, width))
+        unit = (full * inverse * attend_gain).astype(bf16)
+        qkg = dot(unit, w_an[...])
+        c, s = cosine[at, :], sine[at, :]
+        one, two = qkg[:, :width], qkg[:, width : 2 * width]
+        q[at, :] = (one * c + swap_halves(one) * s).astype(bf16)
+        k[at, :] = (two * c + swap_halves(two) * s).astype(bf16)
+        squashed = jax.nn.sigmoid(qkg[:, 2 * width :])
+        squash[at, :] = squashed
+        gates = squashed * gate_mask[at, :]
+        values = dot(own, w_v[...])
+        vx[at, :] = values.astype(bf16)
+        value = gates[:, 0:1] * values[:, :width]
+        for e in range(1, experts):
+            value += gates[:, e : e + 1] * values[:, e * width : (e + 1) * width]
+        v[at, :] = value.astype(bf16)
+
+    project(h)
+    for step in (1, 2, 3):
+        x_copies[step].wait_recv()
+        project(xor(h, step))
+    cot_copies = spread(2, lambda s: cot_ref, lambda s: cot.at[own_block, :])
+    for half in range(2):
+        for array in range(2):
+            slabs[1 + half, half, array].wait_recv()
+            halves_on[half, array] = weights(
+                8 + 2 * half + array,
+                slot(array, xor(chip, 1 + half), core, half),
+                across(2 - half),
+            )
+
+    for copy in for_scores:
+        copy.wait()
+    seg_col = gate_grads
+    seg_col[...] = jnp.broadcast_to(seg[...].astype(f32), (lanes, group)).T
+
+    def attend(block):
+        at = at_block(block, tokens)
+        score = dot(q[at, :], k[...], NT) * scale
+        row = block * tokens + lax.broadcasted_iota(jnp.int32, (tokens, group), 0)
+        place = lax.broadcasted_iota(jnp.int32, (tokens, group), 1)
+        allowed = (place <= row) & (seg_col[at, 0:1] == seg[...].astype(f32))
+        score = jnp.where(allowed, score, negative)
+        exponents = jnp.exp(score - jnp.max(score, axis=-1, keepdims=True))
+        chance = exponents / jnp.sum(exponents, axis=-1, keepdims=True)
+        probs[at, :] = chance.astype(bf16)
+        attended = dot(chance.astype(bf16), v[...])
+        att[at, :] = attended
+        gates = squash[at, :] * gate_mask[at, :]
+        weighted = jnp.concatenate(
+            [
+                (gates[:, experts + e : experts + e + 1] * attended).astype(bf16)
+                for e in range(experts)
+            ],
+            axis=-1,
+        )
+        return dot(weighted, w_o[...])
+
+    def send_part(kind, step):
+        copy = remote(
+            part.at[at_block(xor(h, step), tokens), :],
+            got.at[step - 1],
+            z_send.at[kind, step - 1],
+            z_recv.at[kind, step - 1],
+            along(step),
+        )
+        copy.start()
+        return copy
+
+    back = {}
+    for step in peers:
+        part[at_block(xor(h, step), tokens), :] = attend(xor(h, step)).astype(bf16)
+        back[step] = send_part(3, step)
+    mid = rows[own_block, :].astype(f32) + attend(h)
+
+    for bit in (1, 2):
+        slabs[bit, 2 - bit, 0].wait_recv()
+        to_core[bit, 0] = weights(14 + (bit - 1) * 2, slot(0, xor(chip, bit), core), partner)
+        slabs[bit, 2 - bit, 1].wait_recv()
+        to_core[bit, 1] = weights(15 + (bit - 1) * 2, slot(1, xor(chip, bit), core), partner)
+    for_router.wait()
+    slot_of = lax.broadcasted_iota(jnp.int32, (lanes, lanes), 1)
+    name = lax.broadcasted_iota(jnp.int32, (lanes, lanes), 0)
+    expert = (slot_of // per_device * n_head + h) * per_device + slot_of % per_device
+    expert = jnp.where(slot_of < n_dp * per_device, expert, -1)
+    my_router[...] = dot(turned[:, pl.ds(0, lanes)], jnp.where(name == expert, 1.0, 0.0).astype(bf16)).astype(bf16)
+
+    for step in peers:
+        back[step].wait()
+        mid += got[step - 1].astype(f32)
+    middle[...] = mid
+    inverse = lax.rsqrt(jnp.mean(mid * mid, axis=-1, keepdims=True) + epsilon)
+    mrs[own_block, :] = (mid * inverse * expert_gain).astype(bf16)
+    mr_copies = spread(4, lambda s: mrs.at[own_block, :], lambda s: mrs.at[own_block, :], (1, 2, 3))
+
+    for array in range(2):
+        for half in range(2):
+            halves_on[half, array].wait_recv()
+            diagonal[half, array] = weights(
+                18 + 2 * half + array, slot(array, xor(chip, 3), core, half), partner
+            )
+    for_cot.wait()
+    for step in peers:
+        cot_copies[step].wait()
+        x_copies[step].wait_send()
+        mask_copies[step].wait()
+
+    def weights_here(array):
+        for bit in range(3):
+            to_core[bit, array].wait()
+        for half in range(2):
+            diagonal[half, array].wait()
+            halves_on[half, array].wait_send()
+            for bit in (1, 2):
+                slabs[bit, half, array].wait_send()
+
+    weights_here(0)
+
+    @pl.loop(0, chips)
+    def _(j):
+        lift = dot(cot[...], w_out[j], NT)
+        lifted[j, 0] = lift[:, :slab].astype(bf16)
+        lifted[j, 1] = lift[:, slab:].astype(bf16)
+
+    weights_here(1)
+
+    def spread_lanes(j):
+        lane = lax.broadcasted_iota(jnp.int32, (lanes, wide), 1) // width
+        slot = lax.broadcasted_iota(jnp.int32, (lanes, wide), 0)
+        return jnp.where(slot == lane + j * (wide // width), 1.0, 0.0).astype(bf16)
+
+    def pair_of_blocks(number):
+        at = at_block(number, pair)
+        own = mrs[at, :]
+        gates = jax.nn.sigmoid(dot(own, my_router[...]))
+        live = gates * all_mask[at, :].astype(f32)
+        high = live.astype(bf16)
+        low = (live - high.astype(f32)).astype(bf16)
+        both = jnp.concatenate([high, low], axis=-1)
+
+        def chip_step(j, total):
+            pick = spread_lanes(j)
+            hidden = dot(own, w_in[j])
+            gate = dot(both, jnp.concatenate([pick, pick], axis=0))
+            lift = jnp.concatenate([lifted[j, 0, at, :], lifted[j, 1, at, :]], axis=-1).astype(f32)
+            square = hidden * hidden
+            inner = jnp.tanh(0.7978845608028654 * hidden * (1.0 + 0.044715 * square))
+            half = 0.5 * (1.0 + inner)
+            act = hidden * half
+            slope = half + act * (1.0 - inner) * (
+                0.7978845608028654 + (0.7978845608028654 * 3.0 * 0.044715) * square
+            )
+            acts[j, at, :] = (act * gate).astype(bf16)
+            hids[j, at, :] = (slope * (lift * gate)).astype(bf16)
+            return total + dot((act * lift).astype(bf16), pick, NT)
+
+        total = lax.fori_loop(0, chips, chip_step, jnp.zeros((pair, lanes), f32))
+        dz = (total * live * (1.0 - gates)).astype(bf16)
+        dzs[at, :] = dz
+
+        @pl.loop(0, features // column)
+        def _(c):
+            part_of = at_block(c, column)
+            total = dot(dz, my_router[part_of, :], NT)
+            for j in range(chips):
+                total += dot(hids[j, at, :], w_in[j, part_of, :], NT)
+            part[at, part_of] = total.astype(bf16)
+
+    near = h // 2
+    mr_copies[1].wait_recv()
+    pair_of_blocks(near)
+    back = {1: send_part(5, 1)}
+    mr_copies[2].wait_recv()
+    mr_copies[3].wait_recv()
+    pair_of_blocks(1 - near)
+    back[2], back[3] = send_part(5, 2), send_part(5, 3)
+    pl.semaphore_signal(ready, inc=1, device_id=partner, device_id_type=MESH)
+
+    @pl.loop(0, features // column)
+    def _(c):
+        part_of = at_block(c, column)
+        total = dot(acts[0], w_out[0, :, part_of])
+        for j in range(1, chips):
+            total += dot(acts[j], w_out[j, :, part_of])
+        outs[:, part_of] = total.astype(bf16)
+
+    turned[...] = mrs[...].T
+
+    def expert_grads(place, at):
+        for half in halves_in:
+            w_in[place, half, at] = dot(turned[half, :], hids[place, :, at]).astype(bf16)
+            w_out[place, at, half] = dot(acts[place, :, at], cot[:, half], TN).astype(bf16)
+
+    def to_other_core(n):
+        place = xor(chip, chips - 1 - n)
+        copies = [
+            remote(
+                w_in.at[place, halves_in[half], other_side],
+                lifted.at[place, half],
+                c_send.at[half, n],
+                c_recv.at[half, n],
+                partner,
+            )
+            for half in range(2)
+        ]
+        copies.append(
+            remote(
+                w_out.at[place, other_side, :],
+                core_out.at[place],
+                c_send.at[2, n],
+                c_recv.at[2, n],
+                partner,
+            )
+        )
+        return copies
+
+    pl.semaphore_wait(ready, 1)
+
+    @pl.loop(0, chips)
+    def _(n):
+        expert_grads(xor(chip, chips - 1 - n), other_side)
+        for copy in to_other_core(n):
+            copy.start()
+
+    @pl.loop(0, chips)
+    def _(n):
+        expert_grads(xor(chip, chips - 1 - n), own_side)
+
+    hops = {}
+
+    def hop(half, index, place, toward):
+        copies = (
+            remote(
+                slot(1, place, core, half),
+                hop_in.at[half, index],
+                e_send.at[0, 2 * half + index],
+                e_recv.at[0, 2 * half + index],
+                across(toward),
+            ),
+            remote(
+                slot(0, place, core, half),
+                hop_out.at[half, index],
+                e_send.at[1, 2 * half + index],
+                e_recv.at[1, 2 * half + index],
+                across(toward),
+            ),
+        )
+        for copy in copies:
+            copy.start()
+        hops[half, index] = copies
+
+    for n in range(chips):
+        s = chips - 1 - n
+        place = xor(chip, s)
+        for copy in to_other_core(n):
+            copy.wait()
+        for half in range(2):
+            here = (place, halves_in[half], own_side)
+            w_in[here] = w_in[here] + lifted[place, half]
+        w_out[place, own_side, :] = w_out[place, own_side, :] + core_out[place]
+        if s == 3:
+            hop(0, 1, place, 1)
+            hop(1, 1, place, 2)
+        elif s:
+            hop(s - 1, 0, place, s)
+
+    side = features // 2
+    strip = side // chips
+
+    def section(number, first, count):
+        at = pl.ds(first, count)
+        col = lambda c, j: at_block(c * chips + j, strip)
+        state = {}
+
+        def sem(n):
+            return s_send.at[number, n], s_recv.at[number, n]
+
+        def start():
+            state["core"] = remote(
+                sums.at[at, at_block(1 - core, side)], core_got.at[at, :], *sem(0), partner
+            )
+            state["core"].start()
+
+        def mid():
+            state["core"].wait()
+            half = at_block(core, side)
+            sums[at, half] = sums[at, half] + core_got[at, :]
+            state["chips"] = []
+            for s in range(1, chips):
+                copy = remote(
+                    sums.at[at, col(core, xor(chip, s))], chip_got.at[s - 1, at, :], *sem(s), across(s)
+                )
+                copy.start()
+                state["chips"].append(copy)
+
+        def add():
+            for copy in state["chips"]:
+                copy.wait()
+            total = sums[at, col(core, chip)].astype(f32)
+            for s in range(1, chips):
+                total += chip_got[s - 1, at, :].astype(f32)
+            piece[at, :] = total.astype(bf16)
+
+        def share(src=None, rows_to=at):
+            src = piece.at[at, :] if src is None else src
+            state["rows"] = rows_to
+            here = wide_ref.at[rows_to, col(core, chip)]
+            state["share"] = []
+            for s in range(1, chips):
+                copy = remote(src, here, *sem(chips + s), across(s))
+                copy.start()
+                state["share"].append(copy)
+            over = remote(src, here, *sem(chips), partner)
+            own = pltpu.make_async_copy(src, here, s_send.at[number, 3 * chips - 1])
+            over.start()
+            own.start()
+            state["wait"] = [over, own]
+
+        def forward():
+            for s in range(1, chips):
+                state["share"][s - 1].wait()
+                here = wide_ref.at[state["rows"], col(core, xor(chip, s))]
+                copy = remote(here, here, *sem(2 * chips - 1 + s), partner)
+                copy.start()
+                state["wait"].append(copy)
+
+        def end():
+            for copy in state["wait"]:
+                copy.wait()
+
+        return start, mid, add, share, forward, end
+
+    top = features + w_o.shape[0]
+    small = ceil_to(named + 1, 16)
+    of_o = section(0, features, w_o.shape[0])
+    of_d = section(1, 0, features)
+    of_g = section(2, top + 16, small)
+    of_a = section(3, top, 16)
+    router_part = dot(dzs[...], mrs[...], TN)[:named]
+
+    incoming = part[own_block, :].astype(f32)
+    for step in (1, 2, 3):
+        back[step].wait()
+        incoming += got[step - 1].astype(f32)
+    mid = middle[...]
+    inverse = lax.rsqrt(jnp.mean(mid * mid, axis=-1, keepdims=True) + epsilon)
+    unit = mid * inverse
+    scaled = incoming * expert_gain
+    dmid = cot[own_block, :].astype(f32) + inverse * (
+        scaled - unit * jnp.mean(scaled * unit, axis=-1, keepdims=True)
+    )
+    grad_x_ref[...] = dmid
+    das[own_block, :] = dmid.astype(bf16)
+    da_copies = spread(6, lambda s: das.at[own_block, :], lambda s: das.at[own_block, :])
+    sums[pl.ds(top + 16, small), :] = jnp.concatenate(
+        [
+            router_part,
+            jnp.sum(incoming * unit, axis=0, keepdims=True),
+            jnp.zeros((small - named - 1, features), f32),
+        ],
+        axis=0,
+    ).astype(bf16)
+    of_g[0]()
+    for block in range(n_head):
+        at = pl.ds(block * tokens, tokens)
+        unit = rows[at, :].astype(f32) * inverses[at, 0:1] * attend_gain
+        turned[:, at] = unit.astype(bf16).T
+    rows_t[...] = rows[...].T
+    of_g[1]()
+
+    lane = lax.broadcasted_iota(jnp.int32, (tokens, width), 1)
+
+    def through_output(block):
+        at = at_block(block, tokens)
+        all_five = dot(das[at, :], w_o[...], NT)
+        gates = squash[at, :] * gate_mask[at, :]
+        attended = att[at, :]
+        total = jnp.zeros((tokens, width), f32)
+        gate = jnp.zeros((tokens, width), f32)
+        for e in range(experts):
+            one = all_five[:, e * width : (e + 1) * width]
+            total += gates[:, experts + e : experts + e + 1] * one
+            gate = jnp.where(
+                lane == experts + e, jnp.sum(one * attended, axis=-1, keepdims=True), gate
+            )
+        datt[at, :] = total.astype(bf16)
+        gate_grads[at, :] = gate
+
+    through_output(h)
+    for step in (1, 2, 3):
+        da_copies[step].wait_recv()
+        through_output(xor(h, step))
+    out_copies = spread(
+        7, lambda s: outs.at[at_block(xor(h, s), tokens), :], lambda s: got_out.at[s - 1]
+    )
+
+    gates = squash[...] * gate_mask[...]
+    for e in range(experts):
+        one = (gates[:, experts + e : experts + e + 1] * att[...]).astype(bf16)
+        sums[pl.ds(features + e * width, width), :] = dot(one, das[...], TN).astype(bf16)
+    of_o[0]()
+
+    @pl.loop(0, n_head)
+    def _(block):
+        at = at_block(block, tokens)
+        chance = probs[at, :].astype(f32)
+        dprob = dot(datt[at, :], v[...], NT)
+        centre = jnp.sum(chance * dprob, axis=-1, keepdims=True)
+        scores[at, :] = (chance * (dprob - centre)).astype(bf16)
+
+    dq = dot(scores[...], k[...]) * scale
+    dk = dot(scores[...], q[...], TN) * scale
+    dv = dot(probs[...], datt[...], TN)
+    of_o[1]()
+    qkz[:, pl.ds(0, width)] = (dq * cosine[...] - swap_halves(dq) * sine[...]).astype(bf16)
+    qkz[:, pl.ds(width, width)] = (dk * cosine[...] - swap_halves(dk) * sine[...]).astype(bf16)
+    gate = gate_grads[...]
+    lane = lax.broadcasted_iota(jnp.int32, (group, width), 1)
+    for e in range(experts):
+        vgrads[:, pl.ds(e * width, width)] = (gates[:, e : e + 1] * dv).astype(bf16)
+        one = jnp.sum(vx[:, pl.ds(e * width, width)].astype(f32) * dv, axis=-1, keepdims=True)
+        gate = jnp.where(lane == e, one, gate)
+    qkz[:, pl.ds(2 * width, width)] = (gate * gates * (1.0 - squash[...])).astype(bf16)
+
+    @pl.loop(0, features // column)
+    def _(c):
+        at = at_block(c, column)
+        sums[at, pl.ds(0, 3 * width)] = dot(turned[at, :], qkz[...]).astype(bf16)
+        sums[at, pl.ds(3 * width, experts * width)] = dot(rows_t[at, :], vgrads[...]).astype(bf16)
+
+    of_d[0]()
+
+    def into_rows(block):
+        at = at_block(block, tokens)
+        inverse = inverses[at, 0:1]
+        unit = rows[at, :].astype(f32) * inverse
+        through = dot(qkz[at, :], w_an[...], NT)
+        scaled = through * attend_gain
+        total = inverse * (
+            scaled - unit * jnp.mean(scaled * unit, axis=-1, keepdims=True)
+        ) + dot(vgrads[at, :], w_v[...], NT)
+        return total, jnp.sum(through * unit, axis=0, keepdims=True)
+
+    gain = jnp.zeros((1, features), f32)
+    for step in peers:
+        total, one = into_rows(xor(h, step))
+        gain += one
+        part[at_block(xor(h, step), tokens), :] = total.astype(bf16)
+        back[step] = send_part(8, step)
+    total, one = into_rows(h)
+    gain_part[...] = jnp.broadcast_to(gain + one, gain_part.shape)
+    gain_copies = spread(9, lambda s: gain_part, lambda s: gain_got.at[s - 1])
+    grad_x_ref[...] += total
+    of_d[1]()
+    of_g[2]()
+
+    small_block = at_block(h, small)
+    blocks[small_block, :] = piece[pl.ds(top + 16, small), :]
+    g_copies = spread(10, lambda s: blocks.at[small_block, :], lambda s: blocks.at[small_block, :])
+    of_o[2]()
+    of_o[3]()
+
+    lasts = {}
+    for half in range(2):
+        toward = 2 - half
+        for index, place in ((1, xor(chip, toward)), (0, chip)):
+            for copy in hops[half, index]:
+                copy.wait()
+            at_in = (place, halves_in[half], own_side)
+            at_out = (place, halves_out(core)[half], slice(None))
+            w_in[at_in] = w_in[at_in] + hop_in[half, index]
+            w_out[at_out] = w_out[at_out] + hop_out[half, index]
+            if index:
+                pl.semaphore_signal(
+                    free.at[half], inc=1, device_id=across(toward), device_id_type=MESH
+                )
+                pl.semaphore_wait(free.at[half], 1)
+                lasts[half] = (
+                    remote(
+                        w_in.at[at_in],
+                        hop_in.at[half, 1],
+                        e_send.at[0, 4 + half],
+                        e_recv.at[0, 4 + half],
+                        across(toward),
+                    ),
+                    remote(
+                        w_out.at[at_out],
+                        hop_out.at[half, 1],
+                        e_send.at[1, 4 + half],
+                        e_recv.at[1, 4 + half],
+                        across(toward),
+                    ),
+                )
+                for copy in lasts[half]:
+                    copy.start()
+
+    gain = gain_part[...]
+    for step in peers:
+        gain_copies[step].wait()
+        gain += gain_got[step - 1]
+    sums[pl.ds(top, 16), :] = jnp.concatenate([gain, gain], axis=0).astype(bf16)
+    of_a[0]()
+    for step in peers:
+        g_copies[step].wait()
+    of_g[3](blocks, pl.ds(top + 16, n_head * small))
+    of_a[1]()
+
+    output = middle[...] + outs[own_block, :].astype(f32)
+    for step in peers:
+        out_copies[step].wait()
+        output += got_out[step - 1].astype(f32)
+    output_ref[...] = output
+    of_d[2]()
+    of_d[3]()
+    of_a[2]()
+    of_a[3]()
+    of_o[4]()
+    of_g[4]()
+    for step in peers:
+        back[step].wait()
+        grad_x_ref[...] += got[step - 1].astype(f32)
+    for half in range(2):
+        for copy in lasts[half]:
+            copy.wait()
+        at_in = (chip, halves_in[half], own_side)
+        at_out = (chip, halves_out(core)[half], slice(None))
+        w_in[at_in] = w_in[at_in] + hop_in[half, 1]
+        w_out[at_out] = w_out[at_out] + hop_out[half, 1]
+    stores = (
+        pltpu.make_async_copy(w_in.at[chip, :, own_side], fin_in_ref, local_sem.at[0]),
+        pltpu.make_async_copy(w_out.at[chip, own_side, :], fin_out_ref, local_sem.at[1]),
+    )
+    for store in stores:
+        store.start()
+    of_d[4]()
+    of_a[4]()
+    for one in (of_o, of_g, of_d, of_a):
+        one[5]()
+    for store in stores:
+        store.wait()
+    for step in peers:
+        mr_copies[step].wait_send()
+        da_copies[step].wait_send()
+
+
+def layer_call(n_dp, n_head, args):
+    x, picks, router, value_mat, expert_in = args[0], args[2], args[13], args[11], args[14]
+    tokens, features = x.shape
+    per_device, _, width = expert_in.shape
+    held_experts = value_mat.shape[1]
+    group = tokens * n_head
+    chips = n_dp // 2
+    slab = per_device * width
+    lanes = 128
+    peers = n_head - 1
+    named = ceil_to(n_dp * per_device, 8)
+    small = ceil_to(named + 1, 16)
+    top = features + held_experts
+    held = top + 16 + small
+    strip = features // n_dp
+    shape = jax.ShapeDtypeStruct
+    vm, dma = pltpu.VMEM, pltpu.SemaphoreType.DMA
+    outs = [
+        (shape((tokens, features), f32), VM),
+        (shape((tokens, features), f32), VM),
+        (shape((top + 16 + n_head * small, features), bf16), ANY),
+        (shape((features, slab), bf16), ANY),
+        (shape((slab, features), bf16), ANY),
+    ]
+    scratch = dict(
+        picks=vm(picks.shape, jnp.int32),
+        head_picks=vm(args[3].shape, jnp.int32),
+        seg=vm((1, group), jnp.int32),
+        gains=vm(args[5].shape, f32),
+        cosine=vm((group, width), f32),
+        sine=vm((group, width), f32),
+        w_an=vm((features, 3 * width), bf16),
+        w_v=vm((features, held_experts), bf16),
+        w_o=vm((held_experts, features), bf16),
+        my_router=vm((features, lanes), bf16),
+        w_in=vm((chips, features, 2 * slab), bf16),
+        w_out=vm((chips, 2 * slab, features), bf16),
+        rows=vm((group, features), bf16),
+        cot=vm((group, features), bf16),
+        mrs=vm((group, features), bf16),
+        das=vm((group, features), bf16),
+        turned=vm((features, group), bf16),
+        rows_t=vm((features, group), bf16),
+        inverses=vm((group, width), f32),
+        my_mask=vm((n_head, tokens, lanes), bf16),
+        all_mask=vm((group, lanes), bf16),
+        gate_mask=vm((group, width), f32),
+        q=vm((group, width), bf16),
+        k=vm((group, width), bf16),
+        v=vm((group, width), bf16),
+        vx=vm((group, held_experts), bf16),
+        squash=vm((group, width), f32),
+        att=vm((group, width), f32),
+        middle=vm((tokens, features), f32),
+        part=vm((group, features), bf16),
+        got=vm((peers, tokens, features), bf16),
+        outs=vm((group, features), bf16),
+        got_out=vm((peers, tokens, features), bf16),
+        lifted=vm((chips, 2, group, slab), bf16),
+        core_out=vm((chips, slab, features), bf16),
+        acts=vm((chips, group, 2 * slab), bf16),
+        hids=vm((chips, group, 2 * slab), bf16),
+        dzs=vm((group, lanes), bf16),
+        datt=vm((group, width), bf16),
+        gate_grads=vm((group, width), f32),
+        probs=vm((group, group), bf16),
+        scores=vm((group, group), bf16),
+        qkz=vm((group, 3 * width), bf16),
+        vgrads=vm((group, held_experts), bf16),
+        gain_part=vm((8, features), f32),
+        gain_got=vm((peers, 8, features), f32),
+        sums=vm((held, features), bf16),
+        core_got=vm((held, features // 2), bf16),
+        chip_got=vm((chips - 1, held, strip), bf16),
+        piece=vm((held, strip), bf16),
+        blocks=vm((n_head * small, strip), bf16),
+        hop_in=vm((2, 2, features // 2, slab), bf16),
+        hop_out=vm((2, 2, slab // 2, features), bf16),
+        local_sem=dma((15 + 1 + per_device,)),
+        z_send=dma((11, peers)),
+        z_recv=dma((11, peers)),
+        w_send=dma((22,)),
+        w_recv=dma((22,)),
+        c_send=dma((3, chips)),
+        c_recv=dma((3, chips)),
+        e_send=dma((2, 6)),
+        e_recv=dma((2, 6)),
+        s_send=dma((4, 3 * chips)),
+        s_recv=dma((4, 3 * chips)),
+        ready=pltpu.SemaphoreType.REGULAR,
+        free=pltpu.SemaphoreType.REGULAR((2,)),
+    )
+    return pl.pallas_call(
+        functools.partial(layer_kernel, n_dp, n_head),
+        out_shape=[o[0] for o in outs],
+        out_specs=[o[1] for o in outs],
+        in_specs=[ANY] * 16,
+        scratch_shapes=list(scratch.values()),
+        compiler_params=pltpu.CompilerParams(
+            collective_id=1, has_side_effects=True, vmem_limit_bytes=vmem_bytes
+        ),
+    )(*args)
+
+
+def finish_kernel(
+    n_dp,
+    n_head,
+    output_ref,
+    grad_x_ref,
+    wide_ref,
+    in_ref,
+    out_ref,
+    final_ref,
+    input_ref,
+    attend_ref,
+    query_ref,
+    key_ref,
+    value_ref,
+    mix_ref,
+    gate_ref,
+    expert_ref,
+    router_ref,
+    grad_in_ref,
+    grad_out_ref,
+    wide,
+    flat_in,
+    flat_out,
+    value,
+    mix,
+    grad_in,
+    grad_out,
+    sem,
+):
+    features, slab = in_ref.shape
+    per_device, _, width = grad_in_ref.shape
+    experts_total = router_ref.shape[1]
+    gates = gate_ref.shape[1]
+    top = features + mix_ref.shape[0]
+    small = (wide_ref.shape[0] - top - 16) // n_head
+    named = n_dp * per_device
+
+    def copy(src, dst, number):
+        one = pltpu.make_async_copy(src, dst, sem.at[number])
+        one.start()
+        return one
+
+    rest = pl.ds(top, wide_ref.shape[0] - top)
+    loads = [
+        copy(wide_ref.at[pl.ds(0, features), :], wide.at[pl.ds(0, features), :], 0),
+        copy(wide_ref.at[pl.ds(features, top - features), :], wide.at[pl.ds(features, top - features), :], 1),
+        copy(in_ref, flat_in, 2),
+        copy(out_ref, flat_out, 3),
+        copy(wide_ref.at[rest, :], wide.at[rest, :], 4),
+    ]
+    stores = [copy(output_ref, final_ref, 5), copy(grad_x_ref, input_ref, 6)]
+    loads[0].wait()
+    first = pl.ds(0, features)
+    value[...] = wide[first, pl.ds(3 * width, value.shape[1])].astype(f32)
+    stores.append(copy(value, value_ref, 7))
+    query_ref[...] = wide[first, pl.ds(0, width)].astype(f32)
+    key_ref[...] = wide[first, pl.ds(width, width)].astype(f32)
+    gate_ref[...] = wide[first, pl.ds(2 * width, width)][:, :gates].astype(f32)
+    loads[1].wait()
+    mix[...] = wide[pl.ds(features, top - features), :].astype(f32)
+    stores.append(copy(mix, mix_ref, 8))
+    loads[2].wait()
+    for e in range(per_device):
+        grad_in[e] = flat_in[:, pl.ds(e * width, width)].astype(f32)
+    stores.append(copy(grad_in, grad_in_ref, 9))
+    loads[3].wait()
+    for e in range(per_device):
+        grad_out[e] = flat_out[pl.ds(e * width, width), :].astype(f32)
+    stores.append(copy(grad_out, grad_out_ref, 10))
+    loads[4].wait()
+    attend_ref[...] = wide[pl.ds(top, 16), :][0:1].astype(f32)
+    planes = wide[pl.ds(top + 16, n_head * small), :]
+    place = lax.broadcasted_iota(jnp.int32, (n_head * small, experts_total), 0)
+    name = lax.broadcasted_iota(jnp.int32, (n_head * small, experts_total), 1)
+    slot, plane = place % small, place // small
+    expert = (slot // per_device * n_head + plane) * per_device + slot % per_device
+    chosen = (slot < named) & (expert == name)
+    router_ref[...] = dot(planes, jnp.where(chosen, 1.0, 0.0).astype(bf16), TN)
+    gain = jnp.zeros((1, features), f32)
+    for z in range(n_head):
+        row = z * small + ceil_to(named, 8)
+        gain += planes[row : row + 1].astype(f32)
+    expert_ref[...] = gain
+    for store in stores:
+        store.wait()
+
+
+def finish_call(n_dp, n_head, shapes, args):
+    shape = jax.ShapeDtypeStruct
+    wide, flat_in, flat_out = args[2], args[3], args[4]
+    value, mix, grad_in, grad_out = shapes[5], shapes[6], shapes[10], shapes[11]
+    specs = [VM] * 12
+    for number in (0, 1, 5, 6, 10, 11):
+        specs[number] = ANY
+    return pl.pallas_call(
+        functools.partial(finish_kernel, n_dp, n_head),
+        out_shape=[shape(s, f32) for s in shapes],
+        out_specs=specs,
+        in_specs=[ANY] * 5,
+        scratch_shapes=[
+            pltpu.VMEM(wide.shape, bf16),
+            pltpu.VMEM(flat_in.shape, bf16),
+            pltpu.VMEM(flat_out.shape, bf16),
+            pltpu.VMEM(value, f32),
+            pltpu.VMEM(mix, f32),
+            pltpu.VMEM(grad_in, f32),
+            pltpu.VMEM(grad_out, f32),
+            pltpu.SemaphoreType.DMA((11,)),
+        ],
+        compiler_params=pltpu.CompilerParams(vmem_limit_bytes=48 << 20),
+    )(*args)
+
+
+def kernel_body(
+    n_dp,
+    n_head,
+    hidden_in,
+    segments,
+    value_pick,
+    output_pick,
+    expert_pick,
+    attend_gain,
+    query_weight,
+    key_weight,
+    value_weight,
+    output_weight,
+    head_router,
+    expert_gain,
+    router,
+    expert_in,
+    expert_out,
+    cotangent,
+):
+    tokens, features = hidden_in.shape
+    per_device, _, width = expert_in.shape
+    experts = head_router.shape[2] // 2
+    group = tokens * n_head
+    angles = np.arange(group)[:, None] * theta ** (-2.0 * np.arange(width // 2) / width)[None, :]
+    cosine = np.concatenate([np.cos(angles)] * 2, axis=1).astype(np.float32)
+    sine = np.concatenate([-np.sin(angles), np.sin(angles)], axis=1).astype(np.float32)
+    head_picks = jnp.concatenate([value_pick[:, 0], output_pick[:, 0] + experts], axis=1)
+    gains = jnp.stack([attend_gain, expert_gain]).astype(f32)
+    results = layer_call(
+        n_dp,
+        n_head,
+        (
+            hidden_in,
+            cotangent,
+            expert_pick,
+            head_picks,
+            segments[None, :],
+            gains,
+            cosine,
+            sine,
+            query_weight[0],
+            key_weight[0],
+            jnp.pad(head_router[0], ((0, 0), (0, width - 2 * experts))),
+            value_weight[0],
+            output_weight[0],
+            jnp.pad(router, ((0, 0), (0, width - router.shape[1]))),
+            expert_in,
+            expert_out.reshape(per_device * width, features),
+        ),
+    )
+    shapes = (
+        (tokens, features),
+        (tokens, features),
+        (1, features),
+        query_weight.shape[1:],
+        key_weight.shape[1:],
+        value_weight.shape[1:],
+        output_weight.shape[1:],
+        head_router.shape[1:],
+        (1, features),
+        router.shape,
+        expert_in.shape,
+        expert_out.shape,
+    )
+    done = list(finish_call(n_dp, n_head, shapes, results))
+    for number in (3, 4, 5, 6, 7):
+        done[number] = done[number][None]
+    done[2], done[8] = done[2][0], done[8][0]
+    return tuple(done)
+
+
 def solution(mesh):
     rows = P(everywhere, None)
     heads = P("head", None, None)
@@ -235,4 +1326,12 @@
     out_specs = (
         rows, rows, P(), heads, heads, heads, heads, heads, P(), P(), experts, experts,
     )
-    return jax.shard_map(body, mesh=mesh, in_specs=in_specs, out_specs=out_specs, check_vma=False)
+    n_dp, n_head = mesh.shape["dp"], mesh.shape["head"]
+
+    def program(*args):
+        held = 2 * n_dp * args[13].shape[0] * args[13].shape[1] * args[13].shape[2] * 2
+        if n_head == 4 and held <= vmem_for_weights:
+            return kernel_body(n_dp, n_head, *args)
+        return body(*args)
+
+    return jax.shard_map(program, mesh=mesh, in_specs=in_specs, out_specs=out_specs, check_vma=False)

time: 806 us -> 245 us (0.30)
  waiting for transfers between devices: 438 us -> 0 us
  Pallas kernels: 2.62 us -> 228 us
  blocking collectives: 206 us -> 0 us
  matrix products: 103 us -> 0 us
  other arithmetic: 21.9 us -> 2 us
  between operations: 15.1 us -> 0.69 us
    reduce_scatter x4 -> x0, waiting for transfers between devices: 309 us -> none  [the longest x1 184 us: turn(): lax.psum_scatter(part_grad, everywhere, scatter_dimension=0, tiled=True)]
    pallas_call x0 -> x2, Pallas kernels: none -> 228 us  [the longest x1 222 us: layer_call(): pl.pallas_call(functools.partial(layer_kernel, n_dp, n_head), out_shape=[...]
    all_gather x2 -> x0, blocking collectives: 142 us -> none  [the longest x1 73 us: body(): grad_router = lax.all_gather(grads[2], everywhere, axis=0, tiled=True).T]
    all_gather x4 -> x0, waiting for transfers between devices: 127 us -> none  [the longest x1 67.6 us: turn(): all_cot = lax.all_gather(own_cot, everywhere, axis=0, tiled=True)]
    dot_general x29 -> x0, matrix products: 103 us -> none  [product(): lax.dot_general(left, right, (((left_axis,), (right_axis,)), ((), ())), p...]
    psum x2 -> x0, blocking collectives: 63.5 us -> none  [the longest x1 39.9 us: body(): lax.psum((grad_attend, grad_gain_expert), everywhere)]
  transfers between devices with their start and end apart: 9 -> 0, of which waited for: 8 -> 0; matrix products, arithmetic and copies ran while one was open for 9% -> 0% of each run, Pallas kernels for 0% -> 0%
where the time goes in v4:
time: 245 us; the launch traced here: 244 us
  Pallas kernels  228 us (93%)
  local copies, waits for them, and re-layouts  13.3 us (5%)
    pallas_call x1, Pallas kernels, layer_call(): pl.pallas_call(functools.partial(layer_kernel, n_dp, n_head), out_shape=[...  222 us
    unnamed x13, local copies, waits for them, and re-layouts  9.55 us
    pallas_call x1, Pallas kernels, finish_call(): pl.pallas_call(functools.partial(finish_kernel, n_dp, n_head), out_shape=...  6.54 us

profile of v4, /device:TPU:0, one launch (start us, length us, event | category | flops | bytes accessed | tf_op | source)
XLA Modules:
  0.0 244.2 jit_solution(2979911801611011779)
XLA Ops:
  0.6 0.7 add_bitcast_fusion
  1.3 0.7 pad_add_fusion
  2.0 0.7 stack.9
  2.7 0.7 stack.10
  3.4 0.6 maximum_convert_fusion.gain_ref
  4.0 1.4 copy.39.pick_ref
  5.4 0.9 copy.40.head_pick_ref
  6.3 0.9 copy.37
  7.2 0.8 pad.8.wg_ref
  8.0 1.1 copy.38
  9.1 0.8 pad.9.router_ref
  9.9 221.7 %shard_map.265 = (f32[128,1024]{1,0:T(8,128)}, f32[128,1024]{1,0:T(8,128)}, bf16[1808,1024]{1,0:T(8,128)(2,1)}, bf16[1024,384]{1,0:T(8,128)(2,1)}, bf16[384,1024]{1,0:T(8,128)(2,1)}) custom-call(bf16[128,1024]{1,0:T(8,128)(2,1)} %x_ref.1, bf16[128,1024]{1,0:T(8,128)(2,1)} %cot_ref.1, s32[128,16]{1,0:T(8,128)} %copy.39.pick_ref, ...), custom_call_target="tpu_custom_call" | custom-call | tf_op jit(solution)/shard_map/pallas_call | solution.py:1120
  231.6 0.0 copy-start
  231.6 1.1 copy-done
  232.7 0.0 copy-start.1
  232.7 1.1 copy-done.1
  233.8 0.0 copy-start.2
  233.8 1.0 copy-done.2
  234.9 0.0 copy-start.3
  234.9 1.0 copy-done.3
  235.9 6.5 %shard_map.266 = (f32[128,1024]{1,0:T(8,128)}, f32[128,1024]{1,0:T(8,128)}, f32[1,1024]{1,0:T(1,128)}, f32[1024,128]{1,0:T(8,128)}, f32[1024,128]{1,0:T(8,128)},...) custom-call(f32[128,1024]{1,0:T(8,128)S(1)} %copy-done.2, ...), custom_call_target="tpu_custom_call" | custom-call | tf_op jit(solution)/shard_map/pallas_call | solution.py:1226
  242.5 0.8 copy.41
  243.3 0.9 copy.42
Async XLA Ops:
  231.6 1.1 copy-start
  232.7 1.1 copy-start.1
  233.8 1.0 copy-start.2
  234.9 1.0 copy-start.3

commit v5 on v4

--- a/solution.py
+++ b/solution.py
@@ -270,8 +270,7 @@
     head_pick_ref,
     seg_ref,
     gain_ref,
-    cos_ref,
-    sin_ref,
+    angle_ref,
     wq_ref,
     wk_ref,
     wg_ref,
@@ -289,8 +288,7 @@
     head_picks,
     seg,
     gains,
-    cosine,
-    sine,
+    angles,
     w_an,
     w_v,
     w_o,
@@ -302,18 +300,14 @@
     mrs,
     das,
     turned,
-    rows_t,
-    inverses,
     my_mask,
     all_mask,
-    gate_mask,
+    gates,
     q,
     k,
     v,
     vx,
-    squash,
     att,
-    middle,
     part,
     got,
     outs,
@@ -352,6 +346,7 @@
     ready,
     free,
 ):
+    middle = output_ref
     xor = jnp.bitwise_xor
     d, h = lax.axis_index("dp"), lax.axis_index("head")
     chip, core = d // 2, d % 2
@@ -403,8 +398,7 @@
         load(wk_ref, w_an.at[:, pl.ds(width, width)]),
         load(wv_ref, w_v),
         load(head_pick_ref, head_picks),
-        load(cos_ref, cosine),
-        load(sin_ref, sine),
+        load(angle_ref, angles),
     ]
     for_scores = [load(seg_ref, seg), load(wo_ref, w_o)]
     for_mask = load(pick_ref, picks)
@@ -416,6 +410,114 @@
     for friend in friends:
         pl.semaphore_signal(barrier, inc=1, device_id=friend, device_id_type=MESH)
     pl.semaphore_wait(barrier, len(friends))
+
+    right, left = (d, jnp.minimum(h + 1, n_head - 1)), (d, jnp.maximum(h - 1, 0))
+    last = n_head - 1
+
+    def pick(*by_place):
+        value = jnp.int32(by_place[-1])
+        for place in range(n_head - 2, -1, -1):
+            value = jnp.where(h == place, by_place[place], value)
+        return value
+
+    arrival = (xor(h, 1), pick(2, 2, 1, 1), pick(3, 3, 0, 0))
+    leaving = (pick(3, 3, 0, 0), pick(2, 0, 3, 1), pick(1, 2, 1, 2))
+
+    def gather(kind, buffer):
+        def go(side, step):
+            block = jnp.clip(h - step if side == 0 else h + step, 0, last)
+            here = buffer.at[at_block(block, tokens), :]
+            number = side * last + step
+            return remote(
+                here, here, z_send.at[kind, number], z_recv.at[kind, number], (right, left)[side]
+            )
+
+        def start():
+            @pl.when(h < last)
+            def _():
+                go(0, 0).start()
+
+            @pl.when(h > 0)
+            def _():
+                go(1, 0).start()
+
+        def stage(step):
+            @pl.when(h >= step)
+            def _():
+                go(0, step - 1).wait_recv()
+
+            if step < last:
+
+                @pl.when((h >= step) & (h < last))
+                def _():
+                    go(0, step).start()
+
+            @pl.when(h + step <= last)
+            def _():
+                go(1, step - 1).wait_recv()
+
+            if step < last:
+
+                @pl.when((h + step <= last) & (h > 0))
+                def _():
+                    go(1, step).start()
+
+        def end():
+            for step in range(last):
+
+                @pl.when((h >= step) & (h < last))
+                def _():
+                    go(0, step).wait_send()
+
+                @pl.when((h + step <= last) & (h > 0))
+                def _():
+                    go(1, step).wait_send()
+
+        return start, stage, end
+
+    def chain_sum(kind, parts, slots):
+        def go(number):
+            block = leaving[number]
+            rightward = block > h
+            slot = jnp.where(rightward, block - 1, last + block)
+            where = (d, jnp.clip(jnp.where(rightward, h + 1, h - 1), 0, last))
+            at = at_block(block, tokens)
+            copy = remote(
+                parts.at[at, :], slots.at[slot], z_send.at[kind, number], z_recv.at[kind, slot], where
+            )
+            middle_one = (rightward & (h > 0)) | (jnp.logical_not(rightward) & (h < last))
+            return copy, middle_one, at, slot
+
+        def now(number):
+            copy, middle_one, _, _ = go(number)
+
+            @pl.when(jnp.logical_not(middle_one))
+            def _():
+                copy.start()
+
+        def later(number):
+            copy, middle_one, at, slot = go(number)
+
+            @pl.when(middle_one)
+            def _():
+                copy.wait_recv()
+                parts[at, :] = parts[at, :] + slots[slot]
+                copy.start()
+
+        def end(total):
+            for slot, there in ((jnp.maximum(h - 1, 0), h > 0), (last + jnp.minimum(h, last - 1), h < last)):
+
+                @pl.when(there)
+                def _():
+                    remote(
+                        parts.at[own_block, :], slots.at[slot], z_send.at[kind, 0], z_recv.at[kind, slot], right
+                    ).wait_recv()
+                    total[...] += slots[slot].astype(f32)
+
+            for number in range(last):
+                go(number)[0].wait_send()
+
+        return now, later, end
 
     def spread(kind, src, dst, steps=peers):
         copies = {}
@@ -426,7 +528,9 @@
             copies[step].start()
         return copies
 
-    x_copies = spread(0, lambda s: x_ref, lambda s: rows.at[own_block, :])
+    x_start, x_stage, x_end = gather(0, rows)
+    for_rows[0].wait()
+    x_start()
 
     def slot(array, place, side, half=None):
         if array == 0:
@@ -465,52 +569,52 @@
     mask_copies = spread(1, lambda s: my_mask.at[xor(h, s)], lambda s: all_mask.at[own_block, :])
     all_mask[own_block, :] = my_mask[h]
 
-    for copy in for_rows:
+    for copy in for_rows[1:]:
         copy.wait()
     attend_gain = gains[0:1, :]
     expert_gain = gains[1:2, :]
-    lane = lax.broadcasted_iota(jnp.int32, (group, width), 1)
-    hit = lane == head_picks[:, 0:1]
-    for c in range(1, head_picks.shape[1]):
-        hit = hit | (lane == head_picks[:, c : c + 1])
-    gate_mask[...] = jnp.where(hit, 1.0, 0.0)
+    half_lanes = lax.broadcasted_iota(jnp.int32, (1, width), 1) < width // 2
+
+    def turns(at):
+        both = angles[at, :]
+        turned_over = swap_halves(both)
+        return (
+            jnp.where(half_lanes, both, turned_over),
+            jnp.where(half_lanes, -turned_over, both),
+        )
 
     def project(block):
         at = at_block(block, tokens)
         own = rows[at, :]
         full = own.astype(f32)
         inverse = lax.rsqrt(jnp.mean(full * full, axis=-1, keepdims=True) + epsilon)
-        inverses[at, :] = jnp.broadcast_to(inverse, (tokens, width))
         unit = (full * inverse * attend_gain).astype(bf16)
         qkg = dot(unit, w_an[...])
-        c, s = cosine[at, :], sine[at, :]
+        c, s = turns(at)
         one, two = qkg[:, :width], qkg[:, width : 2 * width]
         q[at, :] = (one * c + swap_halves(one) * s).astype(bf16)
         k[at, :] = (two * c + swap_halves(two) * s).astype(bf16)
-        squashed = jax.nn.sigmoid(qkg[:, 2 * width :])
-        squash[at, :] = squashed
-        gates = squashed * gate_mask[at, :]
+        lane = lax.broadcasted_iota(jnp.int32, (tokens, width), 1)
+        chosen = head_picks[at, :]
+        hit = lane == chosen[:, 0:1]
+        for c in range(1, chosen.shape[1]):
+            hit = hit | (lane == chosen[:, c : c + 1])
+        gate = jnp.where(hit, jax.nn.sigmoid(qkg[:, 2 * width :]), 0.0)
+        gates[at, :] = jnp.where(lane == width - 1, inverse, gate)
         values = dot(own, w_v[...])
         vx[at, :] = values.astype(bf16)
-        value = gates[:, 0:1] * values[:, :width]
+        value = gate[:, 0:1] * values[:, :width]
         for e in range(1, experts):
-            value += gates[:, e : e + 1] * values[:, e * width : (e + 1) * width]
+            value += gate[:, e : e + 1] * values[:, e * width : (e + 1) * width]
         v[at, :] = value.astype(bf16)
 
     project(h)
     for step in (1, 2, 3):
-        x_copies[step].wait_recv()
-        project(xor(h, step))
-    cot_copies = spread(2, lambda s: cot_ref, lambda s: cot.at[own_block, :])
-    for half in range(2):
-        for array in range(2):
-            slabs[1 + half, half, array].wait_recv()
-            halves_on[half, array] = weights(
-                8 + 2 * half + array,
-                slot(array, xor(chip, 1 + half), core, half),
-                across(2 - half),
-            )
-
+        x_stage(step)
+        project(arrival[step - 1])
+    cot_start, cot_stage, cot_end = gather(2, cot)
+    for_cot.wait()
+    cot_start()
     for copy in for_scores:
         copy.wait()
     seg_col = gate_grads
@@ -528,33 +632,36 @@
         probs[at, :] = chance.astype(bf16)
         attended = dot(chance.astype(bf16), v[...])
         att[at, :] = attended
-        gates = squash[at, :] * gate_mask[at, :]
+        gate = gates[at, :]
         weighted = jnp.concatenate(
             [
-                (gates[:, experts + e : experts + e + 1] * attended).astype(bf16)
+                (gate[:, experts + e : experts + e + 1] * attended).astype(bf16)
                 for e in range(experts)
             ],
             axis=-1,
         )
         return dot(weighted, w_o[...])
 
-    def send_part(kind, step):
-        copy = remote(
-            part.at[at_block(xor(h, step), tokens), :],
-            got.at[step - 1],
-            z_send.at[kind, step - 1],
-            z_recv.at[kind, step - 1],
-            along(step),
-        )
-        copy.start()
-        return copy
-
-    back = {}
-    for step in peers:
-        part[at_block(xor(h, step), tokens), :] = attend(xor(h, step)).astype(bf16)
-        back[step] = send_part(3, step)
-    mid = rows[own_block, :].astype(f32) + attend(h)
-
+    to_mid = chain_sum(3, part, got)
+    for number in range(last):
+        block = leaving[number]
+        part[at_block(block, tokens), :] = attend(block).astype(bf16)
+        to_mid[0](number)
+    middle[...] = rows[own_block, :].astype(f32) + attend(h)
+    to_mid[1](0)
+    cot_stage(1)
+    for half in range(2):
+        for array in range(2):
+            slabs[1 + half, half, array].wait_recv()
+            halves_on[half, array] = weights(
+                8 + 2 * half + array,
+                slot(array, xor(chip, 1 + half), core, half),
+                across(2 - half),
+            )
+
+    to_mid[1](1)
+    cot_stage(2)
+    to_mid[1](2)
     for bit in (1, 2):
         slabs[bit, 2 - bit, 0].wait_recv()
         to_core[bit, 0] = weights(14 + (bit - 1) * 2, slot(0, xor(chip, bit), core), partner)
@@ -567,13 +674,13 @@
     expert = jnp.where(slot_of < n_dp * per_device, expert, -1)
     my_router[...] = dot(turned[:, pl.ds(0, lanes)], jnp.where(name == expert, 1.0, 0.0).astype(bf16)).astype(bf16)
 
-    for step in peers:
-        back[step].wait()
-        mid += got[step - 1].astype(f32)
-    middle[...] = mid
+    to_mid[2](middle)
+    mid = middle[...]
     inverse = lax.rsqrt(jnp.mean(mid * mid, axis=-1, keepdims=True) + epsilon)
     mrs[own_block, :] = (mid * inverse * expert_gain).astype(bf16)
-    mr_copies = spread(4, lambda s: mrs.at[own_block, :], lambda s: mrs.at[own_block, :], (1, 2, 3))
+    mr_start, mr_stage, mr_end = gather(4, mrs)
+    mr_start()
+    cot_stage(3)
 
     for array in range(2):
         for half in range(2):
@@ -581,11 +688,10 @@
             diagonal[half, array] = weights(
                 18 + 2 * half + array, slot(array, xor(chip, 3), core, half), partner
             )
-    for_cot.wait()
     for step in peers:
-        cot_copies[step].wait()
-        x_copies[step].wait_send()
         mask_copies[step].wait()
+    cot_end()
+    x_end()
 
     def weights_here(array):
         for bit in range(3):
@@ -611,7 +717,7 @@
         slot = lax.broadcasted_iota(jnp.int32, (lanes, wide), 0)
         return jnp.where(slot == lane + j * (wide // width), 1.0, 0.0).astype(bf16)
 
-    def pair_of_blocks(number):
+    def pair_of_blocks(number, between):
         at = at_block(number, pair)
         own = mrs[at, :]
         gates = jax.nn.sigmoid(dot(own, my_router[...]))
@@ -639,6 +745,7 @@
         total = lax.fori_loop(0, chips, chip_step, jnp.zeros((pair, lanes), f32))
         dz = (total * live * (1.0 - gates)).astype(bf16)
         dzs[at, :] = dz
+        between()
 
         @pl.loop(0, features // column)
         def _(c):
@@ -648,23 +755,29 @@
                 total += dot(hids[j, at, :], w_in[j, part_of, :], NT)
             part[at, part_of] = total.astype(bf16)
 
+    def outputs(number):
+        at = at_block(number, pair)
+
+        @pl.loop(0, features // column)
+        def _(c):
+            part_of = at_block(c, column)
+            total = dot(acts[0, at, :], w_out[0, :, part_of])
+            for j in range(1, chips):
+                total += dot(acts[j, at, :], w_out[j, :, part_of])
+            outs[at, part_of] = total.astype(bf16)
+
     near = h // 2
-    mr_copies[1].wait_recv()
-    pair_of_blocks(near)
-    back = {1: send_part(5, 1)}
-    mr_copies[2].wait_recv()
-    mr_copies[3].wait_recv()
-    pair_of_blocks(1 - near)
-    back[2], back[3] = send_part(5, 2), send_part(5, 3)
+    to_dmr = chain_sum(5, part, got)
+    mr_stage(1)
+    pair_of_blocks(near, lambda: mr_stage(2))
+    to_dmr[0](2)
+    outputs(near)
+    mr_stage(3)
+    pair_of_blocks(1 - near, lambda: None)
+    to_dmr[0](0)
+    to_dmr[0](1)
+    outputs(1 - near)
     pl.semaphore_signal(ready, inc=1, device_id=partner, device_id_type=MESH)
-
-    @pl.loop(0, features // column)
-    def _(c):
-        part_of = at_block(c, column)
-        total = dot(acts[0], w_out[0, :, part_of])
-        for j in range(1, chips):
-            total += dot(acts[j], w_out[j, :, part_of])
-        outs[:, part_of] = total.astype(bf16)
 
     turned[...] = mrs[...].T
 
@@ -708,6 +821,7 @@
     def _(n):
         expert_grads(xor(chip, chips - 1 - n), own_side)
 
+    to_dmr[1](0)
     hops = {}
 
     def hop(half, index, place, toward):
@@ -746,6 +860,8 @@
         elif s:
             hop(s - 1, 0, place, s)
 
+    to_dmr[1](1)
+    to_dmr[1](2)
     side = features // 2
     strip = side // chips
 
@@ -820,10 +936,9 @@
     of_a = section(3, top, 16)
     router_part = dot(dzs[...], mrs[...], TN)[:named]
 
-    incoming = part[own_block, :].astype(f32)
-    for step in (1, 2, 3):
-        back[step].wait()
-        incoming += got[step - 1].astype(f32)
+    grad_x_ref[...] = part[own_block, :].astype(f32)
+    to_dmr[2](grad_x_ref)
+    incoming = grad_x_ref[...]
     mid = middle[...]
     inverse = lax.rsqrt(jnp.mean(mid * mid, axis=-1, keepdims=True) + epsilon)
     unit = mid * inverse
@@ -833,7 +948,8 @@
     )
     grad_x_ref[...] = dmid
     das[own_block, :] = dmid.astype(bf16)
-    da_copies = spread(6, lambda s: das.at[own_block, :], lambda s: das.at[own_block, :])
+    da_start, da_stage, da_end = gather(6, das)
+    da_start()
     sums[pl.ds(top + 16, small), :] = jnp.concatenate(
         [
             router_part,
@@ -843,25 +959,19 @@
         axis=0,
     ).astype(bf16)
     of_g[0]()
-    for block in range(n_head):
-        at = pl.ds(block * tokens, tokens)
-        unit = rows[at, :].astype(f32) * inverses[at, 0:1] * attend_gain
-        turned[:, at] = unit.astype(bf16).T
-    rows_t[...] = rows[...].T
+    turned[...] = rows[...].T
     of_g[1]()
-
     lane = lax.broadcasted_iota(jnp.int32, (tokens, width), 1)
 
     def through_output(block):
         at = at_block(block, tokens)
         all_five = dot(das[at, :], w_o[...], NT)
-        gates = squash[at, :] * gate_mask[at, :]
         attended = att[at, :]
         total = jnp.zeros((tokens, width), f32)
         gate = jnp.zeros((tokens, width), f32)
         for e in range(experts):
             one = all_five[:, e * width : (e + 1) * width]
-            total += gates[:, experts + e : experts + e + 1] * one
+            total += gates[at, experts + e : experts + e + 1] * one
             gate = jnp.where(
                 lane == experts + e, jnp.sum(one * attended, axis=-1, keepdims=True), gate
             )
@@ -870,13 +980,11 @@
 
     through_output(h)
     for step in (1, 2, 3):
-        da_copies[step].wait_recv()
-        through_output(xor(h, step))
-    out_copies = spread(
-        7, lambda s: outs.at[at_block(xor(h, s), tokens), :], lambda s: got_out.at[s - 1]
-    )
-
-    gates = squash[...] * gate_mask[...]
+        da_stage(step)
+        through_output(arrival[step - 1])
+    to_out = chain_sum(7, outs, got_out)
+    to_out[0](0)
+
     for e in range(experts):
         one = (gates[:, experts + e : experts + e + 1] * att[...]).astype(bf16)
         sums[pl.ds(features + e * width, width), :] = dot(one, das[...], TN).astype(bf16)
@@ -894,27 +1002,30 @@
     dk = dot(scores[...], q[...], TN) * scale
     dv = dot(probs[...], datt[...], TN)
     of_o[1]()
-    qkz[:, pl.ds(0, width)] = (dq * cosine[...] - swap_halves(dq) * sine[...]).astype(bf16)
-    qkz[:, pl.ds(width, width)] = (dk * cosine[...] - swap_halves(dk) * sine[...]).astype(bf16)
+    c, s = turns(slice(None))
+    qkz[:, pl.ds(0, width)] = (dq * c - swap_halves(dq) * s).astype(bf16)
+    qkz[:, pl.ds(width, width)] = (dk * c - swap_halves(dk) * s).astype(bf16)
     gate = gate_grads[...]
     lane = lax.broadcasted_iota(jnp.int32, (group, width), 1)
     for e in range(experts):
         vgrads[:, pl.ds(e * width, width)] = (gates[:, e : e + 1] * dv).astype(bf16)
         one = jnp.sum(vx[:, pl.ds(e * width, width)].astype(f32) * dv, axis=-1, keepdims=True)
         gate = jnp.where(lane == e, one, gate)
-    qkz[:, pl.ds(2 * width, width)] = (gate * gates * (1.0 - squash[...])).astype(bf16)
+    qkz[:, pl.ds(2 * width, width)] = (gate * gates[...] * (1.0 - gates[...])).astype(bf16)
+
+    scaled_qkz = (qkz[...].astype(f32) * gates[:, width - 1 : width]).astype(bf16)
 
     @pl.loop(0, features // column)
     def _(c):
         at = at_block(c, column)
-        sums[at, pl.ds(0, 3 * width)] = dot(turned[at, :], qkz[...]).astype(bf16)
-        sums[at, pl.ds(3 * width, experts * width)] = dot(rows_t[at, :], vgrads[...]).astype(bf16)
+        sums[at, pl.ds(0, 3 * width)] = dot(turned[at, :], scaled_qkz).astype(bf16)
+        sums[at, pl.ds(3 * width, experts * width)] = dot(turned[at, :], vgrads[...]).astype(bf16)
 
     of_d[0]()
 
     def into_rows(block):
         at = at_block(block, tokens)
-        inverse = inverses[at, 0:1]
+        inverse = gates[at, width - 1 : width]
         unit = rows[at, :].astype(f32) * inverse
         through = dot(qkz[at, :], w_an[...], NT)
         scaled = through * attend_gain
@@ -923,25 +1034,18 @@
         ) + dot(vgrads[at, :], w_v[...], NT)
         return total, jnp.sum(through * unit, axis=0, keepdims=True)
 
+    to_x = chain_sum(8, part, got)
     gain = jnp.zeros((1, features), f32)
-    for step in peers:
-        total, one = into_rows(xor(h, step))
+    for number in range(last):
+        total, one = into_rows(leaving[number])
         gain += one
-        part[at_block(xor(h, step), tokens), :] = total.astype(bf16)
-        back[step] = send_part(8, step)
+        part[at_block(leaving[number], tokens), :] = total.astype(bf16)
+        to_x[0](number)
     total, one = into_rows(h)
     gain_part[...] = jnp.broadcast_to(gain + one, gain_part.shape)
     gain_copies = spread(9, lambda s: gain_part, lambda s: gain_got.at[s - 1])
     grad_x_ref[...] += total
     of_d[1]()
-    of_g[2]()
-
-    small_block = at_block(h, small)
-    blocks[small_block, :] = piece[pl.ds(top + 16, small), :]
-    g_copies = spread(10, lambda s: blocks.at[small_block, :], lambda s: blocks.at[small_block, :])
-    of_o[2]()
-    of_o[3]()
-
     lasts = {}
     for half in range(2):
         toward = 2 - half
@@ -976,6 +1080,21 @@
                 for copy in lasts[half]:
                     copy.start()
 
+    to_x[1](0)
+    of_o[2]()
+    of_o[3]()
+    of_g[2]()
+    small_block = at_block(h, small)
+    blocks[small_block, :] = piece[pl.ds(top + 16, small), :]
+    g_copies = spread(10, lambda s: blocks.at[small_block, :], lambda s: blocks.at[small_block, :])
+    to_x[1](1)
+    to_x[1](2)
+    to_out[0](1)
+    to_out[0](2)
+    of_d[2]()
+    of_d[3]()
+    to_x[2](grad_x_ref)
+    to_out[1](0)
     gain = gain_part[...]
     for step in peers:
         gain_copies[step].wait()
@@ -985,22 +1104,16 @@
     for step in peers:
         g_copies[step].wait()
     of_g[3](blocks, pl.ds(top + 16, n_head * small))
+    of_o[4]()
+    to_out[1](1)
     of_a[1]()
-
-    output = middle[...] + outs[own_block, :].astype(f32)
-    for step in peers:
-        out_copies[step].wait()
-        output += got_out[step - 1].astype(f32)
-    output_ref[...] = output
-    of_d[2]()
-    of_d[3]()
+    to_out[1](2)
     of_a[2]()
     of_a[3]()
-    of_o[4]()
+    of_d[4]()
     of_g[4]()
-    for step in peers:
-        back[step].wait()
-        grad_x_ref[...] += got[step - 1].astype(f32)
+    output_ref[...] = middle[...] + outs[own_block, :].astype(f32)
+    to_out[2](output_ref)
     for half in range(2):
         for copy in lasts[half]:
             copy.wait()
@@ -1014,19 +1127,17 @@
     )
     for store in stores:
         store.start()
-    of_d[4]()
     of_a[4]()
     for one in (of_o, of_g, of_d, of_a):
         one[5]()
     for store in stores:
         store.wait()
-    for step in peers:
-        mr_copies[step].wait_send()
-        da_copies[step].wait_send()
+    mr_end()
+    da_end()
 
 
 def layer_call(n_dp, n_head, args):
-    x, picks, router, value_mat, expert_in = args[0], args[2], args[13], args[11], args[14]
+    x, picks, _, value_mat, expert_in = args[0], args[2], args[12], args[10], args[13]
     tokens, features = x.shape
     per_device, _, width = expert_in.shape
     held_experts = value_mat.shape[1]
@@ -1054,8 +1165,7 @@
         head_picks=vm(args[3].shape, jnp.int32),
         seg=vm((1, group), jnp.int32),
         gains=vm(args[5].shape, f32),
-        cosine=vm((group, width), f32),
-        sine=vm((group, width), f32),
+        angles=vm((group, width), f32),
         w_an=vm((features, 3 * width), bf16),
         w_v=vm((features, held_experts), bf16),
         w_o=vm((held_experts, features), bf16),
@@ -1067,22 +1177,18 @@
         mrs=vm((group, features), bf16),
         das=vm((group, features), bf16),
         turned=vm((features, group), bf16),
-        rows_t=vm((features, group), bf16),
-        inverses=vm((group, width), f32),
         my_mask=vm((n_head, tokens, lanes), bf16),
         all_mask=vm((group, lanes), bf16),
-        gate_mask=vm((group, width), f32),
+        gates=vm((group, width), f32),
         q=vm((group, width), bf16),
         k=vm((group, width), bf16),
         v=vm((group, width), bf16),
         vx=vm((group, held_experts), bf16),
-        squash=vm((group, width), f32),
         att=vm((group, width), f32),
-        middle=vm((tokens, features), f32),
         part=vm((group, features), bf16),
-        got=vm((peers, tokens, features), bf16),
+        got=vm((2 * peers, tokens, features), bf16),
         outs=vm((group, features), bf16),
-        got_out=vm((peers, tokens, features), bf16),
+        got_out=vm((2 * peers, tokens, features), bf16),
         lifted=vm((chips, 2, group, slab), bf16),
         core_out=vm((chips, slab, features), bf16),
         acts=vm((chips, group, 2 * slab), bf16),
@@ -1104,8 +1210,8 @@
         hop_in=vm((2, 2, features // 2, slab), bf16),
         hop_out=vm((2, 2, slab // 2, features), bf16),
         local_sem=dma((15 + 1 + per_device,)),
-        z_send=dma((11, peers)),
-        z_recv=dma((11, peers)),
+        z_send=dma((11, 2 * peers)),
+        z_recv=dma((11, 2 * peers)),
         w_send=dma((22,)),
         w_recv=dma((22,)),
         c_send=dma((3, chips)),
@@ -1121,7 +1227,7 @@
         functools.partial(layer_kernel, n_dp, n_head),
         out_shape=[o[0] for o in outs],
         out_specs=[o[1] for o in outs],
-        in_specs=[ANY] * 16,
+        in_specs=[ANY] * 15,
         scratch_shapes=list(scratch.values()),
         compiler_params=pltpu.CompilerParams(
             collective_id=1, has_side_effects=True, vmem_limit_bytes=vmem_bytes
@@ -1137,6 +1243,7 @@
     wide_ref,
     in_ref,
     out_ref,
+    gain_ref,
     final_ref,
     input_ref,
     attend_ref,
@@ -1156,6 +1263,8 @@
     mix,
     grad_in,
     grad_out,
+    output,
+    grad_x,
     sem,
 ):
     features, slab = in_ref.shape
@@ -1179,14 +1288,19 @@
         copy(out_ref, flat_out, 3),
         copy(wide_ref.at[rest, :], wide.at[rest, :], 4),
     ]
-    stores = [copy(output_ref, final_ref, 5), copy(grad_x_ref, input_ref, 6)]
+    loads += [copy(output_ref, output, 11), copy(grad_x_ref, grad_x, 12)]
+    stores = []
+    for number, (held, result) in enumerate(((output, final_ref), (grad_x, input_ref))):
+        loads[5 + number].wait()
+        stores.append(copy(held, result, 5 + number))
     loads[0].wait()
     first = pl.ds(0, features)
     value[...] = wide[first, pl.ds(3 * width, value.shape[1])].astype(f32)
     stores.append(copy(value, value_ref, 7))
-    query_ref[...] = wide[first, pl.ds(0, width)].astype(f32)
-    key_ref[...] = wide[first, pl.ds(width, width)].astype(f32)
-    gate_ref[...] = wide[first, pl.ds(2 * width, width)][:, :gates].astype(f32)
+    gain = jnp.broadcast_to(gain_ref[0:1, :], (width, features)).T
+    query_ref[...] = wide[first, pl.ds(0, width)].astype(f32) * gain
+    key_ref[...] = wide[first, pl.ds(width, width)].astype(f32) * gain
+    gate_ref[...] = (wide[first, pl.ds(2 * width, width)].astype(f32) * gain)[:, :gates]
     loads[1].wait()
     mix[...] = wide[pl.ds(features, top - features), :].astype(f32)
     stores.append(copy(mix, mix_ref, 8))
@@ -1227,7 +1341,7 @@
         functools.partial(finish_kernel, n_dp, n_head),
         out_shape=[shape(s, f32) for s in shapes],
         out_specs=specs,
-        in_specs=[ANY] * 5,
+        in_specs=[ANY] * 5 + [VM],
         scratch_shapes=[
             pltpu.VMEM(wide.shape, bf16),
             pltpu.VMEM(flat_in.shape, bf16),
@@ -1236,9 +1350,11 @@
             pltpu.VMEM(mix, f32),
             pltpu.VMEM(grad_in, f32),
             pltpu.VMEM(grad_out, f32),
-            pltpu.SemaphoreType.DMA((11,)),
+            pltpu.VMEM(shapes[0], f32),
+            pltpu.VMEM(shapes[1], f32),
+            pltpu.SemaphoreType.DMA((13,)),
         ],
-        compiler_params=pltpu.CompilerParams(vmem_limit_bytes=48 << 20),
+        compiler_params=pltpu.CompilerParams(vmem_limit_bytes=60 << 20),
     )(*args)
 
 
@@ -1267,8 +1383,7 @@
     experts = head_router.shape[2] // 2
     group = tokens * n_head
     angles = np.arange(group)[:, None] * theta ** (-2.0 * np.arange(width // 2) / width)[None, :]
-    cosine = np.concatenate([np.cos(angles)] * 2, axis=1).astype(np.float32)
-    sine = np.concatenate([-np.sin(angles), np.sin(angles)], axis=1).astype(np.float32)
+    angles = np.concatenate([np.cos(angles), np.sin(angles)], axis=1).astype(np.float32)
     head_picks = jnp.concatenate([value_pick[:, 0], output_pick[:, 0] + experts], axis=1)
     gains = jnp.stack([attend_gain, expert_gain]).astype(f32)
     results = layer_call(
@@ -1281,8 +1396,7 @@
             head_picks,
             segments[None, :],
             gains,
-            cosine,
-            sine,
+            angles,
             query_weight[0],
             key_weight[0],
             jnp.pad(head_router[0], ((0, 0), (0, width - 2 * experts))),
@@ -1307,7 +1421,7 @@
         expert_in.shape,
         expert_out.shape,
     )
-    done = list(finish_call(n_dp, n_head, shapes, results))
+    done = list(finish_call(n_dp, n_head, shapes, (*results, gains)))
     for number in (3, 4, 5, 6, 7):
         done[number] = done[number][None]
     done[2], done[8] = done[2][0], done[8][0]

time: 245 us -> 225 us (0.918)
  Pallas kernels: 228 us -> 211 us
    pallas_call x1, Pallas kernels: 222 us -> 202 us  [layer_call(): pl.pallas_call(functools.partial(layer_kernel, n_dp, n_head), out_shape=[...]
    unnamed x13 -> x5, local copies, waits for them, and re-layouts: 9.55 us -> 7.29 us
where the time goes in v5:
time: 225 us
  Pallas kernels  211 us (94%)
  local copies, waits for them, and re-layouts  11 us (5%)
    pallas_call x1, Pallas kernels, layer_call(): pl.pallas_call(functools.partial(layer_kernel, n_dp, n_head), out_shape=[...  202 us
    pallas_call x1, Pallas kernels, finish_call(): pl.pallas_call(functools.partial(finish_kernel, n_dp, n_head), out_shape=...  8.7 us
    unnamed x5, local copies, waits for them, and re-layouts  7.29 us

profile of v5, /device:TPU:0, one launch (start us, length us, event | category | flops | bytes accessed | tf_op | source)
XLA Modules:
  0.0 224.6 jit_solution(11368080050953362107)
XLA Ops:
  0.6 0.7 add_bitcast_fusion
  1.3 0.7 pad_add_fusion
  2.0 0.7 stack.9
  2.7 0.7 stack.10
  3.4 0.6 maximum_convert_fusion.gain_ref
  4.0 1.4 copy.38.pick_ref
  5.4 0.9 copy.39.head_pick_ref
  6.3 0.9 copy.36
  7.2 0.8 pad.8.wg_ref
  8.0 1.1 copy.37
  9.1 0.8 pad.9.router_ref
  9.9 202.2 %shard_map.256 = (f32[128,1024]{1,0:T(8,128)}, f32[128,1024]{1,0:T(8,128)}, bf16[1808,1024]{1,0:T(8,128)(2,1)}, bf16[1024,384]{1,0:T(8,128)(2,1)}, bf16[384,1024]{1,0:T(8,128)(2,1)}) custom-call(bf16[128,1024]{1,0:T(8,128)(2,1)} %x_ref.1, bf16[128,1024]{1,0:T(8,128)(2,1)} %cot_ref.1, s32[128,16]{1,0:T(8,128)} %copy.38.pick_ref, ...), custom_call_target="tpu_custom_call" | custom-call | tf_op jit(solution)/shard_map/pallas_call | solution.py:1226
  212.1 8.7 %shard_map.257 = (f32[128,1024]{1,0:T(8,128)}, f32[128,1024]{1,0:T(8,128)}, f32[1,1024]{1,0:T(1,128)}, f32[1024,128]{1,0:T(8,128)}, f32[1024,128]{1,0:T(8,128)},...) custom-call(f32[128,1024]{1,0:T(8,128)} %get-tuple-element.29.output, ...), custom_call_target="tpu_custom_call" | custom-call | tf_op jit(solution)/shard_map/pallas_call | solution.py:1340
  220.8 1.8 copy.40
  222.6 2.0 copy.41

commit v6 on v5

--- a/solution.py
+++ b/solution.py
@@ -267,7 +267,8 @@
     x_ref,
     cot_ref,
     pick_ref,
-    head_pick_ref,
+    value_pick_ref,
+    output_pick_ref,
     seg_ref,
     gain_ref,
     angle_ref,
@@ -285,7 +286,10 @@
     fin_in_ref,
     fin_out_ref,
     picks,
+    two_picks,
     head_picks,
+    w_g,
+    w_r,
     seg,
     gains,
     angles,
@@ -393,17 +397,18 @@
     for_rows = [
         load(x_ref, rows.at[own_block, :]),
         load(gain_ref, gains),
-        load(wg_ref, w_an.at[:, pl.ds(2 * width, width)]),
+        load(wg_ref, w_g),
         load(wq_ref, w_an.at[:, pl.ds(0, width)]),
         load(wk_ref, w_an.at[:, pl.ds(width, width)]),
         load(wv_ref, w_v),
-        load(head_pick_ref, head_picks),
+        load(value_pick_ref, two_picks.at[0]),
+        load(output_pick_ref, two_picks.at[1]),
         load(angle_ref, angles),
     ]
     for_scores = [load(seg_ref, seg), load(wo_ref, w_o)]
     for_mask = load(pick_ref, picks)
     for_cot = load(cot_ref, cot.at[own_block, :])
-    for_router = load(router_ref, turned.at[:, pl.ds(0, lanes)])
+    for_router = load(router_ref, w_r)
 
     barrier = pltpu.get_barrier_semaphore()
     friends = [along(s) for s in peers] + [partner] + [across(s) for s in range(1, chips)]
@@ -462,6 +467,15 @@
                 def _():
                     go(1, step).start()
 
+        def follow(step):
+            @pl.when((h < last) & (jnp.maximum(h, 1) == step))
+            def _():
+                go(0, 0).start()
+
+            @pl.when((h > 0) & (jnp.maximum(last - h, 1) == step))
+            def _():
+                go(1, 0).start()
+
         def end():
             for step in range(last):
 
@@ -473,7 +487,7 @@
                 def _():
                     go(1, step).wait_send()
 
-        return start, stage, end
+        return start, stage, end, follow
 
     def chain_sum(kind, parts, slots):
         def go(number):
@@ -528,7 +542,7 @@
             copies[step].start()
         return copies
 
-    x_start, x_stage, x_end = gather(0, rows)
+    x_start, x_stage, x_end, _ = gather(0, rows)
     for_rows[0].wait()
     x_start()
 
@@ -558,13 +572,16 @@
         to_core[0, array] = weights(12 + array, slot(array, chip, core), partner)
 
     for_mask.wait()
+    own_picks = jnp.concatenate(
+        [picks[...].astype(f32), jnp.zeros((lanes - picks.shape[0], tokens), f32)], axis=0
+    ).T.astype(jnp.int32)
     lane = lax.broadcasted_iota(jnp.int32, (tokens, lanes), 1)
     for plane in range(n_head):
         expert = (lane // per_device * n_head + plane) * per_device + lane % per_device
         expert = jnp.where(lane < n_dp * per_device, expert, -1)
-        hit = picks[:, 0:1] == expert
-        for c in range(1, picks.shape[1]):
-            hit = hit | (picks[:, c : c + 1] == expert)
+        hit = own_picks[:, 0:1] == expert
+        for c in range(1, picks.shape[0]):
+            hit = hit | (own_picks[:, c : c + 1] == expert)
         my_mask[plane] = jnp.where(hit, 1.0, 0.0).astype(bf16)
     mask_copies = spread(1, lambda s: my_mask.at[xor(h, s)], lambda s: all_mask.at[own_block, :])
     all_mask[own_block, :] = my_mask[h]
@@ -573,6 +590,22 @@
         copy.wait()
     attend_gain = gains[0:1, :]
     expert_gain = gains[1:2, :]
+    one_hot = lambda count: jnp.where(
+        lax.broadcasted_iota(jnp.int32, (count, width), 0)
+        == lax.broadcasted_iota(jnp.int32, (count, width), 1),
+        1.0,
+        0.0,
+    ).astype(bf16)
+    w_an[:, pl.ds(2 * width, width)] = dot(w_g[...], one_hot(w_g.shape[0]), TN).astype(bf16)
+    uses = two_picks.shape[1]
+    head_picks[...] = jnp.concatenate(
+        [
+            two_picks[0].astype(f32),
+            two_picks[1].astype(f32) + experts,
+            jnp.zeros((lanes - 2 * uses, group), f32),
+        ],
+        axis=0,
+    ).T.astype(jnp.int32)
     half_lanes = lax.broadcasted_iota(jnp.int32, (1, width), 1) < width // 2
 
     def turns(at):
@@ -597,7 +630,7 @@
         lane = lax.broadcasted_iota(jnp.int32, (tokens, width), 1)
         chosen = head_picks[at, :]
         hit = lane == chosen[:, 0:1]
-        for c in range(1, chosen.shape[1]):
+        for c in range(1, 2 * uses):
             hit = hit | (lane == chosen[:, c : c + 1])
         gate = jnp.where(hit, jax.nn.sigmoid(qkg[:, 2 * width :]), 0.0)
         gates[at, :] = jnp.where(lane == width - 1, inverse, gate)
@@ -609,12 +642,12 @@
         v[at, :] = value.astype(bf16)
 
     project(h)
+    _, cot_stage, cot_end, cot_follow = gather(2, cot)
+    for_cot.wait()
     for step in (1, 2, 3):
         x_stage(step)
+        cot_follow(step)
         project(arrival[step - 1])
-    cot_start, cot_stage, cot_end = gather(2, cot)
-    for_cot.wait()
-    cot_start()
     for copy in for_scores:
         copy.wait()
     seg_col = gate_grads
@@ -648,8 +681,8 @@
         part[at_block(block, tokens), :] = attend(block).astype(bf16)
         to_mid[0](number)
     middle[...] = rows[own_block, :].astype(f32) + attend(h)
+    cot_stage(1)
     to_mid[1](0)
-    cot_stage(1)
     for half in range(2):
         for array in range(2):
             slabs[1 + half, half, array].wait_recv()
@@ -662,25 +695,27 @@
     to_mid[1](1)
     cot_stage(2)
     to_mid[1](2)
+    cot_stage(3)
     for bit in (1, 2):
         slabs[bit, 2 - bit, 0].wait_recv()
         to_core[bit, 0] = weights(14 + (bit - 1) * 2, slot(0, xor(chip, bit), core), partner)
         slabs[bit, 2 - bit, 1].wait_recv()
         to_core[bit, 1] = weights(15 + (bit - 1) * 2, slot(1, xor(chip, bit), core), partner)
     for_router.wait()
-    slot_of = lax.broadcasted_iota(jnp.int32, (lanes, lanes), 1)
-    name = lax.broadcasted_iota(jnp.int32, (lanes, lanes), 0)
+    slot_of = lax.broadcasted_iota(jnp.int32, (w_r.shape[0], lanes), 1)
+    name = lax.broadcasted_iota(jnp.int32, (w_r.shape[0], lanes), 0)
     expert = (slot_of // per_device * n_head + h) * per_device + slot_of % per_device
     expert = jnp.where(slot_of < n_dp * per_device, expert, -1)
-    my_router[...] = dot(turned[:, pl.ds(0, lanes)], jnp.where(name == expert, 1.0, 0.0).astype(bf16)).astype(bf16)
+    my_router[...] = dot(
+        w_r[...], jnp.where(name == expert, 1.0, 0.0).astype(bf16), TN
+    ).astype(bf16)
 
     to_mid[2](middle)
     mid = middle[...]
     inverse = lax.rsqrt(jnp.mean(mid * mid, axis=-1, keepdims=True) + epsilon)
     mrs[own_block, :] = (mid * inverse * expert_gain).astype(bf16)
-    mr_start, mr_stage, mr_end = gather(4, mrs)
+    mr_start, mr_stage, mr_end, _ = gather(4, mrs)
     mr_start()
-    cot_stage(3)
 
     for array in range(2):
         for half in range(2):
@@ -704,11 +739,14 @@
 
     weights_here(0)
 
-    @pl.loop(0, chips)
-    def _(j):
+    def lift_chip(j):
         lift = dot(cot[...], w_out[j], NT)
         lifted[j, 0] = lift[:, :slab].astype(bf16)
         lifted[j, 1] = lift[:, slab:].astype(bf16)
+
+    pl.loop(0, chips // 2)(lift_chip)
+    mr_stage(1)
+    pl.loop(chips // 2, chips)(lift_chip)
 
     weights_here(1)
 
@@ -768,7 +806,6 @@
 
     near = h // 2
     to_dmr = chain_sum(5, part, got)
-    mr_stage(1)
     pair_of_blocks(near, lambda: mr_stage(2))
     to_dmr[0](2)
     outputs(near)
@@ -811,17 +848,6 @@
 
     pl.semaphore_wait(ready, 1)
 
-    @pl.loop(0, chips)
-    def _(n):
-        expert_grads(xor(chip, chips - 1 - n), other_side)
-        for copy in to_other_core(n):
-            copy.start()
-
-    @pl.loop(0, chips)
-    def _(n):
-        expert_grads(xor(chip, chips - 1 - n), own_side)
-
-    to_dmr[1](0)
     hops = {}
 
     def hop(half, index, place, toward):
@@ -845,21 +871,31 @@
             copy.start()
         hops[half, index] = copies
 
-    for n in range(chips):
-        s = chips - 1 - n
-        place = xor(chip, s)
+    def both_cores(n):
+        step = chips - 1 - n
+        place = xor(chip, step)
         for copy in to_other_core(n):
             copy.wait()
         for half in range(2):
             here = (place, halves_in[half], own_side)
             w_in[here] = w_in[here] + lifted[place, half]
         w_out[place, own_side, :] = w_out[place, own_side, :] + core_out[place]
-        if s == 3:
+        if step == 3:
             hop(0, 1, place, 1)
             hop(1, 1, place, 2)
-        elif s:
-            hop(s - 1, 0, place, s)
-
+        elif step:
+            hop(step - 1, 0, place, step)
+
+    for n in range(chips):
+        place = xor(chip, chips - 1 - n)
+        expert_grads(place, other_side)
+        for copy in to_other_core(n):
+            copy.start()
+        if n:
+            both_cores(n - 1)
+        expert_grads(place, own_side)
+    to_dmr[1](0)
+    both_cores(chips - 1)
     to_dmr[1](1)
     to_dmr[1](2)
     side = features // 2
@@ -948,7 +984,7 @@
     )
     grad_x_ref[...] = dmid
     das[own_block, :] = dmid.astype(bf16)
-    da_start, da_stage, da_end = gather(6, das)
+    da_start, da_stage, da_end, _ = gather(6, das)
     da_start()
     sums[pl.ds(top + 16, small), :] = jnp.concatenate(
         [
@@ -979,16 +1015,19 @@
         gate_grads[at, :] = gate
 
     through_output(h)
+    to_out = chain_sum(7, outs, got_out)
     for step in (1, 2, 3):
         da_stage(step)
+        if step == 1:
+            for number in range(last):
+                to_out[0](number)
         through_output(arrival[step - 1])
-    to_out = chain_sum(7, outs, got_out)
-    to_out[0](0)
 
     for e in range(experts):
         one = (gates[:, experts + e : experts + e + 1] * att[...]).astype(bf16)
         sums[pl.ds(features + e * width, width), :] = dot(one, das[...], TN).astype(bf16)
     of_o[0]()
+    to_out[1](0)
 
     @pl.loop(0, n_head)
     def _(block):
@@ -1002,6 +1041,7 @@
     dk = dot(scores[...], q[...], TN) * scale
     dv = dot(probs[...], datt[...], TN)
     of_o[1]()
+    to_out[1](1)
     c, s = turns(slice(None))
     qkz[:, pl.ds(0, width)] = (dq * c - swap_halves(dq) * s).astype(bf16)
     qkz[:, pl.ds(width, width)] = (dk * c - swap_halves(dk) * s).astype(bf16)
@@ -1023,6 +1063,7 @@
 
     of_d[0]()
 
+    to_out[1](2)
     def into_rows(block):
         at = at_block(block, tokens)
         inverse = gates[at, width - 1 : width]
@@ -1089,12 +1130,9 @@
     g_copies = spread(10, lambda s: blocks.at[small_block, :], lambda s: blocks.at[small_block, :])
     to_x[1](1)
     to_x[1](2)
-    to_out[0](1)
-    to_out[0](2)
     of_d[2]()
     of_d[3]()
     to_x[2](grad_x_ref)
-    to_out[1](0)
     gain = gain_part[...]
     for step in peers:
         gain_copies[step].wait()
@@ -1105,9 +1143,7 @@
         g_copies[step].wait()
     of_g[3](blocks, pl.ds(top + 16, n_head * small))
     of_o[4]()
-    to_out[1](1)
     of_a[1]()
-    to_out[1](2)
     of_a[2]()
     of_a[3]()
     of_d[4]()
@@ -1137,7 +1173,7 @@
 
 
 def layer_call(n_dp, n_head, args):
-    x, picks, _, value_mat, expert_in = args[0], args[2], args[12], args[10], args[13]
+    x, picks, router, value_mat, expert_in = args[0], args[2], args[13], args[11], args[14]
     tokens, features = x.shape
     per_device, _, width = expert_in.shape
     held_experts = value_mat.shape[1]
@@ -1162,9 +1198,12 @@
     ]
     scratch = dict(
         picks=vm(picks.shape, jnp.int32),
-        head_picks=vm(args[3].shape, jnp.int32),
+        two_picks=vm((2, *args[3].shape), jnp.int32),
+        head_picks=vm((group, lanes), jnp.int32),
+        w_g=vm(args[10].shape, bf16),
+        w_r=vm(router.shape, bf16),
         seg=vm((1, group), jnp.int32),
-        gains=vm(args[5].shape, f32),
+        gains=vm(args[6].shape, f32),
         angles=vm((group, width), f32),
         w_an=vm((features, 3 * width), bf16),
         w_v=vm((features, held_experts), bf16),
@@ -1209,7 +1248,7 @@
         blocks=vm((n_head * small, strip), bf16),
         hop_in=vm((2, 2, features // 2, slab), bf16),
         hop_out=vm((2, 2, slab // 2, features), bf16),
-        local_sem=dma((15 + 1 + per_device,)),
+        local_sem=dma((16 + 1 + per_device,)),
         z_send=dma((11, 2 * peers)),
         z_recv=dma((11, 2 * peers)),
         w_send=dma((22,)),
@@ -1227,7 +1266,7 @@
         functools.partial(layer_kernel, n_dp, n_head),
         out_shape=[o[0] for o in outs],
         out_specs=[o[1] for o in outs],
-        in_specs=[ANY] * 15,
+        in_specs=[ANY] * 16,
         scratch_shapes=list(scratch.values()),
         compiler_params=pltpu.CompilerParams(
             collective_id=1, has_side_effects=True, vmem_limit_bytes=vmem_bytes
@@ -1269,8 +1308,7 @@
 ):
     features, slab = in_ref.shape
     per_device, _, width = grad_in_ref.shape
-    experts_total = router_ref.shape[1]
-    gates = gate_ref.shape[1]
+    experts_total, gates = router_ref.shape[0], gate_ref.shape[0]
     top = features + mix_ref.shape[0]
     small = (wide_ref.shape[0] - top - 16) // n_head
     named = n_dp * per_device
@@ -1300,7 +1338,7 @@
     gain = jnp.broadcast_to(gain_ref[0:1, :], (width, features)).T
     query_ref[...] = wide[first, pl.ds(0, width)].astype(f32) * gain
     key_ref[...] = wide[first, pl.ds(width, width)].astype(f32) * gain
-    gate_ref[...] = (wide[first, pl.ds(2 * width, width)].astype(f32) * gain)[:, :gates]
+    gate_ref[...] = (wide[first, pl.ds(2 * width, width)].astype(f32) * gain).T[:gates]
     loads[1].wait()
     mix[...] = wide[pl.ds(features, top - features), :].astype(f32)
     stores.append(copy(mix, mix_ref, 8))
@@ -1320,7 +1358,7 @@
     slot, plane = place % small, place // small
     expert = (slot // per_device * n_head + plane) * per_device + slot % per_device
     chosen = (slot < named) & (expert == name)
-    router_ref[...] = dot(planes, jnp.where(chosen, 1.0, 0.0).astype(bf16), TN)
+    router_ref[...] = dot(jnp.where(chosen, 1.0, 0.0).astype(bf16), planes, TN)
     gain = jnp.zeros((1, features), f32)
     for z in range(n_head):
         row = z * small + ceil_to(named, 8)
@@ -1384,25 +1422,26 @@
     group = tokens * n_head
     angles = np.arange(group)[:, None] * theta ** (-2.0 * np.arange(width // 2) / width)[None, :]
     angles = np.concatenate([np.cos(angles), np.sin(angles)], axis=1).astype(np.float32)
-    head_picks = jnp.concatenate([value_pick[:, 0], output_pick[:, 0] + experts], axis=1)
-    gains = jnp.stack([attend_gain, expert_gain]).astype(f32)
+    both = np.eye(2, dtype=np.float32)
+    gains = attend_gain.astype(f32) * both[:, :1] + expert_gain.astype(f32) * both[:, 1:]
     results = layer_call(
         n_dp,
         n_head,
         (
             hidden_in,
             cotangent,
-            expert_pick,
-            head_picks,
+            expert_pick.T,
+            value_pick.transpose(1, 2, 0)[0],
+            output_pick.transpose(1, 2, 0)[0],
             segments[None, :],
             gains,
             angles,
             query_weight[0],
             key_weight[0],
-            jnp.pad(head_router[0], ((0, 0), (0, width - 2 * experts))),
+            head_router.transpose(0, 2, 1)[0],
             value_weight[0],
             output_weight[0],
-            jnp.pad(router, ((0, 0), (0, width - router.shape[1]))),
+            router.T,
             expert_in,
             expert_out.reshape(per_device * width, features),
         ),
@@ -1415,15 +1454,17 @@
         key_weight.shape[1:],
         value_weight.shape[1:],
         output_weight.shape[1:],
-        head_router.shape[1:],
+        (2 * experts, features),
         (1, features),
-        router.shape,
+        (router.shape[1], features),
         expert_in.shape,
         expert_out.shape,
     )
     done = list(finish_call(n_dp, n_head, shapes, (*results, gains)))
     for number in (3, 4, 5, 6, 7):
         done[number] = done[number][None]
+    done[7] = done[7].transpose(0, 2, 1)
+    done[9] = done[9].T
     done[2], done[8] = done[2][0], done[8][0]
     return tuple(done)
 

time: 225 us -> 210 us (0.933)
  local copies, waits for them, and re-layouts: 11 us -> 1.5 us
  Pallas kernels: 211 us -> 205 us
    pallas_call x1, Pallas kernels: 202 us -> 196 us  [layer_call(): pl.pallas_call(functools.partial(layer_kernel, n_dp, n_head), out_shape=[...]
    unnamed x5 -> x1, local copies, waits for them, and re-layouts: 7.29 us -> 1.5 us
where the time goes in v6:
time: 210 us
  Pallas kernels  205 us (98%)
  other arithmetic  2.69 us (1%)
    pallas_call x1, Pallas kernels, layer_call(): pl.pallas_call(functools.partial(layer_kernel, n_dp, n_head), out_shape=[...  196 us
    pallas_call x1, Pallas kernels, finish_call(): pl.pallas_call(functools.partial(finish_kernel, n_dp, n_head), out_shape=...  8.46 us

profile of v6, /device:TPU:0, one launch (start us, length us, event | category | flops | bytes accessed | tf_op | source)
XLA Modules:
  0.0 209.6 jit_solution(18027267829668783189)
XLA Ops:
  0.6 0.7 convert_element_type.6
  1.3 0.7 convert_element_type.7
  2.0 1.3 fusion.gain_ref
  3.3 196.3 %shard_map.274 = (f32[128,1024]{1,0:T(8,128)}, f32[128,1024]{1,0:T(8,128)}, bf16[1808,1024]{1,0:T(8,128)(2,1)}, bf16[1024,384]{1,0:T(8,128)(2,1)}, bf16[384,1024]{1,0:T(8,128)(2,1)}) custom-call(bf16[128,1024]{1,0:T(8,128)(2,1)} %x_ref.1, bf16[128,1024]{1,0:T(8,128)(2,1)} %cot_ref.1, s32[16,128]{1,0:T(8,128)} %bitcast.35, s32[2,512]{1,0:T(2,128)} %bitcast.36, ...), custom_call_target="tpu_custom_call" | custom-call | tf_op jit(solution)/shard_map/pallas_call | solution.py:1265
  199.7 8.5 %shard_map.275 = (f32[128,1024]{1,0:T(8,128)}, f32[128,1024]{1,0:T(8,128)}, f32[1,1024]{1,0:T(1,128)}, f32[1024,128]{1,0:T(8,128)}, f32[1024,128]{1,0:T(8,128)},...) custom-call(f32[128,1024]{1,0:T(8,128)} %get-tuple-element.29.output, ...), custom_call_target="tpu_custom_call" | custom-call | tf_op jit(solution)/shard_map/pallas_call | solution.py:1378
  208.1 1.5 copy.31

commit v7 on v6

--- a/solution.py
+++ b/solution.py
@@ -431,61 +431,57 @@
     def gather(kind, buffer):
         def go(side, step):
             block = jnp.clip(h - step if side == 0 else h + step, 0, last)
-            here = buffer.at[at_block(block, tokens), :]
-            number = side * last + step
-            return remote(
-                here, here, z_send.at[kind, number], z_recv.at[kind, number], (right, left)[side]
-            )
+            copies = []
+            for half in range(2):
+                here = buffer.at[at_block(2 * block + half, tokens // 2), :]
+                number = (side * last + step) * 2 + half
+                copies.append(
+                    remote(
+                        here, here, z_send.at[kind, number], z_recv.at[kind, number], (right, left)[side]
+                    )
+                )
+            return copies
+
+        def begin(side):
+            for copy in go(side, 0):
+                copy.start()
 
         def start():
-            @pl.when(h < last)
-            def _():
-                go(0, 0).start()
-
-            @pl.when(h > 0)
-            def _():
-                go(1, 0).start()
+            pl.when(h < last)(lambda: begin(0))
+            pl.when(h > 0)(lambda: begin(1))
+
+        def pass_on(side, step, there, onward):
+            for half in range(2):
+
+                @pl.when(there)
+                def _():
+                    go(side, step - 1)[half].wait_recv()
+
+                if step < last:
+
+                    @pl.when(there & onward)
+                    def _():
+                        go(side, step)[half].start()
 
         def stage(step):
-            @pl.when(h >= step)
-            def _():
-                go(0, step - 1).wait_recv()
-
-            if step < last:
-
-                @pl.when((h >= step) & (h < last))
-                def _():
-                    go(0, step).start()
-
-            @pl.when(h + step <= last)
-            def _():
-                go(1, step - 1).wait_recv()
-
-            if step < last:
-
-                @pl.when((h + step <= last) & (h > 0))
-                def _():
-                    go(1, step).start()
+            pass_on(0, step, h >= step, h < last)
+            pass_on(1, step, h + step <= last, h > 0)
 
         def follow(step):
-            @pl.when((h < last) & (jnp.maximum(h, 1) == step))
-            def _():
-                go(0, 0).start()
-
-            @pl.when((h > 0) & (jnp.maximum(last - h, 1) == step))
-            def _():
-                go(1, 0).start()
+            pl.when((h < last) & (jnp.maximum(h, 1) == step))(lambda: begin(0))
+            pl.when((h > 0) & (jnp.maximum(last - h, 1) == step))(lambda: begin(1))
 
         def end():
             for step in range(last):
-
-                @pl.when((h >= step) & (h < last))
-                def _():
-                    go(0, step).wait_send()
-
-                @pl.when((h + step <= last) & (h > 0))
-                def _():
-                    go(1, step).wait_send()
+                for side, sent in (
+                    (0, (h >= step) & (h < last)),
+                    (1, (h + step <= last) & (h > 0)),
+                ):
+
+                    @pl.when(sent)
+                    def _():
+                        for copy in go(side, step):
+                            copy.wait_send()
 
         return start, stage, end, follow
 
@@ -495,41 +491,59 @@
             rightward = block > h
             slot = jnp.where(rightward, block - 1, last + block)
             where = (d, jnp.clip(jnp.where(rightward, h + 1, h - 1), 0, last))
-            at = at_block(block, tokens)
-            copy = remote(
-                parts.at[at, :], slots.at[slot], z_send.at[kind, number], z_recv.at[kind, slot], where
-            )
             middle_one = (rightward & (h > 0)) | (jnp.logical_not(rightward) & (h < last))
-            return copy, middle_one, at, slot
+            pieces = []
+            for half in range(2):
+                at = at_block(2 * block + half, tokens // 2)
+                rows_of = pl.ds(half * (tokens // 2), tokens // 2)
+                copy = remote(
+                    parts.at[at, :],
+                    slots.at[slot, rows_of, :],
+                    z_send.at[kind, 2 * number + half],
+                    z_recv.at[kind, 2 * slot + half],
+                    where,
+                )
+                pieces.append((copy, at, slot, rows_of))
+            return pieces, middle_one
 
         def now(number):
-            copy, middle_one, _, _ = go(number)
+            pieces, middle_one = go(number)
 
             @pl.when(jnp.logical_not(middle_one))
             def _():
-                copy.start()
+                for copy, _, _, _ in pieces:
+                    copy.start()
 
         def later(number):
-            copy, middle_one, at, slot = go(number)
+            pieces, middle_one = go(number)
 
             @pl.when(middle_one)
             def _():
-                copy.wait_recv()
-                parts[at, :] = parts[at, :] + slots[slot]
-                copy.start()
+                for copy, at, slot, rows_of in pieces:
+                    copy.wait_recv()
+                    parts[at, :] = parts[at, :] + slots[slot, rows_of, :]
+                    copy.start()
 
         def end(total):
-            for slot, there in ((jnp.maximum(h - 1, 0), h > 0), (last + jnp.minimum(h, last - 1), h < last)):
+            ends = ((jnp.maximum(h - 1, 0), h > 0), (last + jnp.minimum(h, last - 1), h < last))
+            for slot, there in ends:
 
                 @pl.when(there)
                 def _():
-                    remote(
-                        parts.at[own_block, :], slots.at[slot], z_send.at[kind, 0], z_recv.at[kind, slot], right
-                    ).wait_recv()
+                    for half in range(2):
+                        rows_of = pl.ds(half * (tokens // 2), tokens // 2)
+                        remote(
+                            parts.at[at_block(2 * h, tokens // 2), :],
+                            slots.at[slot, rows_of, :],
+                            z_send.at[kind, 0],
+                            z_recv.at[kind, 2 * slot + half],
+                            right,
+                        ).wait_recv()
                     total[...] += slots[slot].astype(f32)
 
             for number in range(last):
-                go(number)[0].wait_send()
+                for copy, _, _, _ in go(number)[0]:
+                    copy.wait_send()
 
         return now, later, end
 
@@ -683,8 +697,8 @@
     middle[...] = rows[own_block, :].astype(f32) + attend(h)
     cot_stage(1)
     to_mid[1](0)
-    for half in range(2):
-        for array in range(2):
+    for array in range(2):
+        for half in range(2):
             slabs[1 + half, half, array].wait_recv()
             halves_on[half, array] = weights(
                 8 + 2 * half + array,
@@ -717,12 +731,14 @@
     mr_start, mr_stage, mr_end, _ = gather(4, mrs)
     mr_start()
 
-    for array in range(2):
+    def last_halves(array):
         for half in range(2):
             halves_on[half, array].wait_recv()
             diagonal[half, array] = weights(
                 18 + 2 * half + array, slot(array, xor(chip, 3), core, half), partner
             )
+
+    last_halves(0)
     for step in peers:
         mask_copies[step].wait()
     cot_end()
@@ -730,12 +746,19 @@
 
     def weights_here(array):
         for bit in range(3):
-            to_core[bit, array].wait()
+            to_core[bit, array].wait_recv()
         for half in range(2):
-            diagonal[half, array].wait()
-            halves_on[half, array].wait_send()
-            for bit in (1, 2):
-                slabs[bit, half, array].wait_send()
+            diagonal[half, array].wait_recv()
+
+    def weights_sent():
+        for array in range(2):
+            for bit in range(3):
+                to_core[bit, array].wait_send()
+            for half in range(2):
+                diagonal[half, array].wait_send()
+                halves_on[half, array].wait_send()
+                for bit in (1, 2):
+                    slabs[bit, half, array].wait_send()
 
     weights_here(0)
 
@@ -746,6 +769,7 @@
 
     pl.loop(0, chips // 2)(lift_chip)
     mr_stage(1)
+    last_halves(1)
     pl.loop(chips // 2, chips)(lift_chip)
 
     weights_here(1)
@@ -760,15 +784,13 @@
         own = mrs[at, :]
         gates = jax.nn.sigmoid(dot(own, my_router[...]))
         live = gates * all_mask[at, :].astype(f32)
-        high = live.astype(bf16)
-        low = (live - high.astype(f32)).astype(bf16)
-        both = jnp.concatenate([high, low], axis=-1)
+        narrow = live.astype(bf16)
 
         def chip_step(j, total):
             pick = spread_lanes(j)
             hidden = dot(own, w_in[j])
-            gate = dot(both, jnp.concatenate([pick, pick], axis=0))
-            lift = jnp.concatenate([lifted[j, 0, at, :], lifted[j, 1, at, :]], axis=-1).astype(f32)
+            gate = dot(narrow, pick).astype(bf16)
+            lift = jnp.concatenate([lifted[j, 0, at, :], lifted[j, 1, at, :]], axis=-1)
             square = hidden * hidden
             inner = jnp.tanh(0.7978845608028654 * hidden * (1.0 + 0.044715 * square))
             half = 0.5 * (1.0 + inner)
@@ -776,9 +798,10 @@
             slope = half + act * (1.0 - inner) * (
                 0.7978845608028654 + (0.7978845608028654 * 3.0 * 0.044715) * square
             )
-            acts[j, at, :] = (act * gate).astype(bf16)
-            hids[j, at, :] = (slope * (lift * gate)).astype(bf16)
-            return total + dot((act * lift).astype(bf16), pick, NT)
+            act = act.astype(bf16)
+            acts[j, at, :] = act * gate
+            hids[j, at, :] = slope.astype(bf16) * (lift * gate)
+            return total + dot(act * lift, pick, NT)
 
         total = lax.fori_loop(0, chips, chip_step, jnp.zeros((pair, lanes), f32))
         dz = (total * live * (1.0 - gates)).astype(bf16)
@@ -793,29 +816,27 @@
                 total += dot(hids[j, at, :], w_in[j, part_of, :], NT)
             part[at, part_of] = total.astype(bf16)
 
-    def outputs(number):
-        at = at_block(number, pair)
-
+    def outputs():
         @pl.loop(0, features // column)
         def _(c):
             part_of = at_block(c, column)
-            total = dot(acts[0, at, :], w_out[0, :, part_of])
+            total = dot(acts[0], w_out[0, :, part_of])
             for j in range(1, chips):
-                total += dot(acts[j, at, :], w_out[j, :, part_of])
-            outs[at, part_of] = total.astype(bf16)
+                total += dot(acts[j], w_out[j, :, part_of])
+            outs[:, part_of] = total.astype(bf16)
 
     near = h // 2
     to_dmr = chain_sum(5, part, got)
     pair_of_blocks(near, lambda: mr_stage(2))
     to_dmr[0](2)
-    outputs(near)
     mr_stage(3)
     pair_of_blocks(1 - near, lambda: None)
     to_dmr[0](0)
     to_dmr[0](1)
-    outputs(1 - near)
+    outputs()
     pl.semaphore_signal(ready, inc=1, device_id=partner, device_id_type=MESH)
 
+    weights_sent()
     turned[...] = mrs[...].T
 
     def expert_grads(place, at):
@@ -900,10 +921,10 @@
     to_dmr[1](2)
     side = features // 2
     strip = side // chips
+    col = lambda c, j: at_block(c * chips + j, strip)
 
     def section(number, first, count):
         at = pl.ds(first, count)
-        col = lambda c, j: at_block(c * chips + j, strip)
         state = {}
 
         def sem(n):
@@ -935,26 +956,28 @@
                 total += chip_got[s - 1, at, :].astype(f32)
             piece[at, :] = total.astype(bf16)
 
-        def share(src=None, rows_to=at):
-            src = piece.at[at, :] if src is None else src
-            state["rows"] = rows_to
+        return start, mid, add
+
+    def to_plane(number, src, rows_to):
+        state = {}
+
+        def sem(n):
+            return s_send.at[number, chips + n], s_recv.at[number, chips + n]
+
+        def start():
             here = wide_ref.at[rows_to, col(core, chip)]
-            state["share"] = []
-            for s in range(1, chips):
-                copy = remote(src, here, *sem(chips + s), across(s))
+            state["share"] = [remote(src, here, *sem(s), across(s)) for s in range(1, chips)]
+            over = remote(src, here, *sem(0), partner)
+            own = pltpu.make_async_copy(src, here, s_send.at[number, 3 * chips - 1])
+            state["wait"] = [over, own]
+            for copy in state["share"] + state["wait"]:
                 copy.start()
-                state["share"].append(copy)
-            over = remote(src, here, *sem(chips), partner)
-            own = pltpu.make_async_copy(src, here, s_send.at[number, 3 * chips - 1])
-            over.start()
-            own.start()
-            state["wait"] = [over, own]
 
         def forward():
             for s in range(1, chips):
                 state["share"][s - 1].wait()
-                here = wide_ref.at[state["rows"], col(core, xor(chip, s))]
-                copy = remote(here, here, *sem(2 * chips - 1 + s), partner)
+                here = wide_ref.at[rows_to, col(core, xor(chip, s))]
+                copy = remote(here, here, *sem(chips - 1 + s), partner)
                 copy.start()
                 state["wait"].append(copy)
 
@@ -962,14 +985,21 @@
             for copy in state["wait"]:
                 copy.wait()
 
-        return start, mid, add, share, forward, end
-
-    top = features + w_o.shape[0]
+        return start, forward, end
+
+    mixed = w_o.shape[0]
     small = ceil_to(named + 1, 16)
-    of_o = section(0, features, w_o.shape[0])
-    of_d = section(1, 0, features)
-    of_g = section(2, top + 16, small)
-    of_a = section(3, top, 16)
+    at_a = pl.ds(features, 16)
+    at_o = pl.ds(features + 16, mixed)
+    at_g = pl.ds(features + 16 + mixed, small)
+    of_d = [section(n, n * features // 2, features // 2) for n in range(2)]
+    of_o = section(2, features + 16, mixed)
+    of_g = section(3, features + 16 + mixed, small)
+    of_a = section(4, features, 16)
+    out_d = [to_plane(n, piece.at[halves_in[n], :], halves_in[n]) for n in range(2)]
+    out_o = to_plane(2, piece.at[at_o, :], at_o)
+    out_g = to_plane(3, blocks, pl.ds(features + 16 + mixed, n_head * small))
+    out_a = to_plane(4, piece.at[at_a, :], at_a)
     router_part = dot(dzs[...], mrs[...], TN)[:named]
 
     grad_x_ref[...] = part[own_block, :].astype(f32)
@@ -986,7 +1016,7 @@
     das[own_block, :] = dmid.astype(bf16)
     da_start, da_stage, da_end, _ = gather(6, das)
     da_start()
-    sums[pl.ds(top + 16, small), :] = jnp.concatenate(
+    sums[at_g, :] = jnp.concatenate(
         [
             router_part,
             jnp.sum(incoming * unit, axis=0, keepdims=True),
@@ -997,6 +1027,40 @@
     of_g[0]()
     turned[...] = rows[...].T
     of_g[1]()
+    lasts = {}
+
+    def first_hop(half, index, place):
+        for copy in hops[half, index]:
+            copy.wait()
+        at_in = (place, halves_in[half], own_side)
+        at_out = (place, halves_out(core)[half], slice(None))
+        w_in[at_in] = w_in[at_in] + hop_in[half, index]
+        w_out[at_out] = w_out[at_out] + hop_out[half, index]
+
+    for half in range(2):
+        toward = 2 - half
+        place = xor(chip, toward)
+        first_hop(half, 1, place)
+        pl.semaphore_signal(free.at[half], inc=1, device_id=across(toward), device_id_type=MESH)
+        pl.semaphore_wait(free.at[half], 1)
+        lasts[half] = (
+            remote(
+                slot(1, place, core, half),
+                hop_in.at[half, 1],
+                e_send.at[0, 4 + half],
+                e_recv.at[0, 4 + half],
+                across(toward),
+            ),
+            remote(
+                slot(0, place, core, half),
+                hop_out.at[half, 1],
+                e_send.at[1, 4 + half],
+                e_recv.at[1, 4 + half],
+                across(toward),
+            ),
+        )
+        for copy in lasts[half]:
+            copy.start()
     lane = lax.broadcasted_iota(jnp.int32, (tokens, width), 1)
 
     def through_output(block):
@@ -1025,9 +1089,8 @@
 
     for e in range(experts):
         one = (gates[:, experts + e : experts + e + 1] * att[...]).astype(bf16)
-        sums[pl.ds(features + e * width, width), :] = dot(one, das[...], TN).astype(bf16)
+        sums[pl.ds(features + 16 + e * width, width), :] = dot(one, das[...], TN).astype(bf16)
     of_o[0]()
-    to_out[1](0)
 
     @pl.loop(0, n_head)
     def _(block):
@@ -1041,7 +1104,6 @@
     dk = dot(scores[...], q[...], TN) * scale
     dv = dot(probs[...], datt[...], TN)
     of_o[1]()
-    to_out[1](1)
     c, s = turns(slice(None))
     qkz[:, pl.ds(0, width)] = (dq * c - swap_halves(dq) * s).astype(bf16)
     qkz[:, pl.ds(width, width)] = (dk * c - swap_halves(dk) * s).astype(bf16)
@@ -1055,15 +1117,15 @@
 
     scaled_qkz = (qkz[...].astype(f32) * gates[:, width - 1 : width]).astype(bf16)
 
-    @pl.loop(0, features // column)
-    def _(c):
+    def matrix_rows(c):
         at = at_block(c, column)
         sums[at, pl.ds(0, 3 * width)] = dot(turned[at, :], scaled_qkz).astype(bf16)
         sums[at, pl.ds(3 * width, experts * width)] = dot(turned[at, :], vgrads[...]).astype(bf16)
 
-    of_d[0]()
-
-    to_out[1](2)
+    steps_each = features // column // 2
+    for n in range(2):
+        pl.loop(n * steps_each, (n + 1) * steps_each)(matrix_rows)
+        of_d[n][0]()
     def into_rows(block):
         at = at_block(block, tokens)
         inverse = gates[at, width - 1 : width]
@@ -1082,75 +1144,46 @@
         gain += one
         part[at_block(leaving[number], tokens), :] = total.astype(bf16)
         to_x[0](number)
+        if number < 2:
+            of_d[number][1]()
     total, one = into_rows(h)
-    gain_part[...] = jnp.broadcast_to(gain + one, gain_part.shape)
-    gain_copies = spread(9, lambda s: gain_part, lambda s: gain_got.at[s - 1])
+    sums[at_a, :] = jnp.broadcast_to(gain + one, (16, features)).astype(bf16)
+    of_a[0]()
     grad_x_ref[...] += total
-    of_d[1]()
-    lasts = {}
-    for half in range(2):
-        toward = 2 - half
-        for index, place in ((1, xor(chip, toward)), (0, chip)):
-            for copy in hops[half, index]:
-                copy.wait()
-            at_in = (place, halves_in[half], own_side)
-            at_out = (place, halves_out(core)[half], slice(None))
-            w_in[at_in] = w_in[at_in] + hop_in[half, index]
-            w_out[at_out] = w_out[at_out] + hop_out[half, index]
-            if index:
-                pl.semaphore_signal(
-                    free.at[half], inc=1, device_id=across(toward), device_id_type=MESH
-                )
-                pl.semaphore_wait(free.at[half], 1)
-                lasts[half] = (
-                    remote(
-                        w_in.at[at_in],
-                        hop_in.at[half, 1],
-                        e_send.at[0, 4 + half],
-                        e_recv.at[0, 4 + half],
-                        across(toward),
-                    ),
-                    remote(
-                        w_out.at[at_out],
-                        hop_out.at[half, 1],
-                        e_send.at[1, 4 + half],
-                        e_recv.at[1, 4 + half],
-                        across(toward),
-                    ),
-                )
-                for copy in lasts[half]:
-                    copy.start()
-
-    to_x[1](0)
-    of_o[2]()
-    of_o[3]()
+    to_out[1](0)
+    to_out[1](1)
+    of_a[1]()
     of_g[2]()
     small_block = at_block(h, small)
-    blocks[small_block, :] = piece[pl.ds(top + 16, small), :]
-    g_copies = spread(10, lambda s: blocks.at[small_block, :], lambda s: blocks.at[small_block, :])
+    blocks[small_block, :] = piece[at_g, :]
+    g_copies = spread(9, lambda s: blocks.at[small_block, :], lambda s: blocks.at[small_block, :])
+    to_x[1](0)
+    to_out[1](2)
+    of_o[2]()
+    out_o[0]()
     to_x[1](1)
     to_x[1](2)
-    of_d[2]()
-    of_d[3]()
-    to_x[2](grad_x_ref)
-    gain = gain_part[...]
+    of_d[0][2]()
+    out_d[0][0]()
+    of_a[2]()
+    gain_part[...] = piece[at_a, :]
+    gain_copies = spread(10, lambda s: gain_part, lambda s: gain_got.at[s - 1])
+    of_d[1][2]()
+    out_d[1][0]()
+    for step in peers:
+        g_copies[step].wait()
+    out_g[0]()
+    gain = gain_part[...].astype(f32)
     for step in peers:
         gain_copies[step].wait()
-        gain += gain_got[step - 1]
-    sums[pl.ds(top, 16), :] = jnp.concatenate([gain, gain], axis=0).astype(bf16)
-    of_a[0]()
-    for step in peers:
-        g_copies[step].wait()
-    of_g[3](blocks, pl.ds(top + 16, n_head * small))
-    of_o[4]()
-    of_a[1]()
-    of_a[2]()
-    of_a[3]()
-    of_d[4]()
-    of_g[4]()
+        gain += gain_got[step - 1].astype(f32)
+    piece[at_a, :] = gain.astype(bf16)
+    out_a[0]()
+    to_x[2](grad_x_ref)
     output_ref[...] = middle[...] + outs[own_block, :].astype(f32)
     to_out[2](output_ref)
     for half in range(2):
+        first_hop(half, 0, chip)
         for copy in lasts[half]:
             copy.wait()
         at_in = (chip, halves_in[half], own_side)
@@ -1163,9 +1196,10 @@
     )
     for store in stores:
         store.start()
-    of_a[4]()
-    for one in (of_o, of_g, of_d, of_a):
-        one[5]()
+    for one in (out_o, out_d[0], out_g, out_a, out_d[1]):
+        one[1]()
+    for one in (out_o, out_d[0], out_g, out_a, out_d[1]):
+        one[2]()
     for store in stores:
         store.wait()
     mr_end()
@@ -1239,8 +1273,8 @@
         scores=vm((group, group), bf16),
         qkz=vm((group, 3 * width), bf16),
         vgrads=vm((group, held_experts), bf16),
-        gain_part=vm((8, features), f32),
-        gain_got=vm((peers, 8, features), f32),
+        gain_part=vm((16, strip), bf16),
+        gain_got=vm((peers, 16, strip), bf16),
         sums=vm((held, features), bf16),
         core_got=vm((held, features // 2), bf16),
         chip_got=vm((chips - 1, held, strip), bf16),
@@ -1249,16 +1283,16 @@
         hop_in=vm((2, 2, features // 2, slab), bf16),
         hop_out=vm((2, 2, slab // 2, features), bf16),
         local_sem=dma((16 + 1 + per_device,)),
-        z_send=dma((11, 2 * peers)),
-        z_recv=dma((11, 2 * peers)),
+        z_send=dma((11, 4 * peers)),
+        z_recv=dma((11, 4 * peers)),
         w_send=dma((22,)),
         w_recv=dma((22,)),
         c_send=dma((3, chips)),
         c_recv=dma((3, chips)),
         e_send=dma((2, 6)),
         e_recv=dma((2, 6)),
-        s_send=dma((4, 3 * chips)),
-        s_recv=dma((4, 3 * chips)),
+        s_send=dma((5, 3 * chips)),
+        s_recv=dma((5, 3 * chips)),
         ready=pltpu.SemaphoreType.REGULAR,
         free=pltpu.SemaphoreType.REGULAR((2,)),
     )
@@ -1309,8 +1343,9 @@
     features, slab = in_ref.shape
     per_device, _, width = grad_in_ref.shape
     experts_total, gates = router_ref.shape[0], gate_ref.shape[0]
-    top = features + mix_ref.shape[0]
-    small = (wide_ref.shape[0] - top - 16) // n_head
+    mixed = mix_ref.shape[0]
+    top = features + 16 + mixed
+    small = (wide_ref.shape[0] - top) // n_head
     named = n_dp * per_device
 
     def copy(src, dst, number):
@@ -1340,7 +1375,7 @@
     key_ref[...] = wide[first, pl.ds(width, width)].astype(f32) * gain
     gate_ref[...] = (wide[first, pl.ds(2 * width, width)].astype(f32) * gain).T[:gates]
     loads[1].wait()
-    mix[...] = wide[pl.ds(features, top - features), :].astype(f32)
+    mix[...] = wide[pl.ds(features + 16, mixed), :].astype(f32)
     stores.append(copy(mix, mix_ref, 8))
     loads[2].wait()
     for e in range(per_device):
@@ -1351,8 +1386,8 @@
         grad_out[e] = flat_out[pl.ds(e * width, width), :].astype(f32)
     stores.append(copy(grad_out, grad_out_ref, 10))
     loads[4].wait()
-    attend_ref[...] = wide[pl.ds(top, 16), :][0:1].astype(f32)
-    planes = wide[pl.ds(top + 16, n_head * small), :]
+    attend_ref[...] = wide[pl.ds(features, 16), :][0:1].astype(f32)
+    planes = wide[pl.ds(top, n_head * small), :]
     place = lax.broadcasted_iota(jnp.int32, (n_head * small, experts_total), 0)
     name = lax.broadcasted_iota(jnp.int32, (n_head * small, experts_total), 1)
     slot, plane = place % small, place // small

time: 210 us -> 201 us (0.957)
  Pallas kernels: 205 us -> 196 us
    pallas_call x1, Pallas kernels: 196 us -> 188 us  [layer_call(): pl.pallas_call(functools.partial(layer_kernel, n_dp, n_head), out_shape=[...]
where the time goes in v7:
time: 201 us
  Pallas kernels  196 us (98%)
  other arithmetic  2.69 us (1%)
    pallas_call x1, Pallas kernels, layer_call(): pl.pallas_call(functools.partial(layer_kernel, n_dp, n_head), out_shape=[...  188 us
    pallas_call x1, Pallas kernels, finish_call(): pl.pallas_call(functools.partial(finish_kernel, n_dp, n_head), out_shape=...  8.46 us

profile of v7, /device:TPU:0, one launch (start us, length us, event | category | flops | bytes accessed | tf_op | source)
XLA Modules:
  0.0 200.9 jit_solution(6382157901027239632)
XLA Ops:
  0.6 0.7 convert_element_type.6
  1.3 0.7 convert_element_type.7
  2.0 1.3 fusion.gain_ref
  3.3 187.6 %shard_map.274 = (f32[128,1024]{1,0:T(8,128)}, f32[128,1024]{1,0:T(8,128)}, bf16[1808,1024]{1,0:T(8,128)(2,1)}, bf16[1024,384]{1,0:T(8,128)(2,1)}, bf16[384,1024]{1,0:T(8,128)(2,1)}) custom-call(bf16[128,1024]{1,0:T(8,128)(2,1)} %x_ref.1, bf16[128,1024]{1,0:T(8,128)(2,1)} %cot_ref.1, s32[16,128]{1,0:T(8,128)} %bitcast.35, s32[2,512]{1,0:T(2,128)} %bitcast.36, ...), custom_call_target="tpu_custom_call" | custom-call | tf_op jit(solution)/shard_map/pallas_call | solution.py:1299
  191.0 8.5 %shard_map.275 = (f32[128,1024]{1,0:T(8,128)}, f32[128,1024]{1,0:T(8,128)}, f32[1,1024]{1,0:T(1,128)}, f32[1024,128]{1,0:T(8,128)}, f32[1024,128]{1,0:T(8,128)},...) custom-call(f32[128,1024]{1,0:T(8,128)} %get-tuple-element.29.output, ...), custom_call_target="tpu_custom_call" | custom-call | tf_op jit(solution)/shard_map/pallas_call | solution.py:1413
  199.4 1.5 copy.31

commit v8 on v7

--- a/solution.py
+++ b/solution.py
@@ -347,6 +347,8 @@
     e_recv,
     s_send,
     s_recv,
+    t_send,
+    t_recv,
     ready,
     free,
 ):
@@ -450,22 +452,24 @@
             pl.when(h < last)(lambda: begin(0))
             pl.when(h > 0)(lambda: begin(1))
 
-        def pass_on(side, step, there, onward):
+        def arrive(side, step, there, onward):
             for half in range(2):
 
                 @pl.when(there)
                 def _():
                     go(side, step - 1)[half].wait_recv()
-
-                if step < last:
-
-                    @pl.when(there & onward)
-                    def _():
+                    if onward:
                         go(side, step)[half].start()
 
-        def stage(step):
-            pass_on(0, step, h >= step, h < last)
-            pass_on(1, step, h + step <= last, h > 0)
+        def stage(step, which="all"):
+            ways = ((0, h >= step, h < last), (1, h + step <= last, h > 0))
+            for side, there, onward in ways:
+                if step < last and which != "rest":
+                    arrive(side, step, there & onward, True)
+            for side, there, onward in ways:
+                if which != "duty":
+                    ends_here = there if step == last else there & jnp.logical_not(onward)
+                    arrive(side, step, ends_here, False)
 
         def follow(step):
             pl.when((h < last) & (jnp.maximum(h, 1) == step))(lambda: begin(0))
@@ -695,7 +699,7 @@
         part[at_block(block, tokens), :] = attend(block).astype(bf16)
         to_mid[0](number)
     middle[...] = rows[own_block, :].astype(f32) + attend(h)
-    cot_stage(1)
+    cot_stage(1, "duty")
     to_mid[1](0)
     for array in range(2):
         for half in range(2):
@@ -707,9 +711,8 @@
             )
 
     to_mid[1](1)
-    cot_stage(2)
+    cot_stage(2, "duty")
     to_mid[1](2)
-    cot_stage(3)
     for bit in (1, 2):
         slabs[bit, 2 - bit, 0].wait_recv()
         to_core[bit, 0] = weights(14 + (bit - 1) * 2, slot(0, xor(chip, bit), core), partner)
@@ -738,6 +741,8 @@
                 18 + 2 * half + array, slot(array, xor(chip, 3), core, half), partner
             )
 
+    for step in (1, 2, 3):
+        cot_stage(step, "rest")
     last_halves(0)
     for step in peers:
         mask_copies[step].wait()
@@ -768,8 +773,8 @@
         lifted[j, 1] = lift[:, slab:].astype(bf16)
 
     pl.loop(0, chips // 2)(lift_chip)
+    last_halves(1)
     mr_stage(1)
-    last_halves(1)
     pl.loop(chips // 2, chips)(lift_chip)
 
     weights_here(1)
@@ -827,8 +832,9 @@
 
     near = h // 2
     to_dmr = chain_sum(5, part, got)
-    pair_of_blocks(near, lambda: mr_stage(2))
+    pair_of_blocks(near, lambda: mr_stage(2, "duty"))
     to_dmr[0](2)
+    mr_stage(2, "rest")
     mr_stage(3)
     pair_of_blocks(1 - near, lambda: None)
     to_dmr[0](0)
@@ -958,6 +964,122 @@
 
         return start, mid, add
 
+    def two_hop_section(number, first, count):
+        at = pl.ds(first, count)
+        half_at = [pl.ds(first + n * (count // 2), count // 2) for n in range(2)]
+        begin, state = section(number, first, count)[0], {}
+
+        def hop(half, index, place, toward, n):
+            copy = remote(
+                sums.at[half_at[half], col(core, place)],
+                chip_got.at[index, half_at[half], :],
+                t_send.at[number, n],
+                t_recv.at[number, n],
+                across(toward),
+            )
+            copy.start()
+            return copy
+
+        def mid():
+            over = remote(
+                sums.at[at, at_block(1 - core, side)],
+                core_got.at[at, :],
+                s_send.at[number, 0],
+                s_recv.at[number, 0],
+                partner,
+            )
+            over.wait()
+            half = at_block(core, side)
+            sums[at, half] = sums[at, half] + core_got[at, :]
+            for half in range(2):
+                toward = 1 + half
+                state[half, 1] = hop(half, 1, xor(chip, 3), toward, 2 * half + 1)
+                state[half, 0] = hop(half, 0, xor(chip, toward), toward, 2 * half)
+
+        def second():
+            for half in range(2):
+                here = (half_at[half], col(core, xor(chip, 2 - half)))
+                state[half, 1].wait()
+                sums[here] = sums[here] + chip_got[1, half_at[half], :]
+                state[half, 2] = hop(half, 2, xor(chip, 2 - half), 2 - half, 4 + half)
+
+        def add():
+            for half in range(2):
+                state[half, 0].wait()
+                state[half, 2].wait()
+            total = sums[at, col(core, chip)].astype(f32)
+            for index in (0, 2):
+                total += chip_got[index, at, :].astype(f32)
+            piece[at, :] = total.astype(bf16)
+
+        return begin, mid, second, add
+
+    def two_hop_to_plane(number, first, count):
+        at = pl.ds(first, count)
+        half_at = [pl.ds(first + n * (count // 2), count // 2) for n in range(2)]
+        state = {}
+
+        def send(src, rows_of, place, where, n):
+            copy = remote(
+                src,
+                wide_ref.at[rows_of, col(core, place)],
+                t_send.at[number, n],
+                t_recv.at[number, n],
+                where,
+            )
+            copy.start()
+            return copy
+
+        def start():
+            for urgent in range(2):
+                for bit in (1, 2):
+                    half = bit - 1 if urgent == 0 else 2 - bit
+                    state[bit, half] = send(
+                        piece.at[half_at[half], :],
+                        half_at[half],
+                        chip,
+                        across(bit),
+                        6 + 2 * (bit - 1) + half,
+                    )
+            over = send(piece.at[at, :], at, chip, partner, 12)
+            own = pltpu.make_async_copy(
+                piece.at[at, :], wide_ref.at[at, col(core, chip)], t_send.at[number, 15]
+            )
+            own.start()
+            state["wait"] = [over, own]
+
+        def relay():
+            for half in range(2):
+                bit = 1 + half
+                state[bit, half].wait_recv()
+                place = xor(chip, bit)
+                here = wide_ref.at[half_at[half], col(core, place)]
+                state[3, half] = send(here, half_at[half], place, across(2 - half), 10 + half)
+
+        def forward():
+            for bit in (1, 2):
+                state[bit, 2 - bit].wait_recv()
+                place = xor(chip, bit)
+                here = wide_ref.at[at, col(core, place)]
+                state["wait"].append(send(here, at, place, partner, 12 + bit))
+
+        def end():
+            for half in range(2):
+                state[3, half].wait_recv()
+            place = xor(chip, 3)
+            here = wide_ref.at[at, col(core, place)]
+            state["wait"].append(send(here, at, place, partner, 16))
+
+        def done():
+            for copy in state["wait"]:
+                copy.wait()
+            for half in range(2):
+                state[3, half].wait_send()
+                for bit in (1, 2):
+                    state[bit, half].wait_send()
+
+        return start, relay, forward, end, done
+
     def to_plane(number, src, rows_to):
         state = {}
 
@@ -992,12 +1114,12 @@
     at_a = pl.ds(features, 16)
     at_o = pl.ds(features + 16, mixed)
     at_g = pl.ds(features + 16 + mixed, small)
-    of_d = [section(n, n * features // 2, features // 2) for n in range(2)]
-    of_o = section(2, features + 16, mixed)
+    of_d = [two_hop_section(n, n * features // 2, features // 2) for n in range(2)]
+    of_o = two_hop_section(2, features + 16, mixed)
     of_g = section(3, features + 16 + mixed, small)
     of_a = section(4, features, 16)
-    out_d = [to_plane(n, piece.at[halves_in[n], :], halves_in[n]) for n in range(2)]
-    out_o = to_plane(2, piece.at[at_o, :], at_o)
+    out_d = [two_hop_to_plane(n, n * features // 2, features // 2) for n in range(2)]
+    out_o = two_hop_to_plane(2, features + 16, mixed)
     out_g = to_plane(3, blocks, pl.ds(features + 16 + mixed, n_head * small))
     out_a = to_plane(4, piece.at[at_a, :], at_a)
     router_part = dot(dzs[...], mrs[...], TN)[:named]
@@ -1153,22 +1275,27 @@
     to_out[1](0)
     to_out[1](1)
     of_a[1]()
+    of_o[2]()
     of_g[2]()
     small_block = at_block(h, small)
     blocks[small_block, :] = piece[at_g, :]
     g_copies = spread(9, lambda s: blocks.at[small_block, :], lambda s: blocks.at[small_block, :])
     to_x[1](0)
     to_out[1](2)
-    of_o[2]()
+    of_o[3]()
     out_o[0]()
+    of_d[0][2]()
     to_x[1](1)
     to_x[1](2)
-    of_d[0][2]()
+    of_d[1][2]()
+    out_o[1]()
+    of_d[0][3]()
     out_d[0][0]()
     of_a[2]()
     gain_part[...] = piece[at_a, :]
     gain_copies = spread(10, lambda s: gain_part, lambda s: gain_got.at[s - 1])
-    of_d[1][2]()
+    out_o[2]()
+    of_d[1][3]()
     out_d[1][0]()
     for step in peers:
         g_copies[step].wait()
@@ -1179,6 +1306,7 @@
         gain += gain_got[step - 1].astype(f32)
     piece[at_a, :] = gain.astype(bf16)
     out_a[0]()
+    out_d[0][1]()
     to_x[2](grad_x_ref)
     output_ref[...] = middle[...] + outs[own_block, :].astype(f32)
     to_out[2](output_ref)
@@ -1196,10 +1324,16 @@
     )
     for store in stores:
         store.start()
+    out_d[1][1]()
+    out_o[3]()
+    out_d[0][2]()
+    out_g[1]()
+    out_a[1]()
+    out_d[1][2]()
+    out_d[0][3]()
+    out_d[1][3]()
     for one in (out_o, out_d[0], out_g, out_a, out_d[1]):
-        one[1]()
-    for one in (out_o, out_d[0], out_g, out_a, out_d[1]):
-        one[2]()
+        one[-1]()
     for store in stores:
         store.wait()
     mr_end()
@@ -1293,6 +1427,8 @@
         e_recv=dma((2, 6)),
         s_send=dma((5, 3 * chips)),
         s_recv=dma((5, 3 * chips)),
+        t_send=dma((3, 17)),
+        t_recv=dma((3, 17)),
         ready=pltpu.SemaphoreType.REGULAR,
         free=pltpu.SemaphoreType.REGULAR((2,)),
     )

time: 201 us -> 193 us (0.960)
  Pallas kernels: 196 us -> 188 us
    pallas_call x1, Pallas kernels: 188 us -> 179 us  [layer_call(): pl.pallas_call(functools.partial(layer_kernel, n_dp, n_head), out_shape=[...]
where the time goes in v8:
time: 193 us
  Pallas kernels  188 us (97%)
  other arithmetic  2.69 us (1%)
    pallas_call x1, Pallas kernels, layer_call(): pl.pallas_call(functools.partial(layer_kernel, n_dp, n_head), out_shape=[...  179 us
    pallas_call x1, Pallas kernels, finish_call(): pl.pallas_call(functools.partial(finish_kernel, n_dp, n_head), out_shape=...  8.46 us

profile of v8, /device:TPU:0, one launch (start us, length us, event | category | flops | bytes accessed | tf_op | source)
XLA Modules:
  0.0 192.8 jit_solution(11683374673348480050)
XLA Ops:
  0.6 0.7 convert_element_type.6
  1.3 0.7 convert_element_type.7
  2.0 1.3 fusion.gain_ref
  3.3 179.5 %shard_map.274 = (f32[128,1024]{1,0:T(8,128)}, f32[128,1024]{1,0:T(8,128)}, bf16[1808,1024]{1,0:T(8,128)(2,1)}, bf16[1024,384]{1,0:T(8,128)(2,1)}, bf16[384,1024]{1,0:T(8,128)(2,1)}) custom-call(bf16[128,1024]{1,0:T(8,128)(2,1)} %x_ref.1, bf16[128,1024]{1,0:T(8,128)(2,1)} %cot_ref.1, s32[16,128]{1,0:T(8,128)} %bitcast.35, s32[2,512]{1,0:T(2,128)} %bitcast.36, ...), custom_call_target="tpu_custom_call" | custom-call | tf_op jit(solution)/shard_map/pallas_call | solution.py:1435
  182.8 8.5 %shard_map.275 = (f32[128,1024]{1,0:T(8,128)}, f32[128,1024]{1,0:T(8,128)}, f32[1,1024]{1,0:T(1,128)}, f32[1024,128]{1,0:T(8,128)}, f32[1024,128]{1,0:T(8,128)},...) custom-call(f32[128,1024]{1,0:T(8,128)} %get-tuple-element.29.output, ...), custom_call_target="tpu_custom_call" | custom-call | tf_op jit(solution)/shard_map/pallas_call | solution.py:1549
  191.3 1.5 copy.31

commit v9 on v8

--- a/solution.py
+++ b/solution.py
@@ -432,15 +432,15 @@
 
     def gather(kind, buffer):
         def go(side, step):
-            block = jnp.clip(h - step if side == 0 else h + step, 0, last)
+            sign = 1 - 2 * side
+            block = jnp.clip(h - sign * step, 0, last)
+            where = (d, jnp.clip(h + sign, 0, last))
             copies = []
             for half in range(2):
                 here = buffer.at[at_block(2 * block + half, tokens // 2), :]
                 number = (side * last + step) * 2 + half
                 copies.append(
-                    remote(
-                        here, here, z_send.at[kind, number], z_recv.at[kind, number], (right, left)[side]
-                    )
+                    remote(here, here, z_send.at[kind, number], z_recv.at[kind, number], where)
                 )
             return copies
 
@@ -462,7 +462,11 @@
                         go(side, step)[half].start()
 
         def stage(step, which="all"):
-            ways = ((0, h >= step, h < last), (1, h + step <= last, h > 0))
+            nearer = jnp.where(2 * h < n_head, 0, 1)
+            ways = []
+            for side in (nearer, 1 - nearer):
+                there = jnp.where(side == 0, h >= step, h + step <= last)
+                ways.append((side, there, jnp.where(side == 0, h < last, h > 0)))
             for side, there, onward in ways:
                 if step < last and which != "rest":
                     arrive(side, step, there & onward, True)
@@ -773,8 +777,8 @@
         lifted[j, 1] = lift[:, slab:].astype(bf16)
 
     pl.loop(0, chips // 2)(lift_chip)
+    mr_stage(1, "duty")
     last_halves(1)
-    mr_stage(1)
     pl.loop(chips // 2, chips)(lift_chip)
 
     weights_here(1)
@@ -808,10 +812,11 @@
             hids[j, at, :] = slope.astype(bf16) * (lift * gate)
             return total + dot(act * lift, pick, NT)
 
-        total = lax.fori_loop(0, chips, chip_step, jnp.zeros((pair, lanes), f32))
+        total = lax.fori_loop(0, chips // 2, chip_step, jnp.zeros((pair, lanes), f32))
+        between()
+        total = lax.fori_loop(chips // 2, chips, chip_step, total)
         dz = (total * live * (1.0 - gates)).astype(bf16)
         dzs[at, :] = dz
-        between()
 
         @pl.loop(0, features // column)
         def _(c):
@@ -831,6 +836,7 @@
             outs[:, part_of] = total.astype(bf16)
 
     near = h // 2
+    mr_stage(1, "rest")
     to_dmr = chain_sum(5, part, got)
     pair_of_blocks(near, lambda: mr_stage(2, "duty"))
     to_dmr[0](2)
@@ -839,20 +845,24 @@
     pair_of_blocks(1 - near, lambda: None)
     to_dmr[0](0)
     to_dmr[0](1)
-    outputs()
     pl.semaphore_signal(ready, inc=1, device_id=partner, device_id_type=MESH)
 
     weights_sent()
     turned[...] = mrs[...].T
 
-    def expert_grads(place, at):
-        for half in halves_in:
-            w_in[place, half, at] = dot(turned[half, :], hids[place, :, at]).astype(bf16)
-            w_out[place, at, half] = dot(acts[place, :, at], cot[:, half], TN).astype(bf16)
-
-    def to_other_core(n):
+    def to_other_core(n, array):
         place = xor(chip, chips - 1 - n)
-        copies = [
+        if array == 0:
+            return [
+                remote(
+                    w_out.at[place, other_side, :],
+                    core_out.at[place],
+                    c_send.at[2, n],
+                    c_recv.at[2, n],
+                    partner,
+                )
+            ]
+        return [
             remote(
                 w_in.at[place, halves_in[half], other_side],
                 lifted.at[place, half],
@@ -862,67 +872,61 @@
             )
             for half in range(2)
         ]
-        copies.append(
-            remote(
-                w_out.at[place, other_side, :],
-                core_out.at[place],
-                c_send.at[2, n],
-                c_recv.at[2, n],
-                partner,
-            )
+
+    pl.semaphore_wait(ready, 1)
+    hops = {}
+
+    def hop(half, index, place, toward, array):
+        copy = remote(
+            slot(array, place, core, half),
+            (hop_out, hop_in)[array].at[half, index],
+            e_send.at[1 - array, 2 * half + index],
+            e_recv.at[1 - array, 2 * half + index],
+            across(toward),
         )
-        return copies
-
-    pl.semaphore_wait(ready, 1)
-
-    hops = {}
-
-    def hop(half, index, place, toward):
-        copies = (
-            remote(
-                slot(1, place, core, half),
-                hop_in.at[half, index],
-                e_send.at[0, 2 * half + index],
-                e_recv.at[0, 2 * half + index],
-                across(toward),
-            ),
-            remote(
-                slot(0, place, core, half),
-                hop_out.at[half, index],
-                e_send.at[1, 2 * half + index],
-                e_recv.at[1, 2 * half + index],
-                across(toward),
-            ),
-        )
-        for copy in copies:
-            copy.start()
-        hops[half, index] = copies
-
-    def both_cores(n):
+        copy.start()
+        hops[half, index, array] = copy
+
+    def both_cores(n, array):
         step = chips - 1 - n
         place = xor(chip, step)
-        for copy in to_other_core(n):
+        for copy in to_other_core(n, array):
             copy.wait()
-        for half in range(2):
-            here = (place, halves_in[half], own_side)
-            w_in[here] = w_in[here] + lifted[place, half]
-        w_out[place, own_side, :] = w_out[place, own_side, :] + core_out[place]
+        if array == 0:
+            w_out[place, own_side, :] = w_out[place, own_side, :] + core_out[place]
+        else:
+            for half in range(2):
+                here = (place, halves_in[half], own_side)
+                w_in[here] = w_in[here] + lifted[place, half]
         if step == 3:
-            hop(0, 1, place, 1)
-            hop(1, 1, place, 2)
+            hop(0, 1, place, 1, array)
+            hop(1, 1, place, 2, array)
         elif step:
-            hop(step - 1, 0, place, step)
-
-    for n in range(chips):
-        place = xor(chip, chips - 1 - n)
-        expert_grads(place, other_side)
-        for copy in to_other_core(n):
-            copy.start()
-        if n:
-            both_cores(n - 1)
-        expert_grads(place, own_side)
+            hop(step - 1, 0, place, step, array)
+
+    def expert_grads(array, place, at):
+        for half in halves_in:
+            if array == 0:
+                w_out[place, at, half] = dot(acts[place, :, at], cot[:, half], TN).astype(bf16)
+            else:
+                w_in[place, half, at] = dot(turned[half, :], hids[place, :, at]).astype(bf16)
+
+    def all_grads(array):
+        for n in range(chips):
+            place = xor(chip, chips - 1 - n)
+            expert_grads(array, place, other_side)
+            for copy in to_other_core(n, array):
+                copy.start()
+            if n:
+                both_cores(n - 1, array)
+            expert_grads(array, place, own_side)
+
+    all_grads(1)
+    outputs()
+    both_cores(chips - 1, 1)
     to_dmr[1](0)
-    both_cores(chips - 1)
+    all_grads(0)
+    both_cores(chips - 1, 0)
     to_dmr[1](1)
     to_dmr[1](2)
     side = features // 2
@@ -1152,8 +1156,8 @@
     lasts = {}
 
     def first_hop(half, index, place):
-        for copy in hops[half, index]:
-            copy.wait()
+        for array in range(2):
+            hops[half, index, array].wait()
         at_in = (place, halves_in[half], own_side)
         at_out = (place, halves_out(core)[half], slice(None))
         w_in[at_in] = w_in[at_in] + hop_in[half, index]
@@ -1509,7 +1513,9 @@
     gain = jnp.broadcast_to(gain_ref[0:1, :], (width, features)).T
     query_ref[...] = wide[first, pl.ds(0, width)].astype(f32) * gain
     key_ref[...] = wide[first, pl.ds(width, width)].astype(f32) * gain
-    gate_ref[...] = (wide[first, pl.ds(2 * width, width)].astype(f32) * gain).T[:gates]
+    turned = (wide[first, pl.ds(2 * width, width)].astype(f32) * gain).T
+    for e in range(gates):
+        gate_ref[e] = turned[e : e + 1]
     loads[1].wait()
     mix[...] = wide[pl.ds(features + 16, mixed), :].astype(f32)
     stores.append(copy(mix, mix_ref, 8))
@@ -1625,16 +1631,16 @@
         key_weight.shape[1:],
         value_weight.shape[1:],
         output_weight.shape[1:],
-        (2 * experts, features),
+        (2 * experts, 1, features),
         (1, features),
         (router.shape[1], features),
         expert_in.shape,
         expert_out.shape,
     )
     done = list(finish_call(n_dp, n_head, shapes, (*results, gains)))
-    for number in (3, 4, 5, 6, 7):
+    for number in (3, 4, 5, 6):
         done[number] = done[number][None]
-    done[7] = done[7].transpose(0, 2, 1)
+    done[7] = done[7].transpose(1, 2, 0)
     done[9] = done[9].T
     done[2], done[8] = done[2][0], done[8][0]
     return tuple(done)

time: 193 us -> 184 us (0.953)
  Pallas kernels: 188 us -> 180 us
    pallas_call x1, Pallas kernels: 179 us -> 172 us  [layer_call(): pl.pallas_call(functools.partial(layer_kernel, n_dp, n_head), out_shape=[...]
where the time goes in v9:
time: 184 us
  Pallas kernels  180 us (98%)
  other arithmetic  2.69 us (1%)
    pallas_call x1, Pallas kernels, layer_call(): pl.pallas_call(functools.partial(layer_kernel, n_dp, n_head), out_shape=[...  172 us
    pallas_call x1, Pallas kernels, finish_call(): pl.pallas_call(functools.partial(finish_kernel, n_dp, n_head), out_shape=...  8.46 us

profile of v9, /device:TPU:0, one launch (start us, length us, event | category | flops | bytes accessed | tf_op | source)
XLA Modules:
  0.0 183.5 jit_solution(7545463074501592210)
XLA Ops:
  0.6 0.7 convert_element_type.6
  1.3 0.7 convert_element_type.7
  2.0 1.3 fusion.gain_ref
  3.3 171.5 %shard_map.274 = (f32[128,1024]{1,0:T(8,128)}, f32[128,1024]{1,0:T(8,128)}, bf16[1808,1024]{1,0:T(8,128)(2,1)}, bf16[1024,384]{1,0:T(8,128)(2,1)}, bf16[384,1024]{1,0:T(8,128)(2,1)}) custom-call(bf16[128,1024]{1,0:T(8,128)(2,1)} %x_ref.1, bf16[128,1024]{1,0:T(8,128)(2,1)} %cot_ref.1, s32[16,128]{1,0:T(8,128)} %bitcast.32, s32[2,512]{1,0:T(2,128)} %bitcast.33, ...), custom_call_target="tpu_custom_call" | custom-call | tf_op jit(solution)/shard_map/pallas_call | solution.py:1439
  174.9 8.5 %shard_map.275 = (f32[128,1024]{1,0:T(8,128)}, f32[128,1024]{1,0:T(8,128)}, f32[1,1024]{1,0:T(1,128)}, f32[1024,128]{1,0:T(8,128)}, f32[1024,128]{1,0:T(8,128)},...) custom-call(f32[128,1024]{1,0:T(8,128)} %get-tuple-element.29.output, ...), custom_call_target="tpu_custom_call" | custom-call | tf_op jit(solution)/shard_map/pallas_call | solution.py:1555

commit v10 on v9

--- a/solution.py
+++ b/solution.py
@@ -1280,37 +1280,38 @@
     to_out[1](1)
     of_a[1]()
     of_o[2]()
+    to_x[1](0)
+    of_d[0][2]()
+    of_d[1][2]()
     of_g[2]()
     small_block = at_block(h, small)
     blocks[small_block, :] = piece[at_g, :]
     g_copies = spread(9, lambda s: blocks.at[small_block, :], lambda s: blocks.at[small_block, :])
-    to_x[1](0)
-    to_out[1](2)
+    to_x[1](1)
     of_o[3]()
     out_o[0]()
-    of_d[0][2]()
-    to_x[1](1)
     to_x[1](2)
-    of_d[1][2]()
-    out_o[1]()
     of_d[0][3]()
     out_d[0][0]()
+    of_d[1][3]()
+    out_d[1][0]()
     of_a[2]()
     gain_part[...] = piece[at_a, :]
     gain_copies = spread(10, lambda s: gain_part, lambda s: gain_got.at[s - 1])
-    out_o[2]()
-    of_d[1][3]()
-    out_d[1][0]()
+    to_out[1](2)
+    out_o[1]()
     for step in peers:
         g_copies[step].wait()
     out_g[0]()
+    out_d[0][1]()
     gain = gain_part[...].astype(f32)
     for step in peers:
         gain_copies[step].wait()
         gain += gain_got[step - 1].astype(f32)
     piece[at_a, :] = gain.astype(bf16)
     out_a[0]()
-    out_d[0][1]()
+    out_d[1][1]()
+    out_o[2]()
     to_x[2](grad_x_ref)
     output_ref[...] = middle[...] + outs[own_block, :].astype(f32)
     to_out[2](output_ref)
@@ -1328,7 +1329,6 @@
     )
     for store in stores:
         store.start()
-    out_d[1][1]()
     out_o[3]()
     out_d[0][2]()
     out_g[1]()
@@ -1478,6 +1478,8 @@
     grad_out,
     output,
     grad_x,
+    query,
+    key,
     sem,
 ):
     features, slab = in_ref.shape
@@ -1488,46 +1490,56 @@
     small = (wide_ref.shape[0] - top) // n_head
     named = n_dp * per_device
 
-    def copy(src, dst, number):
-        one = pltpu.make_async_copy(src, dst, sem.at[number])
+    numbers = iter(range(sem.shape[0]))
+
+    def copy(src, dst):
+        one = pltpu.make_async_copy(src, dst, sem.at[next(numbers)])
         one.start()
         return one
 
-    rest = pl.ds(top, wide_ref.shape[0] - top)
-    loads = [
-        copy(wide_ref.at[pl.ds(0, features), :], wide.at[pl.ds(0, features), :], 0),
-        copy(wide_ref.at[pl.ds(features, top - features), :], wide.at[pl.ds(features, top - features), :], 1),
-        copy(in_ref, flat_in, 2),
-        copy(out_ref, flat_out, 3),
-        copy(wide_ref.at[rest, :], wide.at[rest, :], 4),
-    ]
-    loads += [copy(output_ref, output, 11), copy(grad_x_ref, grad_x, 12)]
+    bands = 4
+    band = features // bands
+    load = lambda first, count: copy(
+        wide_ref.at[pl.ds(first, count), :], wide.at[pl.ds(first, count), :]
+    )
+    plain = [(copy(output_ref, output), output, final_ref), (copy(grad_x_ref, grad_x), grad_x, input_ref)]
+    for_out, for_in = copy(out_ref, flat_out), copy(in_ref, flat_in)
+    for_bands = [load(n * band, band) for n in range(bands)]
+    for_mix = [load(features + 16 + n * mixed // 2, mixed // 2) for n in range(2)]
+    others = [load(features, 16), load(top, n_head * small)]
     stores = []
-    for number, (held, result) in enumerate(((output, final_ref), (grad_x, input_ref))):
-        loads[5 + number].wait()
-        stores.append(copy(held, result, 5 + number))
-    loads[0].wait()
-    first = pl.ds(0, features)
-    value[...] = wide[first, pl.ds(3 * width, value.shape[1])].astype(f32)
-    stores.append(copy(value, value_ref, 7))
     gain = jnp.broadcast_to(gain_ref[0:1, :], (width, features)).T
-    query_ref[...] = wide[first, pl.ds(0, width)].astype(f32) * gain
-    key_ref[...] = wide[first, pl.ds(width, width)].astype(f32) * gain
-    turned = (wide[first, pl.ds(2 * width, width)].astype(f32) * gain).T
+    for loaded, held, result in plain:
+        loaded.wait()
+        stores.append(copy(held, result))
+    for_out.wait()
+    for e in range(per_device):
+        grad_out[e] = flat_out[pl.ds(e * width, width), :].astype(f32)
+        stores.append(copy(grad_out.at[e], grad_out_ref.at[e]))
+    for_in.wait()
+    for e in range(per_device):
+        grad_in[e] = flat_in[:, pl.ds(e * width, width)].astype(f32)
+        stores.append(copy(grad_in.at[e], grad_in_ref.at[e]))
+    for n in range(bands):
+        for_bands[n].wait()
+        at = pl.ds(n * band, band)
+        scale = gain[n * band : (n + 1) * band]
+        value[at, :] = wide[at, pl.ds(3 * width, value.shape[1])].astype(f32)
+        stores.append(copy(value.at[at, :], value_ref.at[at, :]))
+        query[at, :] = wide[at, pl.ds(0, width)].astype(f32) * scale
+        stores.append(copy(query.at[at, :], query_ref.at[at, :]))
+        key[at, :] = wide[at, pl.ds(width, width)].astype(f32) * scale
+        stores.append(copy(key.at[at, :], key_ref.at[at, :]))
+    for n in range(2):
+        for_mix[n].wait()
+        at = pl.ds(n * mixed // 2, mixed // 2)
+        mix[at, :] = wide[pl.ds(features + 16 + n * mixed // 2, mixed // 2), :].astype(f32)
+        stores.append(copy(mix.at[at, :], mix_ref.at[at, :]))
+    turned = (wide[pl.ds(0, features), pl.ds(2 * width, width)].astype(f32) * gain).T
     for e in range(gates):
         gate_ref[e] = turned[e : e + 1]
-    loads[1].wait()
-    mix[...] = wide[pl.ds(features + 16, mixed), :].astype(f32)
-    stores.append(copy(mix, mix_ref, 8))
-    loads[2].wait()
-    for e in range(per_device):
-        grad_in[e] = flat_in[:, pl.ds(e * width, width)].astype(f32)
-    stores.append(copy(grad_in, grad_in_ref, 9))
-    loads[3].wait()
-    for e in range(per_device):
-        grad_out[e] = flat_out[pl.ds(e * width, width), :].astype(f32)
-    stores.append(copy(grad_out, grad_out_ref, 10))
-    loads[4].wait()
+    for loaded in others:
+        loaded.wait()
     attend_ref[...] = wide[pl.ds(features, 16), :][0:1].astype(f32)
     planes = wide[pl.ds(top, n_head * small), :]
     place = lax.broadcasted_iota(jnp.int32, (n_head * small, experts_total), 0)
@@ -1550,7 +1562,7 @@
     wide, flat_in, flat_out = args[2], args[3], args[4]
     value, mix, grad_in, grad_out = shapes[5], shapes[6], shapes[10], shapes[11]
     specs = [VM] * 12
-    for number in (0, 1, 5, 6, 10, 11):
+    for number in (0, 1, 3, 4, 5, 6, 10, 11):
         specs[number] = ANY
     return pl.pallas_call(
         functools.partial(finish_kernel, n_dp, n_head),
@@ -1567,7 +1579,9 @@
             pltpu.VMEM(grad_out, f32),
             pltpu.VMEM(shapes[0], f32),
             pltpu.VMEM(shapes[1], f32),
-            pltpu.SemaphoreType.DMA((13,)),
+            pltpu.VMEM(shapes[3], f32),
+            pltpu.VMEM(shapes[4], f32),
+            pltpu.SemaphoreType.DMA((40,)),
         ],
         compiler_params=pltpu.CompilerParams(vmem_limit_bytes=60 << 20),
     )(*args)
@@ -1599,8 +1613,8 @@
     group = tokens * n_head
     angles = np.arange(group)[:, None] * theta ** (-2.0 * np.arange(width // 2) / width)[None, :]
     angles = np.concatenate([np.cos(angles), np.sin(angles)], axis=1).astype(np.float32)
-    both = np.eye(2, dtype=np.float32)
-    gains = attend_gain.astype(f32) * both[:, :1] + expert_gain.astype(f32) * both[:, 1:]
+    first = np.arange(2)[:, None] == 0
+    gains = jnp.where(first, attend_gain[None, :], expert_gain[None, :]).astype(f32)
     results = layer_call(
         n_dp,
         n_head,

time: 184 us -> 180 us (0.978)
  Pallas kernels: 180 us -> 178 us
where the time goes in v10:
time: 180 us
  Pallas kernels  178 us (99%)
    pallas_call x1, Pallas kernels, layer_call(): pl.pallas_call(functools.partial(layer_kernel, n_dp, n_head), out_shape=[...  170 us
    pallas_call x1, Pallas kernels, finish_call(): pl.pallas_call(functools.partial(finish_kernel, n_dp, n_head), out_shape=...  7.6 us

profile of v10, /device:TPU:0, one launch (start us, length us, event | category | flops | bytes accessed | tf_op | source)
XLA Modules:
  0.0 180.1 jit_solution(13997421662972687822)
XLA Ops:
  0.6 1.4 fusion.gain_ref
  2.0 170.3 %shard_map.265 = (f32[128,1024]{1,0:T(8,128)}, f32[128,1024]{1,0:T(8,128)}, bf16[1808,1024]{1,0:T(8,128)(2,1)}, bf16[1024,384]{1,0:T(8,128)(2,1)}, bf16[384,1024]{1,0:T(8,128)(2,1)}) custom-call(bf16[128,1024]{1,0:T(8,128)(2,1)} %x_ref.1, bf16[128,1024]{1,0:T(8,128)(2,1)} %cot_ref.1, s32[16,128]{1,0:T(8,128)} %bitcast.32, s32[2,512]{1,0:T(2,128)} %bitcast.33, ...), custom_call_target="tpu_custom_call" | custom-call | tf_op jit(solution)/shard_map/pallas_call | solution.py:1439
  172.3 7.6 %shard_map.266 = (f32[128,1024]{1,0:T(8,128)}, f32[128,1024]{1,0:T(8,128)}, f32[1,1024]{1,0:T(1,128)}, f32[1024,128]{1,0:T(8,128)}, f32[1024,128]{1,0:T(8,128)},...) custom-call(f32[128,1024]{1,0:T(8,128)} %get-tuple-element.29.output, ...), custom_call_target="tpu_custom_call" | custom-call | tf_op jit(solution)/shard_map/pallas_call | solution.py:1567

commit v11 on v10

--- a/solution.py
+++ b/solution.py
@@ -288,7 +288,6 @@
     picks,
     two_picks,
     head_picks,
-    w_g,
     w_r,
     seg,
     gains,
@@ -399,7 +398,6 @@
     for_rows = [
         load(x_ref, rows.at[own_block, :]),
         load(gain_ref, gains),
-        load(wg_ref, w_g),
         load(wq_ref, w_an.at[:, pl.ds(0, width)]),
         load(wk_ref, w_an.at[:, pl.ds(width, width)]),
         load(wv_ref, w_v),
@@ -618,7 +616,7 @@
         1.0,
         0.0,
     ).astype(bf16)
-    w_an[:, pl.ds(2 * width, width)] = dot(w_g[...], one_hot(w_g.shape[0]), TN).astype(bf16)
+    w_an[:, pl.ds(2 * width, width)] = dot(wg_ref[...], one_hot(wg_ref.shape[0]), TN).astype(bf16)
     uses = two_picks.shape[1]
     head_picks[...] = jnp.concatenate(
         [
@@ -905,21 +903,24 @@
             hop(step - 1, 0, place, step, array)
 
     def expert_grads(array, place, at):
-        for half in halves_in:
-            if array == 0:
+        if array == 0:
+            for half in halves_in:
                 w_out[place, at, half] = dot(acts[place, :, at], cot[:, half], TN).astype(bf16)
-            else:
-                w_in[place, half, at] = dot(turned[half, :], hids[place, :, at]).astype(bf16)
+        else:
+            for n in range(features // column):
+                band = pl.ds(n * column, column)
+                w_in[place, band, at] = dot(turned[band, :], hids[place, :, at]).astype(bf16)
 
     def all_grads(array):
         for n in range(chips):
             place = xor(chip, chips - 1 - n)
-            expert_grads(array, place, other_side)
+            expert_grads(array, place, other_side if array == 0 else slice(None))
             for copy in to_other_core(n, array):
                 copy.start()
             if n:
                 both_cores(n - 1, array)
-            expert_grads(array, place, own_side)
+            if array == 0:
+                expert_grads(array, place, own_side)
 
     all_grads(1)
     outputs()
@@ -1372,7 +1373,6 @@
         picks=vm(picks.shape, jnp.int32),
         two_picks=vm((2, *args[3].shape), jnp.int32),
         head_picks=vm((group, lanes), jnp.int32),
-        w_g=vm(args[10].shape, bf16),
         w_r=vm(router.shape, bf16),
         seg=vm((1, group), jnp.int32),
         gains=vm(args[6].shape, f32),
@@ -1440,7 +1440,7 @@
         functools.partial(layer_kernel, n_dp, n_head),
         out_shape=[o[0] for o in outs],
         out_specs=[o[1] for o in outs],
-        in_specs=[ANY] * 16,
+        in_specs=[VM if number == 10 else ANY for number in range(16)],
         scratch_shapes=list(scratch.values()),
         compiler_params=pltpu.CompilerParams(
             collective_id=1, has_side_effects=True, vmem_limit_bytes=vmem_bytes

time: 180 us -> 181 us (level)
  no operation moved by 1% of the time
where the time goes in v11:
time: 181 us
  Pallas kernels  179 us (99%)
    pallas_call x1, Pallas kernels, layer_call(): pl.pallas_call(functools.partial(layer_kernel, n_dp, n_head), out_shape=[...  171 us
    pallas_call x1, Pallas kernels, finish_call(): pl.pallas_call(functools.partial(finish_kernel, n_dp, n_head), out_shape=...  7.6 us

profile of v11, /device:TPU:0, one launch (start us, length us, event | category | flops | bytes accessed | tf_op | source)
XLA Modules:
  0.0 181.2 jit_solution(1942460439975862904)
XLA Ops:
  0.6 1.4 fusion.gain_ref
  2.0 171.3 %shard_map.265 = (f32[128,1024]{1,0:T(8,128)}, f32[128,1024]{1,0:T(8,128)}, bf16[1808,1024]{1,0:T(8,128)(2,1)}, bf16[1024,384]{1,0:T(8,128)(2,1)}, bf16[384,1024]{1,0:T(8,128)(2,1)}) custom-call(bf16[128,1024]{1,0:T(8,128)(2,1)} %x_ref.1, bf16[128,1024]{1,0:T(8,128)(2,1)} %cot_ref.1, s32[16,128]{1,0:T(8,128)} %bitcast.32, s32[2,512]{1,0:T(2,128)} %bitcast.33, ...), custom_call_target="tpu_custom_call" | custom-call | tf_op jit(solution)/shard_map/pallas_call | solution.py:1439
  173.4 7.6 %shard_map.266 = (f32[128,1024]{1,0:T(8,128)}, f32[128,1024]{1,0:T(8,128)}, f32[1,1024]{1,0:T(1,128)}, f32[1024,128]{1,0:T(8,128)}, f32[1024,128]{1,0:T(8,128)},...) custom-call(f32[128,1024]{1,0:T(8,128)} %get-tuple-element.29.output, ...), custom_call_target="tpu_custom_call" | custom-call | tf_op jit(solution)/shard_map/pallas_call | solution.py:1567
